TPU v7x, 512 devices: a whole 4x4x16 slice. The times are simulated.
512 devices in a mesh: tile: 16 (over y, x), fsdp: 32 (over z, core).
Axes of the slice: x: 4, y: 4, z: 16, core: 2. Of those that a mesh axis runs over, the one named last changes fastest.
Arguments:
- images: bfloat16 [32, 64, 64, 2048], P('fsdp', 'tile'), may hold values from -80 to 80
- w_qkv: bfloat16 [2048, 3072], P(None, ('tile', 'fsdp')), may hold values from -0.125 to 0.125
- prev_scale: float32 [1], replicated, may hold values from 0.06 to 0.11
- extent: int32 [32, 2], P('fsdp'), may hold values from 32 to 64, as said below
Outputs:
- attended: bfloat16 [32, 64, 64, 1024], P('fsdp', 'tile')
- new_scales: float32 [2], replicated
Inputs may be any that keep to these rules, and one draw needn't show every extreme that they name: `extent`: each image's valid tokens are its top-left rows (first entry) and columns (second entry), at least half of each; image 0 is whole.
All inputs are finite; a program needn't handle non-finite values.
Results may differ from a plain program's by a relative error of at most 0.01.
The roundings to bfloat16 on the way count: a program that leaves them out, or rounds other values in their place, can miss the bound.
Values may be sent and summed in bfloat16 or wider, within the bound.
No kernel may reach another device: no remote copies, remote signals or barrier semaphores. Data moves between devices by JAX's collectives and lax.ppermute only.
A program may use at most 128 MiB of HBM per device.

v0:
```python
import jax
import jax.numpy as jnp
from jax import lax
from jax.sharding import PartitionSpec as P

HEADS = 8
HEAD = 128


half_window = 3
fp_top = 448.0


def extended(value, sides, width):
    for axis, dim in sides:
        devices, length = (lax.axis_size(axis), value.shape[dim])
        up = [(i, (i + 1) % devices) for i in range(devices - 1)]
        down = [(j, i) for i, j in up]
        last = lax.slice_in_dim(value, length - width, length, axis=dim)
        first = lax.slice_in_dim(value, 0, width, axis=dim)
        before = lax.ppermute(last, axis, up)
        after = lax.ppermute(first, axis, down)
        value = jnp.concatenate([before, value, after], axis=dim)
    return value


def neighbourhood(query, keys, values, row_start, ext_rows, ext_cols):
    row_count, col_count, head_count, head_size = query.shape
    scaling = float(head_size) ** (-0.5)
    row_ids = row_start + jnp.arange(row_count, dtype=jnp.int32)
    col_ids = jnp.arange(col_count, dtype=jnp.int32)
    scores = []
    allowed = []
    for row_shift in range(2 * half_window + 1):
        for col_shift in range(2 * half_window + 1):
            key_part = keys[row_shift : row_shift + row_count, col_shift : col_shift + col_count]
            scores.append(
                jnp.einsum("rchd,rchd->rch", query, key_part, preferred_element_type=jnp.float32)
                * scaling
            )
            key_rows = row_ids + (row_shift - half_window)
            key_cols = col_ids + (col_shift - half_window)
            inside = ((key_rows >= 0) & (key_rows < ext_rows))[:, None] & (
                (key_cols >= 0) & (key_cols < ext_cols)
            )[None, :]
            if row_shift == half_window and col_shift == half_window:
                inside = jnp.ones_like(inside)
            allowed.append(inside)
    scores = jnp.stack(scores)
    allowed = jnp.stack(allowed)[..., None]
    highest = jnp.max(jnp.where(allowed, scores, -1e30), axis=0)
    weights = jnp.where(allowed, jnp.exp(scores - highest), 0.0)
    denominator = jnp.sum(weights, axis=0)
    probabilities = (weights / denominator).astype(jnp.bfloat16)
    attended = jnp.zeros(query.shape, jnp.float32)
    position = 0
    for row_shift in range(2 * half_window + 1):
        for col_shift in range(2 * half_window + 1):
            value_part = values[
                row_shift : row_shift + row_count, col_shift : col_shift + col_count
            ]
            attended = attended + jnp.einsum(
                "rch,rchd->rchd",
                probabilities[position],
                value_part,
                preferred_element_type=jnp.float32,
            )
            position = position + 1
    query_valid = (row_ids < ext_rows)[:, None] & (col_ids < ext_cols)[None, :]
    attended = jnp.where(query_valid[:, :, None, None], attended, 0.0)
    return attended.astype(jnp.bfloat16).reshape(row_count, col_count, head_count * head_size)


def local(images, w_qkv, prev_scale, extent):
    row_count = images.shape[1]
    col_count = images.shape[2]
    features = images.shape[3]
    scale_prev = prev_scale[0]
    flattened = images.reshape(row_count * col_count, features)
    quantized = jnp.clip(flattened.astype(jnp.float32) / scale_prev, -fp_top, fp_top).astype(
        jnp.bfloat16
    )
    peak_in = jnp.max(jnp.abs(images.astype(jnp.float32)))
    qkv = (
        jnp.dot(
            quantized,
            lax.all_gather(w_qkv, ("tile", "fsdp"), axis=1, tiled=True),
            preferred_element_type=jnp.float32,
        )
        * scale_prev
    ).astype(jnp.bfloat16)
    inner_width = HEADS * HEAD
    qkv = qkv.reshape(row_count, col_count, 3 * inner_width)
    query = qkv[:, :, :inner_width].reshape(row_count, col_count, HEADS, HEAD)
    key_value = qkv[:, :, inner_width:]
    widened = extended(key_value, (("tile", 0),), half_window)
    widened = jnp.pad(widened, ((0, 0), (half_window, half_window), (0, 0)))
    padded_rows = row_count + 2 * half_window
    padded_cols = col_count + 2 * half_window
    keys = widened[:, :, :inner_width].reshape(padded_rows, padded_cols, HEADS, HEAD)
    values = widened[:, :, inner_width:].reshape(padded_rows, padded_cols, HEADS, HEAD)
    row_start = lax.axis_index("tile") * row_count
    attended = neighbourhood(query, keys, values, row_start, extent[0, 0], extent[0, 1])
    peak_out = jnp.max(jnp.abs(attended.astype(jnp.float32)))
    global_in, global_out = lax.pmax((peak_in, peak_out), ("tile", "fsdp"))
    return (attended[None], jnp.stack([global_in, global_out]) / fp_top)


def solution(mesh):
    return jax.shard_map(
        local,
        mesh=mesh,
        in_specs=(P("fsdp", "tile", None, None), P(None, ("tile", "fsdp")), P(), P("fsdp", None)),
        out_specs=(P("fsdp", "tile", None, None), P()),
        check_vma=False,
    )
```

profile of v0, /device:TPU:1, one launch (start us, length us, event | category | flops | bytes accessed | tf_op | source)
XLA Modules:
  0.0 534.0 jit_solution(11258401090461076868)
XLA Ops:
  18.4 2.2 fusion.9
  20.6 217.6 %all-gather.3.cloned.1.call-done = bf16[512,6,2048]{2,1,0:T(8,128)(2,1)} async-done(((bf16[1,6,2048]{2,1,0:T(8,128)(2,1)}), bf16[512,6,2048]{2,1,0:T(8,128)(2,1)}) %all-gather.3.cloned.1.call-update) | async-done | bytes 12582928 | tf_op jit(solution)/shard_map/all_gather | solution.py:87
  238.1 20.6 %reshape.2510 = bf16[3072,2048]{1,0:T(8,128)(2,1)} reshape(bf16[512,6,2048]{2,1,0:T(8,128)(2,1)} %all-gather.3.cloned.1.call-done) | data formatting | bytes 25165824
  258.7 8.0 %fusion.1 = bf16[256,3072]{1,0:T(8,128)(2,1)S(1)} fusion(bf16[256,2048]{1,0:T(8,128)(2,1)S(1)} %bitcast.422, bf16[3072,2048]{1,0:T(8,128)(2,1)} %reshape.2510, f32[]{:T(128)} %bitcast.414), kind=kOutput, calls=%fused_computation.53 | convolution fusion | flops 3222798336 | bytes 15204356 | tf_op jit(solution)/shard_map/dot_general | solution.py:85
  266.9 2.4 collective-permute-start
  271.6 14.3 %collective-permute-done = bf16[3,64,2048]{2,1,0:T(8,128)(2,1)S(1)} collective-permute-done((bf16[3,64,2048]{2,1,0:T(8,128)(2,1)S(1)}, bf16[3,64,2048]{2,1,0:T(8,128)(2,1)S(1)}, u32[]{:S(2)}, u32[]{:S(2)}) %collective-permute-start) | collective-permute-done | bytes 786464 | tf_op jit(solution)/shard_map/ppermute | solution.py:21
  285.9 3.8 collective-permute-done.1
  290.8 1.9 fusion.110
  292.8 2.5 reshape.2409
  295.3 4.5 fusion.22
  299.8 1.6 copy.119
  309.0 6.4 %fusion.40 = (f32[4,64,8]{2,1,0:T(8,128)}, f32[4,64,8]{2,1,0:T(8,128)}, f32[4,64,8]{2,1,0:T(8,128)}, f32[4,64,8]{2,1,0:T(8,128)}, f32[4,64,8]{2,1,0:T(8,128)}, /...) fusion(bf16[10,70,8,128]{3,2,1,0:T(8,128)(2,1)S(1)} %reshape.24, ...), kind=kLoop, calls=%fused_computation.94 | loop fusion | flops 14381056 | bytes 10108928
  317.0 1.6 copy.204
  321.7 1.6 copy.189
  323.3 1.6 copy.184
  324.9 1.6 copy.179
  326.5 1.6 copy.174
  329.7 1.6 copy.164
  331.3 1.6 copy.159
  332.9 1.6 copy.154
  338.6 6.5 %fusion.58 = (f32[4,64,8]{2,1,0:T(8,128)}, f32[4,64,8]{2,1,0:T(8,128)}, f32[4,64,8]{2,1,0:T(8,128)}, f32[4,64,8]{2,1,0:T(8,128)}, f32[4,64,8]{2,1,0:T(8,128)}, /...) fusion(bf16[10,70,8,128]{3,2,1,0:T(8,128)(2,1)S(1)} %reshape.24, ...), kind=kLoop, calls=%fused_computation.112 | loop fusion | flops 14381056 | bytes 10108928
  400.5 18.7 %abs_reduce_fusion = (f32[]{:T(128)}, bf16[4,64,8,128]{3,2,1,0:T(8,128)(2,1)S(1)}) fusion(bf16[10,70,8,128]{3,2,1,0:T(8,128)(2,1)S(1)} %reshape.2411, f32[4,64,8]{2,1,0:T(8,128)} %copy.54, f32[4,64,8]{2,1,0:T(8,128)} %copy.53, f32[4,64,8]{2,1,0:T(8,128)} %copy.52, f32[4,64,8]{2,1,0:T(8,128)} %copy.51, f32[4,64,8]{2,1,0:T(8,128)} %copy.50, ...), kind=kLoop, calls=%fused_computation.113 | loop fusion | flops 39583744 | bytes 26616068 | tf_op jit(solution)/shard_map/reduce_max | solution.py:104
  420.2 105.1 %all-reduce.1 = (f32[1]{0:T(128)}, f32[1]{0:T(128)}) all-reduce(f32[1]{0:T(128)} %bitcast.106, f32[1]{0:T(128)} %bitcast.105), channel_id=1, replica_groups=mesh['tile'=16,'fsdp'=32] {'tile','fsdp'}, use_global_device_ids=true, to_apply=%region_5.6 | all-reduce | flops 2 | bytes 16 | tf_op jit(solution)/shard_map/pmax | solution.py:105
  525.3 1.8 maximum_multiply_fusion
  (329 shorter events, 87.4 us)
Async XLA Ops:
  7.2 231.0 %all-gather.3.cloned.1.call-start = ((), (), s32[]{:S(2)}) async-start(), calls=%async_computation | async-start | bytes 16809984 | tf_op jit(solution)/shard_map/all_gather | solution.py:87
  266.9 19.0 %collective-permute-start = (bf16[3,64,2048]{2,1,0:T(8,128)(2,1)S(1)}, bf16[3,64,2048]{2,1,0:T(8,128)(2,1)S(1)}, u32[]{:S(2)}, u32[]{:S(2)}) collective-permute-start(bf16[3,64,2048]{2,1,0:T(8,128)(2,1)S(1)} %get-tuple-element.57), channel_id=1, source_target_pairs={{0,32},{32,64},{64,96},{96,128},{128,160},{160,192},{192,224},{224... | collective-permute-start | bytes 2359304 | tf_op jit(solution)/shard_map/ppermute | solution.py:21
  269.3 20.5 %collective-permute-start.1 = (bf16[3,64,2048]{2,1,0:T(8,128)(2,1)S(1)}, bf16[3,64,2048]{2,1,0:T(8,128)(2,1)S(1)}, u32[]{:S(2)}, u32[]{:S(2)}) collective-permute-start(bf16[3,64,2048]{2,1,0:T(8,128)(2,1)S(1)} %get-tuple-element.58), channel_id=1, source_target_pairs={{32,0},{64,32},{96,64},{128,96},{160,128},{192,160},{224,192},{256... | collective-permute-start | bytes 2359304 | tf_op jit(solution)/shard_map/ppermute | solution.py:22
  338.6 21.0 %copy-start.45 = (f32[4,64,8]{1,2,0:T(8,128)S(1)}, f32[4,64,8]{1,2,0:T(8,128)}, u32[]{:S(2)}) copy-start(f32[4,64,8]{1,2,0:T(8,128)} %copy.89) | copy-start | bytes 24580
  338.6 21.0 %copy-start.43 = (f32[4,64,8]{1,2,0:T(8,128)S(1)}, f32[4,64,8]{1,2,0:T(8,128)}, u32[]{:S(2)}) copy-start(f32[4,64,8]{1,2,0:T(8,128)} %copy.94) | copy-start | bytes 24580
  338.6 21.0 %copy-start.41 = (f32[4,64,8]{1,2,0:T(8,128)S(1)}, f32[4,64,8]{1,2,0:T(8,128)}, u32[]{:S(2)}) copy-start(f32[4,64,8]{1,2,0:T(8,128)} %copy.99) | copy-start | bytes 24580
  365.0 21.3 %copy-start.19 = (f32[4,64,8]{1,2,0:T(8,128)S(1)}, f32[4,64,8]{1,2,0:T(8,128)}, u32[]{:S(2)}) copy-start(f32[4,64,8]{1,2,0:T(8,128)} %get-tuple-element.98) | copy-start | bytes 24580
  365.0 22.0 %copy-start.20 = (f32[4,64,8]{1,2,0:T(8,128)S(1)}, f32[4,64,8]{1,2,0:T(8,128)}, u32[]{:S(2)}) copy-start(f32[4,64,8]{1,2,0:T(8,128)} %get-tuple-element.62) | copy-start | bytes 24580
  365.0 22.8 %copy-start.18 = (f32[4,64,8]{1,2,0:T(8,128)S(1)}, f32[4,64,8]{1,2,0:T(8,128)}, u32[]{:S(2)}) copy-start(f32[4,64,8]{1,2,0:T(8,128)} %get-tuple-element.63) | copy-start | bytes 24580
  365.0 23.5 %copy-start.17 = (f32[4,64,8]{1,2,0:T(8,128)S(1)}, f32[4,64,8]{1,2,0:T(8,128)}, u32[]{:S(2)}) copy-start(f32[4,64,8]{1,2,0:T(8,128)} %get-tuple-element.64) | copy-start | bytes 24580
  365.0 24.3 %copy-start.16 = (f32[4,64,8]{1,2,0:T(8,128)S(1)}, f32[4,64,8]{1,2,0:T(8,128)}, u32[]{:S(2)}) copy-start(f32[4,64,8]{1,2,0:T(8,128)} %get-tuple-element.65) | copy-start | bytes 24580
  365.0 25.0 %copy-start.15 = (f32[4,64,8]{1,2,0:T(8,128)S(1)}, f32[4,64,8]{1,2,0:T(8,128)}, u32[]{:S(2)}) copy-start(f32[4,64,8]{1,2,0:T(8,128)} %get-tuple-element.66) | copy-start | bytes 24580
  365.0 25.8 %copy-start.14 = (f32[4,64,8]{1,2,0:T(8,128)S(1)}, f32[4,64,8]{1,2,0:T(8,128)}, u32[]{:S(2)}) copy-start(f32[4,64,8]{1,2,0:T(8,128)} %get-tuple-element.67) | copy-start | bytes 24580
  365.0 26.5 %copy-start.13 = (f32[4,64,8]{1,2,0:T(8,128)S(1)}, f32[4,64,8]{1,2,0:T(8,128)}, u32[]{:S(2)}) copy-start(f32[4,64,8]{1,2,0:T(8,128)} %get-tuple-element.68) | copy-start | bytes 24580
  365.1 27.2 %copy-start.12 = (f32[4,64,8]{1,2,0:T(8,128)S(1)}, f32[4,64,8]{1,2,0:T(8,128)}, u32[]{:S(2)}) copy-start(f32[4,64,8]{1,2,0:T(8,128)} %get-tuple-element.69) | copy-start | bytes 24580
  365.1 28.0 %copy-start.11 = (f32[4,64,8]{1,2,0:T(8,128)S(1)}, f32[4,64,8]{1,2,0:T(8,128)}, u32[]{:S(2)}) copy-start(f32[4,64,8]{1,2,0:T(8,128)} %get-tuple-element.70) | copy-start | bytes 24580
  365.2 28.6 %copy-start.10 = (f32[4,64,8]{1,2,0:T(8,128)S(1)}, f32[4,64,8]{1,2,0:T(8,128)}, u32[]{:S(2)}) copy-start(f32[4,64,8]{1,2,0:T(8,128)} %get-tuple-element.71) | copy-start | bytes 24580
  365.3 29.3 %copy-start.9 = (f32[4,64,8]{1,2,0:T(8,128)S(1)}, f32[4,64,8]{1,2,0:T(8,128)}, u32[]{:S(2)}) copy-start(f32[4,64,8]{1,2,0:T(8,128)} %get-tuple-element.72) | copy-start | bytes 24580
  365.4 29.9 %copy-start.8 = (f32[4,64,8]{1,2,0:T(8,128)S(1)}, f32[4,64,8]{1,2,0:T(8,128)}, u32[]{:S(2)}) copy-start(f32[4,64,8]{1,2,0:T(8,128)} %get-tuple-element.73) | copy-start | bytes 24580
  365.5 30.5 %copy-start.7 = (f32[4,64,8]{1,2,0:T(8,128)S(1)}, f32[4,64,8]{1,2,0:T(8,128)}, u32[]{:S(2)}) copy-start(f32[4,64,8]{1,2,0:T(8,128)} %get-tuple-element.74) | copy-start | bytes 24580
  365.6 31.2 %copy-start.6 = (f32[4,64,8]{1,2,0:T(8,128)S(1)}, f32[4,64,8]{1,2,0:T(8,128)}, u32[]{:S(2)}) copy-start(f32[4,64,8]{1,2,0:T(8,128)} %get-tuple-element.75) | copy-start | bytes 24580
  365.7 31.8 %copy-start.5 = (f32[4,64,8]{1,2,0:T(8,128)S(1)}, f32[4,64,8]{1,2,0:T(8,128)}, u32[]{:S(2)}) copy-start(f32[4,64,8]{1,2,0:T(8,128)} %get-tuple-element.76) | copy-start | bytes 24580
  365.8 32.5 %copy-start.4 = (f32[4,64,8]{1,2,0:T(8,128)S(1)}, f32[4,64,8]{1,2,0:T(8,128)}, u32[]{:S(2)}) copy-start(f32[4,64,8]{1,2,0:T(8,128)} %get-tuple-element.77) | copy-start | bytes 24580
  365.9 33.1 %copy-start.3 = (f32[4,64,8]{1,2,0:T(8,128)S(1)}, f32[4,64,8]{1,2,0:T(8,128)}, u32[]{:S(2)}) copy-start(f32[4,64,8]{1,2,0:T(8,128)} %get-tuple-element.78) | copy-start | bytes 24580
  (37 other events, 595.2 us)
Sparse Core Ops, SparseCore 0:
  12.6 225.5 all-gather.2
where the time goes:
time: 536 us; the launch traced here: 534 us
  waiting for transfers between devices  236 us (44%)
  local copies, waits for them, and re-layouts  110 us (21%)
  blocking collectives  105 us (20%)
  other arithmetic  54.5 us (10%)
  between operations  15.9 us (3%)
  matrix products  8.03 us (1%)
    all_gather x1, waiting for transfers between devices, local(): lax.all_gather(w_qkv, ('tile', 'fsdp'), axis=1, tiled=True)  218 us
    pmax x1, blocking collectives, local(): global_in, global_out = lax.pmax((peak_in, peak_out), ('tile', 'fsdp'))  105 us
    dot_general x49, local copies, waits for them, and re-layouts, neighbourhood(): jnp.einsum('rchd,rchd->rch', query, key_part, preferred_element_type=jnp....  45.7 us
    another operation x49, local copies, waits for them, and re-layouts  35.2 us
    unnamed x98, other arithmetic  23.6 us
    unnamed x119, local copies, waits for them, and re-layouts  21.4 us
    reduce_max x1, other arithmetic, local(): peak_out = jnp.max(jnp.abs(attended.astype(jnp.float32)))  18.7 us
    ppermute x1, waiting for transfers between devices, extended(): before = lax.ppermute(last, axis, up)  14.3 us
  transfers between devices with their start and end apart: 3, of which 3 were waited for; matrix products, arithmetic and copies ran while one was open for 2% of the time, Pallas kernels for 0%

commit v1 on v0

v1 whole, which is shorter than its diff:
```python
import functools

import jax
import jax.numpy as jnp
from jax import lax
from jax.experimental import pallas as pl
from jax.experimental.pallas import tpu as pltpu
from jax.sharding import Mesh
from jax.sharding import PartitionSpec as P

HEADS = 8
HEAD = 128
D = 2048
COLS = 64
ROWS = 4
HALO = 3
BLOCK = 16
SET = ROWS * COLS
KV_ROWS = (BLOCK + 2 * HALO) * COLS
FP_TOP = 448.0
AXES = ("y", "x", "z", "core")
GROUP = ("x", "core")
PEAK_ROWS = 16
NEG = -1e30


def device_of(y, x, z, core):
    return ((y * 4 + x) * 16 + z) * 2 + core


def head_permutations():
    main, extra = [], []
    for tile in range(16):
        m, odd = divmod(tile, 2)
        for shard in range(32):
            z, core = divmod(shard, 2)
            source = tile * 32 + shard
            cut = 10 if odd else 21
            first = 3 * m + odd

            def target(block):
                head = block % HEADS
                return device_of(2 * odd + core, head // 2, z, head % 2)

            main.append((source, target(first if shard <= cut else first + 1)))
            if shard == cut:
                extra.append((source, target(first + 1)))
    return main, extra


def column_order(head):
    d = lax.broadcasted_iota(jnp.int32, (3 * HEAD, 3 * HEAD), 1)
    r = lax.broadcasted_iota(jnp.int32, (3 * HEAD, 3 * HEAD), 0)
    natural = ((head + 2 * (d // HEAD)) % 3) * HEAD + d % HEAD
    half, m = natural // 192, natural % 192
    z, core, j = m // 12, (m % 12) // 6, m % 6
    return ((2 * half + core) * 96 + z * 6 + j == r).astype(jnp.bfloat16)


def project_kernel(scale_ref, x_ref, w_ref, order_ref, qkv_ref, top_ref, bottom_ref, w_scr):
    step = pl.program_id(0)

    @pl.when(step == 0)
    def _():
        w_scr[...] = lax.dot_general(
            w_ref[...], order_ref[...], (((0,), (0,)), ((), ())), preferred_element_type=jnp.float32
        ).astype(jnp.bfloat16)

    out = jnp.dot(x_ref[0], w_scr[...], preferred_element_type=jnp.float32) * scale_ref[0]
    out = out.astype(jnp.bfloat16)
    qkv_ref[0] = out
    for core in range(2):

        @pl.when(step == core)
        def _():
            top_ref[core] = out[: HALO * COLS, HEAD:]

        @pl.when(step == 6 + core)
        def _():
            bottom_ref[core] = out[SET - HALO * COLS :, HEAD:]


def project(scale, tokens, weights, order):
    halo = jax.ShapeDtypeStruct((2, HALO * COLS, 2 * HEAD), jnp.bfloat16)
    whole = lambda *shape: pl.BlockSpec(shape, lambda g: (0,) * len(shape))
    return pl.pallas_call(
        project_kernel,
        grid=(8,),
        out_shape=(jax.ShapeDtypeStruct((8, SET, 3 * HEAD), jnp.bfloat16), halo, halo),
        in_specs=[
            pl.BlockSpec(memory_space=pltpu.SMEM),
            pl.BlockSpec((1, SET, D), lambda g: (g, 0, 0)),
            whole(3 * HEAD, D),
            whole(3 * HEAD, 3 * HEAD),
        ],
        out_specs=(
            pl.BlockSpec((1, SET, 3 * HEAD), lambda g: (g, 0, 0)),
            whole(2, HALO * COLS, 2 * HEAD),
            whole(2, HALO * COLS, 2 * HEAD),
        ),
        scratch_shapes=[pltpu.VMEM((D, 3 * HEAD), jnp.bfloat16)],
        compiler_params=pltpu.CompilerParams(vmem_limit_bytes=40 * 2**20),
        cost_estimate=pl.CostEstimate(
            flops=2 * 8 * SET * D * 3 * HEAD, bytes_accessed=12 * 2**20, transcendentals=0
        ),
        name="project",
    )(scale, tokens, weights, order)


def attend_kernel(place_ref, peak_ref, qkv_ref, above_ref, below_ref, out_ref, kv):
    base = place_ref[0]
    scaling = float(HEAD) ** -0.5
    shape = (2 * COLS, 8 * COLS)
    q_row = lax.broadcasted_iota(jnp.int32, shape, 0)
    k_row = lax.broadcasted_iota(jnp.int32, shape, 1)
    row_step = k_row // COLS - q_row // COLS
    col_step = k_row % COLS - q_row % COLS
    window = (row_step >= 0) & (row_step <= 2 * HALO) & (col_step >= -HALO) & (col_step <= HALO)
    window = jnp.where(window, 0.0, NEG)
    centre = jnp.where((row_step == HALO) & (col_step == 0), 0.0, NEG)
    key_at = lax.broadcasted_iota(jnp.int32, (1, 8 * COLS), 1)
    query_at = lax.broadcasted_iota(jnp.int32, (2 * COLS, 1), 0)
    highest = jnp.zeros((2 * COLS, HEAD), jnp.float32)
    for image in range(2):
        ext_rows, ext_cols = place_ref[1 + 2 * image], place_ref[2 + 2 * image]
        kv[image, : HALO * COLS] = above_ref[image]
        for part in range(4):
            start = HALO * COLS + part * SET
            kv[image, start : start + SET] = qkv_ref[2 * part + image, :, HEAD:]
        kv[image, KV_ROWS - HALO * COLS :] = below_ref[image]
        for pair in range(BLOCK // 2):
            group, inner = 2 * (pair // 2) + image, (pair % 2) * 2 * COLS
            query = qkv_ref[group, inner : inner + 2 * COLS, :HEAD]
            start = 2 * pair * COLS
            keys = kv[image, start : start + 8 * COLS, :HEAD]
            values = kv[image, start : start + 8 * COLS, HEAD:]
            scores = lax.dot_general(
                query, keys, (((1,), (1,)), ((), ())), preferred_element_type=jnp.float32
            )
            key_rows = base + (2 * pair - HALO) + key_at // COLS
            key_cols = key_at % COLS
            valid = (key_rows >= 0) & (key_rows < ext_rows) & (key_cols < ext_cols)
            bias = jnp.maximum(jnp.where(valid, 0.0, NEG), centre) + window
            scores = scores * scaling + bias
            weights = jnp.exp(scores - jnp.max(scores, axis=1, keepdims=True))
            weights = weights * (1.0 / jnp.sum(weights, axis=1, keepdims=True))
            result = jnp.dot(
                weights.astype(jnp.bfloat16), values, preferred_element_type=jnp.float32
            )
            inside = (base + 2 * pair + query_at // COLS < ext_rows) & (query_at % COLS < ext_cols)
            result = jnp.where(inside, result, 0.0)
            highest = jnp.maximum(highest, jnp.abs(result))
            out_ref[group, inner : inner + 2 * COLS, :] = result.astype(jnp.bfloat16)
    peak_out = jnp.max(highest, axis=0, keepdims=True)
    lines = lax.broadcasted_iota(jnp.int32, (PEAK_ROWS, HEAD), 0)
    peaks = jnp.where(lines < PEAK_ROWS // 2, peak_out, peak_ref[0]).astype(jnp.bfloat16)
    for group in range(8):
        out_ref[group, SET:, :] = peaks


def attend(place, peak_in, qkv, above, below):
    vmem = pl.BlockSpec(memory_space=pltpu.VMEM)
    smem = pl.BlockSpec(memory_space=pltpu.SMEM)
    return pl.pallas_call(
        attend_kernel,
        out_shape=jax.ShapeDtypeStruct((8, SET + PEAK_ROWS, HEAD), jnp.bfloat16),
        in_specs=[smem, smem, vmem, vmem, vmem],
        out_specs=vmem,
        scratch_shapes=[pltpu.VMEM((2, KV_ROWS, 2 * HEAD), jnp.bfloat16)],
        compiler_params=pltpu.CompilerParams(vmem_limit_bytes=40 * 2**20),
        cost_estimate=pl.CostEstimate(
            flops=4 * 16 * 128 * 512 * HEAD, bytes_accessed=3 * 2**20, transcendentals=16 * 128 * 512
        ),
        name="attend",
    )(place, peak_in, qkv, above, below)


def spread(value, axis):
    size = lax.axis_size(axis)
    copies = jnp.broadcast_to(value[None], (size,) + value.shape)
    return lax.all_to_all(copies, axis, 0, 0, tiled=True)


def head_weights(w_qkv):
    main, extra = head_permutations()
    mine = w_qkv.T
    first = lax.ppermute(mine, AXES, main)
    second = lax.ppermute(mine, AXES, extra)
    y, z = lax.axis_index("y"), lax.axis_index("z")
    shard = 2 * z + y % 2
    cut = jnp.where((y < 2) & (shard == 21), 2, jnp.where((y >= 2) & (shard == 10), 4, 6))
    column = lax.broadcasted_iota(jnp.int32, mine.shape, 0)
    merged = jnp.where(column < cut, first, second)
    with jax.named_scope("weights_over_z"):
        over_z = spread(merged.reshape(96, 128), "z").reshape(96, D)
    with jax.named_scope("weights_over_y"):
        return spread(over_z, "y").reshape(3 * HEAD, D)


def local(images, w_qkv, prev_scale, extent):
    flat = images.reshape(SET, D).astype(jnp.float32)
    quantized = jnp.clip(flat / prev_scale[0], -FP_TOP, FP_TOP).astype(jnp.bfloat16)
    peak_in = jnp.max(jnp.abs(flat)).reshape(1)
    with jax.named_scope("tokens"):
        tokens = lax.all_gather(quantized, GROUP, axis=0, tiled=False)
    weights = head_weights(w_qkv)
    core = lax.axis_index("core")
    order = column_order(2 * lax.axis_index("x") + core)
    other = lax.ppermute(extent, "core", [(0, 1), (1, 0)])
    extents = jnp.where(core == 0, jnp.concatenate([extent, other]), jnp.concatenate([other, extent]))
    place = jnp.concatenate([(lax.axis_index("y") * BLOCK).reshape(1), extents.reshape(4)])
    qkv, top, bottom = project(prev_scale, tokens, weights, order)
    with jax.named_scope("halo"):
        above = lax.ppermute(bottom, "y", [(i, i + 1) for i in range(3)])
        below = lax.ppermute(top, "y", [(i + 1, i) for i in range(3)])
    mixed = attend(place.astype(jnp.int32), peak_in, qkv, above, below)
    with jax.named_scope("heads"):
        mixed = lax.all_to_all(mixed, GROUP, 0, 0, tiled=True)
    attended = mixed[:, :SET].transpose(1, 0, 2).reshape(1, ROWS, COLS, HEADS * HEAD)
    peaks = mixed[:, SET:].astype(jnp.float32).reshape(8, 2, PEAK_ROWS // 2, HEAD)
    peaks = jnp.max(peaks, axis=(0, 2, 3))[::-1]
    for axis in ("y", "z"):
        with jax.named_scope("peaks"):
            peaks = jnp.max(spread(peaks, axis).reshape(-1, 2), axis=0)
    return attended, peaks / FP_TOP


def solution(mesh):
    fine = Mesh(mesh.devices.reshape(4, 4, 16, 2), AXES)
    rows, columns = ("z", "core"), ("y", "x")
    return jax.shard_map(
        local,
        mesh=fine,
        in_specs=(P(rows, columns, None, None), P(None, AXES), P(), P(rows, None)),
        out_specs=(P(rows, columns, None, None), P()),
        check_vma=False,
    )
```

time: 536 us -> 164 us (0.31)
  waiting for transfers between devices: 236 us -> 32.5 us
  local copies, waits for them, and re-layouts: 110 us -> 7.35 us
  other arithmetic: 54.5 us -> 4.4 us
  blocking collectives: 105 us -> 62.5 us
  starting transfers between devices: 3.69 us -> 26.1 us
  Pallas kernels: 0 us -> 14.7 us
  matrix products: 8.03 us -> 0 us
    all_gather x1, waiting for transfers between devices: 218 us -> 0.01 us  [local(): tokens = lax.all_gather(quantized, GROUP, axis=0, tiled=False)]
    pmax x1 -> x0, blocking collectives: 105 us -> none  [local(): global_in, global_out = lax.pmax((peak_in, peak_out), ('tile', 'fsdp'))]
    all_to_all x0 -> x3, blocking collectives: none -> 62.5 us  [the longest x2 43.4 us: spread(): return lax.all_to_all(copies, axis, 0, 0, tiled=True)]
    dot_general x49 -> x0, local copies, waits for them, and re-layouts: 45.7 us -> none  [neighbourhood(): jnp.einsum('rchd,rchd->rch', query, key_part, preferred_element_type=jnp....]
    another operation x50 -> x0, local copies, waits for them, and re-layouts: 36.2 us -> none
    unnamed x98 -> x0, other arithmetic: 23.6 us -> none
    all_to_all x0 -> x2, waiting for transfers between devices: none -> 23.4 us  [spread(): return lax.all_to_all(copies, axis, 0, 0, tiled=True)]
    reduce_max x3 -> x4, other arithmetic: 21 us -> 0.3 us  [the longest x2 0.24 us: local(): peaks = jnp.max(peaks, axis=(0, 2, 3))[::-1]]
  transfers between devices with their start and end apart: 3 -> 8, of which waited for: 3 -> 5; matrix products, arithmetic and copies ran while one was open for 2% -> 2% of each run, Pallas kernels for 0% -> 5%
where the time goes in v1:
time: 164 us; the launch traced here: 162 us
  blocking collectives  62.5 us (38%)
  waiting for transfers between devices  32.5 us (20%)
  starting transfers between devices  26.1 us (16%)
  between operations  14.9 us (9%)
  Pallas kernels  14.7 us (9%)
  local copies, waits for them, and re-layouts  7.35 us (4%)
  other arithmetic  4.4 us (3%)
    all_to_all x2, blocking collectives, spread(): return lax.all_to_all(copies, axis, 0, 0, tiled=True)  43.4 us
    all_to_all x2, waiting for transfers between devices, spread(): return lax.all_to_all(copies, axis, 0, 0, tiled=True)  23.4 us
    all_to_all x1, blocking collectives, local(): mixed = lax.all_to_all(mixed, GROUP, 0, 0, tiled=True)  19.1 us
    all_to_all x2, starting transfers between devices, spread(): return lax.all_to_all(copies, axis, 0, 0, tiled=True)  12.9 us
    pallas_call x1, Pallas kernels, project(): pl.pallas_call(project_kernel, grid=(8,), out_shape=(jax.ShapeDtypeStruct...  7.8 us
    pallas_call x1, Pallas kernels, attend(): pl.pallas_call(attend_kernel, out_shape=jax.ShapeDtypeStruct((8, SET + PE...  6.87 us
    ppermute x1, starting transfers between devices, head_weights(): first = lax.ppermute(mine, AXES, main)  4.59 us
    ppermute x1, starting transfers between devices, local(): other = lax.ppermute(extent, 'core', [(0, 1), (1, 0)])  4.37 us
  transfers between devices with their start and end apart: 8, of which 5 were waited for; matrix products, arithmetic and copies ran while one was open for 2% of the time, Pallas kernels for 5%

profile of v1, /device:TPU:1, one launch (start us, length us, event | category | flops | bytes accessed | tf_op | source)
XLA Modules:
  0.0 162.4 jit_solution(9716859328955528089)
XLA Ops:
  7.9 3.1 %fusion.2 = (bf16[1,4,64,2048]{3,2,1,0:T(8,128)(2,1)}, f32[]{:T(128)}) fusion(bf16[1,4,64,2048]{3,2,1,0:T(8,128)(2,1)} %param.4, f32[]{:T(128)} %bitcast.8), kind=kLoop, calls=%fused_computation.4 | loop fusion | flops 3145727 | bytes 2097160 | tf_op jit(solution)/shard_map/convert_element_type | solution.py:202
  11.0 0.7 collective-permute-start.2
  11.7 4.6 %collective-permute-start.1 = (bf16[6,2048]{1,0:T(8,128)(2,1)S(1)}, bf16[6,2048]{1,0:T(8,128)(2,1)S(1)}, u32[]{:S(2)}, u32[]{:S(2)}) collective-permute-start(bf16[6,2048]{1,0:T(8,128)(2,1)S(1)} %bitcast.12), channel_id=1, source_target_pairs={{0,0},{1,128},{2,2},{3,130},{4,4},{5,132},{6,6},{7,134},{8,8},{9,1... | collective-permute-start | bytes 73736 | tf_op jit(solution)/shard_map/ppermute | solution.py:187
  16.3 4.0 %collective-permute-done.1 = bf16[6,2048]{1,0:T(8,128)(2,1)S(1)} collective-permute-done((bf16[6,2048]{1,0:T(8,128)(2,1)S(1)}, bf16[6,2048]{1,0:T(8,128)(2,1)S(1)}, u32[]{:S(2)}, u32[]{:S(2)}) %collective-permute-start.1) | collective-permute-done | bytes 24608 | tf_op jit(solution)/shard_map/ppermute | solution.py:187
  20.5 36.4 %all_to_all.27 = bf16[16,96,128]{2,1,0:T(8,128)(2,1)S(1)} all-to-all(bf16[16,96,128]{2,1,0:T(8,128)(2,1)S(1)} %broadcast_in_dim.13), channel_id=1, replica_groups=mesh['y'=4,'x'=4,'z'=16,'core'=2] {'z'}, dimensions={0} | all-to-all | bytes 786432 | tf_op jit(solution)/shard_map/weights_over_z/all_to_all | solution.py:181
  57.2 1.4 broadcast_in_dim.29
  58.6 6.9 %all-to-all-start.1 = ((bf16[4,96,2048]{2,1,0:T(8,128)(2,1)}), bf16[4,96,2048]{2,1,0:T(8,128)(2,1)S(1)}, u32[]{:S(2)}, u32[]{:S(2)}) async-start(bf16[4,96,2048]{2,1,0:T(8,128)(2,1)} %broadcast_in_dim.29), calls=%async_computation.1 | async-start | bytes 3145728 | tf_op jit(solution)/shard_map/weights_over_y/all_to_all | solution.py:181
  65.5 4.4 %collective-permute-start = (s32[1,2]{1,0:T(1,128)S(1)}, s32[1,2]{1,0:T(1,128)S(1)}, u32[]{:S(2)}, u32[]{:S(2)}) collective-permute-start(s32[1,2]{1,0:T(1,128)S(1)} %copy-done.1), channel_id=1, source_target_pairs={{0,1},{1,0},{2,3},{3,2},{4,5},{5,4},{6,7},{7,6},{8,9},{9,8},{10,11... | collective-permute-start | bytes 32 | tf_op jit(solution)/shard_map/ppermute | solution.py:209
  70.2 13.6 %all-to-all-done.1 = bf16[4,96,2048]{2,1,0:T(8,128)(2,1)S(1)} async-done(((bf16[4,96,2048]{2,1,0:T(8,128)(2,1)}), bf16[4,96,2048]{2,1,0:T(8,128)(2,1)S(1)}, u32[]{:S(2)}, u32[]{:S(2)}) %all-to-all-start.1) | async-done | bytes 1572896 | tf_op jit(solution)/shard_map/weights_over_y/all_to_all | solution.py:181
  83.7 3.4 %copy-done = bf16[8,256,2048]{2,1,0:T(8,128)(2,1)S(1)} copy-done((bf16[8,256,2048]{2,1,0:T(8,128)(2,1)S(1)}, bf16[8,256,2048]{2,1,0:T(8,128)(2,1)}, u32[]{:S(2)}) %copy-start) | copy-done | bytes 8388632
  87.1 7.8 %project.1 = (bf16[8,256,384]{2,1,0:T(8,128)(2,1)S(1)}, bf16[2,192,256]{2,1,0:T(8,128)(2,1)}, bf16[2,192,256]{2,1,0:T(8,128)(2,1)}) custom-call(f32[1]{0:T(128)} %copy.14.scale_ref, bf16[8,256,2048]{2,1,0:T(8,128)(2,1)S(1)} %copy-done, bf16[384,2048]{1,0:T(8,128)(2,1)S(1)} %bitcast.9, bf16[384,384]{1,0:T(8,128)(2,1)S(1)} %fusion.18.order_ref), custom_call_target="tpu_custom_call" | custom-call | flops 3221225472 | bytes 12582912 | tf_op jit(solution)/shard_map/project/pallas_call | solution.py:86
  94.9 2.2 %collective-permute-start.3 = (bf16[2,192,256]{2,1,0:T(8,128)(2,1)}, bf16[2,192,256]{2,1,0:T(8,128)(2,1)S(1)}, u32[]{:S(2)}, u32[]{:S(2)}) collective-permute-start(bf16[2,192,256]{2,1,0:T(8,128)(2,1)} %get-tuple-element.6), channel_id=1, source_target_pairs={{0,128},{128,256},{256,384},{1,129},{129,257},{257,385},{2,130},{1... | collective-permute-start | bytes 589832 | tf_op jit(solution)/shard_map/halo/ppermute | solution.py:214
  97.1 1.3 collective-permute-start.4
  98.6 1.4 collective-permute-done.3.above_ref
  100.0 3.7 %collective-permute-done.4.below_ref = bf16[2,192,256]{2,1,0:T(8,128)(2,1)S(1)} collective-permute-done((bf16[2,192,256]{2,1,0:T(8,128)(2,1)}, bf16[2,192,256]{2,1,0:T(8,128)(2,1)S(1)}, u32[]{:S(2)}, u32[]{:S(2)}) %collective-permute-start.4) | collective-permute-done | bytes 196640 | tf_op jit(solution)/shard_map/halo/ppermute | solution.py:215
  103.7 6.9 %attend.1 = bf16[8,272,128]{2,1,0:T(8,128)(2,1)S(1)} custom-call(s32[5]{0:T(128)S(1)} %pad_add_fusion.place_ref, f32[1]{0:T(128)} %bitcast.1.peak_ref, bf16[8,256,384]{2,1,0:T(8,128)(2,1)S(1)} %get-tuple-element.5.qkv_ref, bf16[2,192,256]{2,1,0:T(8,128)(2,1)S(1)} %collective-permute-done.3.above_ref, bf16[2,192,256]{2,1,0:T(8,128)(2,1)S(1)} %collective-permute-done.4.below_ref), custom_call_target="tpu_custom_call" | custom-call | flops 536870912 | bytes 3145728 | tf_op jit(solution)/shard_map/attend/pallas_call | solution.py:164
  110.6 19.1 %all_to_all.28 = bf16[8,272,128]{2,1,0:T(8,128)(2,1)S(1)} all-to-all(bf16[8,272,128]{2,1,0:T(8,128)(2,1)S(1)} %attend.1), channel_id=1, replica_groups=mesh['y'=4,'x'=4,'z'=16,'core'=2] {'x','core'}, dimensions={0} | all-to-all | bytes 1114112 | tf_op jit(solution)/shard_map/heads/all_to_all | solution.py:218
  130.1 6.9 %all_to_all.29 = f32[4,1,2]{2,1,0:T(1,128)S(1)} all-to-all(f32[4,1,2]{2,1,0:T(1,128)S(1)} %broadcast_in_dim.30), channel_id=1, replica_groups=mesh['y'=4,'x'=4,'z'=16,'core'=2] {'y'}, dimensions={0} | all-to-all | bytes 64 | tf_op jit(solution)/shard_map/peaks/all_to_all | solution.py:181
  137.1 0.6 broadcast_in_dim.31
  137.7 6.0 %all-to-all-start.4 = ((f32[16,1,2]{2,1,0:T(1,128)}), f32[16,1,2]{2,1,0:T(1,128)S(1)}, u32[]{:S(2)}, u32[]{:S(2)}) async-start(f32[16,1,2]{2,1,0:T(1,128)} %broadcast_in_dim.31), calls=%async_computation.4 | async-start | bytes 16384 | tf_op jit(solution)/shard_map/peaks/all_to_all | solution.py:181
  143.8 0.3 copy.9
  144.1 1.0 reshape.70
  145.2 9.8 %all-to-all-done.4 = f32[16,1,2]{2,1,0:T(1,128)S(1)} async-done(((f32[16,1,2]{2,1,0:T(1,128)}), f32[16,1,2]{2,1,0:T(1,128)S(1)}, u32[]{:S(2)}, u32[]{:S(2)}) %all-to-all-start.4) | async-done | bytes 160 | tf_op jit(solution)/shard_map/peaks/all_to_all | solution.py:181
  155.0 0.5 broadcast_multiply_fusion
  (30 shorter events, 1.4 us)
Async XLA Ops:
  7.2 3.8 %copy-start.2 = (bf16[2048,6]{0,1:T(8,128)(2,1)S(1)}, bf16[2048,6]{0,1:T(8,128)(2,1)}, u32[]{:S(2)}) copy-start(bf16[2048,6]{0,1:T(8,128)(2,1)} %param.5) | copy-start | bytes 73732
  7.2 76.5 %all-gather.2.cloned.1.call-start = ((), (), s32[]{:S(2)}) async-start(), calls=%async_computation.5 | async-start | bytes 9437184 | tf_op jit(solution)/shard_map/tokens/all_gather | solution.py:205
  11.0 5.3 %collective-permute-start.2 = (bf16[6,2048]{1,0:T(8,128)(2,1)S(1)}, bf16[6,2048]{1,0:T(8,128)(2,1)S(1)}, u32[]{:S(2)}, u32[]{:S(2)}) collective-permute-start(bf16[6,2048]{1,0:T(8,128)(2,1)S(1)} %bitcast.11), channel_id=1, source_target_pairs={{21,149},{42,298},{85,212},{106,331},{149,245},{170,266},{213,180}... | collective-permute-start | bytes 73736 | tf_op jit(solution)/shard_map/ppermute | solution.py:188
  11.7 8.6 %collective-permute-start.1 = (bf16[6,2048]{1,0:T(8,128)(2,1)S(1)}, bf16[6,2048]{1,0:T(8,128)(2,1)S(1)}, u32[]{:S(2)}, u32[]{:S(2)}) collective-permute-start(bf16[6,2048]{1,0:T(8,128)(2,1)S(1)} %bitcast.12), channel_id=1, source_target_pairs={{0,0},{1,128},{2,2},{3,130},{4,4},{5,132},{6,6},{7,134},{8,8},{9,1... | collective-permute-start | bytes 73736 | tf_op jit(solution)/shard_map/ppermute | solution.py:187
  57.1 8.3 %copy-start.1 = (s32[1,2]{1,0:T(1,128)S(1)}, s32[1,2]{1,0:T(1,128)}, u32[]{:S(2)}) copy-start(s32[1,2]{1,0:T(1,128)} %param.7) | copy-start | bytes 28
  58.6 25.1 %all-to-all-start.1 = ((bf16[4,96,2048]{2,1,0:T(8,128)(2,1)}), bf16[4,96,2048]{2,1,0:T(8,128)(2,1)S(1)}, u32[]{:S(2)}, u32[]{:S(2)}) async-start(bf16[4,96,2048]{2,1,0:T(8,128)(2,1)} %broadcast_in_dim.29), calls=%async_computation.1 | async-start | bytes 3145728 | tf_op jit(solution)/shard_map/weights_over_y/all_to_all | solution.py:181
  65.5 33.0 %collective-permute-start = (s32[1,2]{1,0:T(1,128)S(1)}, s32[1,2]{1,0:T(1,128)S(1)}, u32[]{:S(2)}, u32[]{:S(2)}) collective-permute-start(s32[1,2]{1,0:T(1,128)S(1)} %copy-done.1), channel_id=1, source_target_pairs={{0,1},{1,0},{2,3},{3,2},{4,5},{5,4},{6,7},{7,6},{8,9},{9,8},{10,11... | collective-permute-start | bytes 32 | tf_op jit(solution)/shard_map/ppermute | solution.py:209
  83.7 3.4 %copy-start = (bf16[8,256,2048]{2,1,0:T(8,128)(2,1)S(1)}, bf16[8,256,2048]{2,1,0:T(8,128)(2,1)}, u32[]{:S(2)}) copy-start(bf16[8,256,2048]{2,1,0:T(8,128)(2,1)} %all-gather.2.cloned.1.call-done.x_ref) | copy-start | bytes 25165828
  94.9 5.1 %collective-permute-start.3 = (bf16[2,192,256]{2,1,0:T(8,128)(2,1)}, bf16[2,192,256]{2,1,0:T(8,128)(2,1)S(1)}, u32[]{:S(2)}, u32[]{:S(2)}) collective-permute-start(bf16[2,192,256]{2,1,0:T(8,128)(2,1)} %get-tuple-element.6), channel_id=1, source_target_pairs={{0,128},{128,256},{256,384},{1,129},{129,257},{257,385},{2,130},{1... | collective-permute-start | bytes 589832 | tf_op jit(solution)/shard_map/halo/ppermute | solution.py:214
  97.1 6.6 %collective-permute-start.4 = (bf16[2,192,256]{2,1,0:T(8,128)(2,1)}, bf16[2,192,256]{2,1,0:T(8,128)(2,1)S(1)}, u32[]{:S(2)}, u32[]{:S(2)}) collective-permute-start(bf16[2,192,256]{2,1,0:T(8,128)(2,1)} %get-tuple-element.7), channel_id=1, source_target_pairs={{128,0},{256,128},{384,256},{129,1},{257,129},{385,257},{130,2},{2... | collective-permute-start | bytes 589832 | tf_op jit(solution)/shard_map/halo/ppermute | solution.py:215
  137.7 17.3 %all-to-all-start.4 = ((f32[16,1,2]{2,1,0:T(1,128)}), f32[16,1,2]{2,1,0:T(1,128)S(1)}, u32[]{:S(2)}, u32[]{:S(2)}) async-start(f32[16,1,2]{2,1,0:T(1,128)} %broadcast_in_dim.31), calls=%async_computation.4 | async-start | bytes 16384 | tf_op jit(solution)/shard_map/peaks/all_to_all | solution.py:181
Sparse Core Ops, SparseCore 0:
  11.1 63.0 all-gather.1

commit v2 on v1

--- a/solution.py
+++ b/solution.py
@@ -1,4 +1,4 @@
-import functools
+import math
 
 import jax
 import jax.numpy as jnp
@@ -58,48 +58,36 @@
 
 
 def project_kernel(scale_ref, x_ref, w_ref, order_ref, qkv_ref, top_ref, bottom_ref, w_scr):
-    step = pl.program_id(0)
-
-    @pl.when(step == 0)
-    def _():
-        w_scr[...] = lax.dot_general(
-            w_ref[...], order_ref[...], (((0,), (0,)), ((), ())), preferred_element_type=jnp.float32
-        ).astype(jnp.bfloat16)
-
-    out = jnp.dot(x_ref[0], w_scr[...], preferred_element_type=jnp.float32) * scale_ref[0]
-    out = out.astype(jnp.bfloat16)
-    qkv_ref[0] = out
-    for core in range(2):
-
-        @pl.when(step == core)
-        def _():
-            top_ref[core] = out[: HALO * COLS, HEAD:]
-
-        @pl.when(step == 6 + core)
-        def _():
-            bottom_ref[core] = out[SET - HALO * COLS :, HEAD:]
+    scale = scale_ref[0]
+    inverse = 1.0 / scale
+    w_scr[...] = lax.dot_general(
+        order_ref[...], w_ref[...], (((0,), (0,)), ((), ())), preferred_element_type=jnp.float32
+    ).astype(jnp.bfloat16)
+    for part in range(4):
+        tokens = x_ref[2 * part : 2 * part + 2].reshape(2 * SET, D)
+        tokens = (tokens.astype(jnp.float32) * inverse).astype(jnp.bfloat16)
+        tokens = jnp.clip(tokens, -FP_TOP, FP_TOP)
+        out = lax.dot_general(
+            tokens, w_scr[...], (((1,), (1,)), ((), ())), preferred_element_type=jnp.float32
+        )
+        out = (out * scale).astype(jnp.bfloat16).reshape(2, SET, 3 * HEAD)
+        qkv_ref[2 * part : 2 * part + 2] = out
+        if part == 0:
+            top_ref[...] = out[:, : HALO * COLS, HEAD:]
+        if part == 3:
+            bottom_ref[...] = out[:, SET - HALO * COLS :, HEAD:]
 
 
 def project(scale, tokens, weights, order):
     halo = jax.ShapeDtypeStruct((2, HALO * COLS, 2 * HEAD), jnp.bfloat16)
-    whole = lambda *shape: pl.BlockSpec(shape, lambda g: (0,) * len(shape))
+    vmem = pl.BlockSpec(memory_space=pltpu.VMEM)
     return pl.pallas_call(
         project_kernel,
-        grid=(8,),
         out_shape=(jax.ShapeDtypeStruct((8, SET, 3 * HEAD), jnp.bfloat16), halo, halo),
-        in_specs=[
-            pl.BlockSpec(memory_space=pltpu.SMEM),
-            pl.BlockSpec((1, SET, D), lambda g: (g, 0, 0)),
-            whole(3 * HEAD, D),
-            whole(3 * HEAD, 3 * HEAD),
-        ],
-        out_specs=(
-            pl.BlockSpec((1, SET, 3 * HEAD), lambda g: (g, 0, 0)),
-            whole(2, HALO * COLS, 2 * HEAD),
-            whole(2, HALO * COLS, 2 * HEAD),
-        ),
-        scratch_shapes=[pltpu.VMEM((D, 3 * HEAD), jnp.bfloat16)],
-        compiler_params=pltpu.CompilerParams(vmem_limit_bytes=40 * 2**20),
+        in_specs=[pl.BlockSpec(memory_space=pltpu.SMEM), vmem, vmem, vmem],
+        out_specs=(vmem, vmem, vmem),
+        scratch_shapes=[pltpu.VMEM((3 * HEAD, D), jnp.bfloat16)],
+        compiler_params=pltpu.CompilerParams(vmem_limit_bytes=24 * 2**20),
         cost_estimate=pl.CostEstimate(
             flops=2 * 8 * SET * D * 3 * HEAD, bytes_accessed=12 * 2**20, transcendentals=0
         ),
@@ -129,8 +117,8 @@
             kv[image, start : start + SET] = qkv_ref[2 * part + image, :, HEAD:]
         kv[image, KV_ROWS - HALO * COLS :] = below_ref[image]
         for pair in range(BLOCK // 2):
-            group, inner = 2 * (pair // 2) + image, (pair % 2) * 2 * COLS
-            query = qkv_ref[group, inner : inner + 2 * COLS, :HEAD]
+            part, inner = pair // 2, (pair % 2) * 2 * COLS
+            query = qkv_ref[2 * part + image, inner : inner + 2 * COLS, :HEAD]
             start = 2 * pair * COLS
             keys = kv[image, start : start + 8 * COLS, :HEAD]
             values = kv[image, start : start + 8 * COLS, HEAD:]
@@ -140,7 +128,7 @@
             key_rows = base + (2 * pair - HALO) + key_at // COLS
             key_cols = key_at % COLS
             valid = (key_rows >= 0) & (key_rows < ext_rows) & (key_cols < ext_cols)
-            bias = jnp.maximum(jnp.where(valid, 0.0, NEG), centre) + window
+            bias = jnp.where(valid, window, centre)
             scores = scores * scaling + bias
             weights = jnp.exp(scores - jnp.max(scores, axis=1, keepdims=True))
             weights = weights * (1.0 / jnp.sum(weights, axis=1, keepdims=True))
@@ -148,12 +136,11 @@
                 weights.astype(jnp.bfloat16), values, preferred_element_type=jnp.float32
             )
             inside = (base + 2 * pair + query_at // COLS < ext_rows) & (query_at % COLS < ext_cols)
-            result = jnp.where(inside, result, 0.0)
-            highest = jnp.maximum(highest, jnp.abs(result))
-            out_ref[group, inner : inner + 2 * COLS, :] = result.astype(jnp.bfloat16)
-    peak_out = jnp.max(highest, axis=0, keepdims=True)
+            result = jnp.where(inside, result, 0.0).astype(jnp.bfloat16)
+            highest = jnp.maximum(highest, jnp.abs(result.astype(jnp.float32)))
+            out_ref[2 * part + image, inner : inner + 2 * COLS, :] = result
     lines = lax.broadcasted_iota(jnp.int32, (PEAK_ROWS, HEAD), 0)
-    peaks = jnp.where(lines < PEAK_ROWS // 2, peak_out, peak_ref[0]).astype(jnp.bfloat16)
+    peaks = jnp.where(lines < PEAK_ROWS // 2, peak_ref[0], jnp.max(highest)).astype(jnp.bfloat16)
     for group in range(8):
         out_ref[group, SET:, :] = peaks
 
@@ -167,7 +154,7 @@
         in_specs=[smem, smem, vmem, vmem, vmem],
         out_specs=vmem,
         scratch_shapes=[pltpu.VMEM((2, KV_ROWS, 2 * HEAD), jnp.bfloat16)],
-        compiler_params=pltpu.CompilerParams(vmem_limit_bytes=40 * 2**20),
+        compiler_params=pltpu.CompilerParams(vmem_limit_bytes=24 * 2**20),
         cost_estimate=pl.CostEstimate(
             flops=4 * 16 * 128 * 512 * HEAD, bytes_accessed=3 * 2**20, transcendentals=16 * 128 * 512
         ),
@@ -176,12 +163,17 @@
 
 
 def spread(value, axis):
-    size = lax.axis_size(axis)
+    size = math.prod(lax.axis_size(name) for name in ((axis,) if isinstance(axis, str) else axis))
     copies = jnp.broadcast_to(value[None], (size,) + value.shape)
     return lax.all_to_all(copies, axis, 0, 0, tiled=True)
 
 
-def head_weights(w_qkv):
+def shift(value, axis, step):
+    size = lax.axis_size(axis)
+    return lax.ppermute(value, axis, [(i, (i + step) % size) for i in range(size)])
+
+
+def head_weights(w_qkv, images):
     main, extra = head_permutations()
     mine = w_qkv.T
     first = lax.ppermute(mine, AXES, main)
@@ -193,32 +185,31 @@
     merged = jnp.where(column < cut, first, second)
     with jax.named_scope("weights_over_z"):
         over_z = spread(merged.reshape(96, 128), "z").reshape(96, D)
+    over_z, late = lax.optimization_barrier((over_z, images))
     with jax.named_scope("weights_over_y"):
-        return spread(over_z, "y").reshape(3 * HEAD, D)
+        return spread(over_z, "y").reshape(3 * HEAD, D), late
 
 
 def local(images, w_qkv, prev_scale, extent):
-    flat = images.reshape(SET, D).astype(jnp.float32)
-    quantized = jnp.clip(flat / prev_scale[0], -FP_TOP, FP_TOP).astype(jnp.bfloat16)
-    peak_in = jnp.max(jnp.abs(flat)).reshape(1)
     with jax.named_scope("tokens"):
-        tokens = lax.all_gather(quantized, GROUP, axis=0, tiled=False)
-    weights = head_weights(w_qkv)
+        tokens = lax.all_gather(images.reshape(SET, D), GROUP, axis=0, tiled=False)
+    weights, late = head_weights(w_qkv, images)
+    peak_in = jnp.max(jnp.abs(late)).astype(jnp.float32).reshape(1)
     core = lax.axis_index("core")
     order = column_order(2 * lax.axis_index("x") + core)
-    other = lax.ppermute(extent, "core", [(0, 1), (1, 0)])
+    other = shift(extent, "core", 1)
     extents = jnp.where(core == 0, jnp.concatenate([extent, other]), jnp.concatenate([other, extent]))
-    place = jnp.concatenate([(lax.axis_index("y") * BLOCK).reshape(1), extents.reshape(4)])
+    place = jnp.stack([lax.axis_index("y") * BLOCK, *extents.reshape(4)]).astype(jnp.int32)
     qkv, top, bottom = project(prev_scale, tokens, weights, order)
     with jax.named_scope("halo"):
         above = lax.ppermute(bottom, "y", [(i, i + 1) for i in range(3)])
         below = lax.ppermute(top, "y", [(i + 1, i) for i in range(3)])
-    mixed = attend(place.astype(jnp.int32), peak_in, qkv, above, below)
+    mixed = attend(place, peak_in, qkv, above, below)
     with jax.named_scope("heads"):
         mixed = lax.all_to_all(mixed, GROUP, 0, 0, tiled=True)
     attended = mixed[:, :SET].transpose(1, 0, 2).reshape(1, ROWS, COLS, HEADS * HEAD)
     peaks = mixed[:, SET:].astype(jnp.float32).reshape(8, 2, PEAK_ROWS // 2, HEAD)
-    peaks = jnp.max(peaks, axis=(0, 2, 3))[::-1]
+    peaks = jnp.max(peaks, axis=(0, 2, 3))
     for axis in ("y", "z"):
         with jax.named_scope("peaks"):
             peaks = jnp.max(spread(peaks, axis).reshape(-1, 2), axis=0)

time: 164 us -> 158 us (0.963)
  Pallas kernels: 14.7 us -> 11.7 us
  other arithmetic: 4.4 us -> 2.03 us
    convert_element_type x1 -> x0, other arithmetic: 3.12 us -> none  [local(): jnp.clip(flat / prev_scale[0], -FP_TOP, FP_TOP).astype(jnp.bfloat16)]
    pallas_call x1, Pallas kernels: 7.8 us -> 5.34 us  [project(): pl.pallas_call(project_kernel, out_shape=(jax.ShapeDtypeStruct((8, SET, 3...]
  transfers between devices with their start and end apart: 8 -> 8, of which waited for: 5 -> 4; matrix products, arithmetic and copies ran while one was open for 2% -> 3% of each run, Pallas kernels for 5% -> 0%
where the time goes in v2:
time: 158 us; the launch traced here: 156 us
  blocking collectives  62.5 us (40%)
  waiting for transfers between devices  31.1 us (20%)
  starting transfers between devices  26.2 us (17%)
  between operations  15.5 us (10%)
  Pallas kernels  11.7 us (7%)
  local copies, waits for them, and re-layouts  7.26 us (5%)
  other arithmetic  2.03 us (1%)
    all_to_all x2, blocking collectives, spread(): return lax.all_to_all(copies, axis, 0, 0, tiled=True)  43.4 us
    all_to_all x2, waiting for transfers between devices, spread(): return lax.all_to_all(copies, axis, 0, 0, tiled=True)  22.6 us
    all_to_all x1, blocking collectives, local(): mixed = lax.all_to_all(mixed, GROUP, 0, 0, tiled=True)  19.1 us
    all_to_all x2, starting transfers between devices, spread(): return lax.all_to_all(copies, axis, 0, 0, tiled=True)  13.1 us
    pallas_call x1, Pallas kernels, attend(): pl.pallas_call(attend_kernel, out_shape=jax.ShapeDtypeStruct((8, SET + PE...  6.34 us
    pallas_call x1, Pallas kernels, project(): pl.pallas_call(project_kernel, out_shape=(jax.ShapeDtypeStruct((8, SET, 3...  5.34 us
    ppermute x1, starting transfers between devices, head_weights(): first = lax.ppermute(mine, AXES, main)  4.59 us
    ppermute x1, starting transfers between devices, shift(): lax.ppermute(value, axis, [(i, (i + step) % size) for i in range(size)])  4.37 us
  transfers between devices with their start and end apart: 8, of which 4 were waited for; matrix products, arithmetic and copies ran while one was open for 3% of the time, Pallas kernels for 0%

profile of v2, /device:TPU:1, one launch (start us, length us, event | category | flops | bytes accessed | tf_op | source)
XLA Modules:
  0.0 156.3 jit_solution(14907340978027759509)
XLA Ops:
  7.2 0.7 all-gather.2.cloned.1.call-update
  7.9 0.7 collective-permute-start.2
  8.6 4.6 %collective-permute-start.1 = (bf16[6,2048]{1,0:T(8,128)(2,1)}, bf16[6,2048]{1,0:T(8,128)(2,1)S(1)}, u32[]{:S(2)}, u32[]{:S(2)}) collective-permute-start(bf16[6,2048]{1,0:T(8,128)(2,1)} %bitcast.11), channel_id=1, source_target_pairs={{0,0},{1,128},{2,2},{3,130},{4,4},{5,132},{6,6},{7,134},{8,8},{9,1... | collective-permute-start | bytes 73736 | tf_op jit(solution)/shard_map/ppermute | solution.py:179
  13.2 4.2 %collective-permute-done.1 = bf16[6,2048]{1,0:T(8,128)(2,1)S(1)} collective-permute-done((bf16[6,2048]{1,0:T(8,128)(2,1)}, bf16[6,2048]{1,0:T(8,128)(2,1)S(1)}, u32[]{:S(2)}, u32[]{:S(2)}) %collective-permute-start.1) | collective-permute-done | bytes 24608 | tf_op jit(solution)/shard_map/ppermute | solution.py:179
  17.6 36.4 %all_to_all.27 = bf16[16,96,128]{2,1,0:T(8,128)(2,1)S(1)} all-to-all(bf16[16,96,128]{2,1,0:T(8,128)(2,1)S(1)} %broadcast_in_dim.11), channel_id=1, replica_groups=mesh['y'=4,'x'=4,'z'=16,'core'=2] {'z'}, dimensions={0} | all-to-all | bytes 786432 | tf_op jit(solution)/shard_map/weights_over_z/all_to_all | solution.py:168
  54.2 1.4 broadcast_in_dim.12
  55.7 7.0 %all-to-all-start.1 = ((bf16[4,96,2048]{2,1,0:T(8,128)(2,1)}), bf16[4,96,2048]{2,1,0:T(8,128)(2,1)S(1)}, u32[]{:S(2)}, u32[]{:S(2)}) async-start(bf16[4,96,2048]{2,1,0:T(8,128)(2,1)} %broadcast_in_dim.12), calls=%async_computation.1 | async-start | bytes 3145728 | tf_op jit(solution)/shard_map/weights_over_y/all_to_all | solution.py:168
  62.7 4.4 %collective-permute-start = (s32[1,2]{1,0:T(1,128)S(1)}, s32[1,2]{1,0:T(1,128)S(1)}, u32[]{:S(2)}, u32[]{:S(2)}) collective-permute-start(s32[1,2]{1,0:T(1,128)S(1)} %copy-done.2), channel_id=1, source_target_pairs={{0,1},{1,0},{2,3},{3,2},{4,5},{5,4},{6,7},{7,6},{8,9},{9,8},{10,11... | collective-permute-start | bytes 32 | tf_op jit(solution)/shard_map/ppermute | solution.py:173
  68.1 12.8 %all-to-all-done.1 = bf16[4,96,2048]{2,1,0:T(8,128)(2,1)S(1)} async-done(((bf16[4,96,2048]{2,1,0:T(8,128)(2,1)}), bf16[4,96,2048]{2,1,0:T(8,128)(2,1)S(1)}, u32[]{:S(2)}, u32[]{:S(2)}) %all-to-all-start.1) | async-done | bytes 1572896 | tf_op jit(solution)/shard_map/weights_over_y/all_to_all | solution.py:168
  80.9 3.4 %copy-done = bf16[8,256,2048]{2,1,0:T(8,128)(2,1)S(1)} copy-done((bf16[8,256,2048]{2,1,0:T(8,128)(2,1)S(1)}, bf16[8,256,2048]{2,1,0:T(8,128)(2,1)}, u32[]{:S(2)}) %copy-start) | copy-done | bytes 8388632
  84.3 5.3 %project.1 = (bf16[8,256,384]{2,1,0:T(8,128)(2,1)S(1)}, bf16[2,192,256]{2,1,0:T(8,128)(2,1)S(1)}, bf16[2,192,256]{2,1,0:T(8,128)(2,1)S(1)}) custom-call(f32[1]{0:T(128)S(6)} %copy.14.scale_ref, bf16[8,256,2048]{2,1,0:T(8,128)(2,1)S(1)} %copy-done, bf16[384,2048]{1,0:T(8,128)(2,1)S(1)} %bitcast.8, bf16[384,384]{1,0:T(8,128)(2,1)S(1)} %fusion.15.order_ref), custom_call_target="tpu_custom_call" | custom-call | flops 3221225472 | bytes 12582912 | tf_op jit(solution)/shard_map/project/pallas_call | solution.py:84
  89.7 2.2 %collective-permute-start.3 = (bf16[2,192,256]{2,1,0:T(8,128)(2,1)S(1)}, bf16[2,192,256]{2,1,0:T(8,128)(2,1)S(1)}, u32[]{:S(2)}, u32[]{:S(2)}) collective-permute-start(bf16[2,192,256]{2,1,0:T(8,128)(2,1)S(1)} %get-tuple-element.10), channel_id=1, source_target_pairs={{0,128},{128,256},{256,384},{1,129},{129,257},{257,385},{2,130},{1... | collective-permute-start | bytes 589832 | tf_op jit(solution)/shard_map/halo/ppermute | solution.py:205
  91.9 1.3 collective-permute-start.4
  93.3 0.7 abs_reduce_fusion
  94.7 3.6 %collective-permute-done.4.below_ref = bf16[2,192,256]{2,1,0:T(8,128)(2,1)S(1)} collective-permute-done((bf16[2,192,256]{2,1,0:T(8,128)(2,1)S(1)}, bf16[2,192,256]{2,1,0:T(8,128)(2,1)S(1)}, u32[]{:S(2)}, u32[]{:S(2)}) %collective-permute-start.4) | collective-permute-done | bytes 196640 | tf_op jit(solution)/shard_map/halo/ppermute | solution.py:206
  98.3 6.3 %attend.1 = bf16[8,272,128]{2,1,0:T(8,128)(2,1)S(1)} custom-call(s32[5]{0:T(128)S(1)} %pad_add_fusion.place_ref, f32[1]{0:T(128)S(6)} %convert.6.peak_ref, bf16[8,256,384]{2,1,0:T(8,128)(2,1)S(1)} %get-tuple-element.9.qkv_ref, bf16[2,192,256]{2,1,0:T(8,128)(2,1)S(1)} %collective-permute-done.3.above_ref, ...), custom_call_target="tpu_custom_call" | custom-call | flops 536870912 | bytes 3145728 | tf_op jit(solution)/shard_map/attend/pallas_call | solution.py:151
  104.6 19.1 %all_to_all.28 = bf16[8,272,128]{2,1,0:T(8,128)(2,1)S(1)} all-to-all(bf16[8,272,128]{2,1,0:T(8,128)(2,1)S(1)} %attend.1), channel_id=1, replica_groups=mesh['y'=4,'x'=4,'z'=16,'core'=2] {'x','core'}, dimensions={0} | all-to-all | bytes 1114112 | tf_op jit(solution)/shard_map/heads/all_to_all | solution.py:209
  124.1 7.0 %all_to_all.29 = f32[4,1,2]{2,1,0:T(1,128)S(1)} all-to-all(f32[4,1,2]{2,1,0:T(1,128)S(1)} %broadcast_in_dim.13), channel_id=1, replica_groups=mesh['y'=4,'x'=4,'z'=16,'core'=2] {'y'}, dimensions={0} | all-to-all | bytes 64 | tf_op jit(solution)/shard_map/peaks/all_to_all | solution.py:168
  131.0 0.6 broadcast_in_dim.14
  131.7 6.0 %all-to-all-start.4 = ((f32[16,1,2]{2,1,0:T(1,128)}), f32[16,1,2]{2,1,0:T(1,128)S(1)}, u32[]{:S(2)}, u32[]{:S(2)}) async-start(f32[16,1,2]{2,1,0:T(1,128)} %broadcast_in_dim.14), calls=%async_computation.4 | async-start | bytes 16384 | tf_op jit(solution)/shard_map/peaks/all_to_all | solution.py:168
  137.8 0.3 copy.9
  138.1 1.0 reshape.49
  139.1 9.8 %all-to-all-done.4 = f32[16,1,2]{2,1,0:T(1,128)S(1)} async-done(((f32[16,1,2]{2,1,0:T(1,128)}), f32[16,1,2]{2,1,0:T(1,128)S(1)}, u32[]{:S(2)}, u32[]{:S(2)}) %all-to-all-start.4) | async-done | bytes 160 | tf_op jit(solution)/shard_map/peaks/all_to_all | solution.py:168
  149.0 0.5 broadcast_multiply_fusion
  (29 shorter events, 1.3 us)
Async XLA Ops:
  7.2 73.8 %all-gather.2.cloned.1.call-start = ((), (), s32[]{:S(2)}) async-start(), calls=%async_computation.5 | async-start | bytes 9437184 | tf_op jit(solution)/shard_map/tokens/all_gather | solution.py:195
  7.9 5.3 %collective-permute-start.2 = (bf16[6,2048]{1,0:T(8,128)(2,1)}, bf16[6,2048]{1,0:T(8,128)(2,1)S(1)}, u32[]{:S(2)}, u32[]{:S(2)}) collective-permute-start(bf16[6,2048]{1,0:T(8,128)(2,1)} %bitcast.10), channel_id=1, source_target_pairs={{21,149},{42,298},{85,212},{106,331},{149,245},{170,266},{213,180}... | collective-permute-start | bytes 73736 | tf_op jit(solution)/shard_map/ppermute | solution.py:180
  8.6 8.9 %collective-permute-start.1 = (bf16[6,2048]{1,0:T(8,128)(2,1)}, bf16[6,2048]{1,0:T(8,128)(2,1)S(1)}, u32[]{:S(2)}, u32[]{:S(2)}) collective-permute-start(bf16[6,2048]{1,0:T(8,128)(2,1)} %bitcast.11), channel_id=1, source_target_pairs={{0,0},{1,128},{2,2},{3,130},{4,4},{5,132},{6,6},{7,134},{8,8},{9,1... | collective-permute-start | bytes 73736 | tf_op jit(solution)/shard_map/ppermute | solution.py:179
  55.7 7.0 %copy-start.2 = (s32[1,2]{1,0:T(1,128)S(1)}, s32[1,2]{1,0:T(1,128)}, u32[]{:S(2)}) copy-start(s32[1,2]{1,0:T(1,128)} %param.7) | copy-start | bytes 28
  55.7 25.3 %all-to-all-start.1 = ((bf16[4,96,2048]{2,1,0:T(8,128)(2,1)}), bf16[4,96,2048]{2,1,0:T(8,128)(2,1)S(1)}, u32[]{:S(2)}, u32[]{:S(2)}) async-start(bf16[4,96,2048]{2,1,0:T(8,128)(2,1)} %broadcast_in_dim.12), calls=%async_computation.1 | async-start | bytes 3145728 | tf_op jit(solution)/shard_map/weights_over_y/all_to_all | solution.py:168
  62.7 5.4 %collective-permute-start = (s32[1,2]{1,0:T(1,128)S(1)}, s32[1,2]{1,0:T(1,128)S(1)}, u32[]{:S(2)}, u32[]{:S(2)}) collective-permute-start(s32[1,2]{1,0:T(1,128)S(1)} %copy-done.2), channel_id=1, source_target_pairs={{0,1},{1,0},{2,3},{3,2},{4,5},{5,4},{6,7},{7,6},{8,9},{9,8},{10,11... | collective-permute-start | bytes 32 | tf_op jit(solution)/shard_map/ppermute | solution.py:173
  80.9 3.4 %copy-start = (bf16[8,256,2048]{2,1,0:T(8,128)(2,1)S(1)}, bf16[8,256,2048]{2,1,0:T(8,128)(2,1)}, u32[]{:S(2)}) copy-start(bf16[8,256,2048]{2,1,0:T(8,128)(2,1)} %all-gather.2.cloned.1.call-done.x_ref) | copy-start | bytes 25165828
  84.3 8.9 %copy-start.1 = (bf16[1,4,64,2048]{3,2,1,0:T(8,128)(2,1)S(1)}, bf16[1,4,64,2048]{3,2,1,0:T(8,128)(2,1)}, u32[]{:S(2)}) copy-start(bf16[1,4,64,2048]{3,2,1,0:T(8,128)(2,1)} %param.4) | copy-start | bytes 3145732
  89.7 5.0 %collective-permute-start.3 = (bf16[2,192,256]{2,1,0:T(8,128)(2,1)S(1)}, bf16[2,192,256]{2,1,0:T(8,128)(2,1)S(1)}, u32[]{:S(2)}, u32[]{:S(2)}) collective-permute-start(bf16[2,192,256]{2,1,0:T(8,128)(2,1)S(1)} %get-tuple-element.10), channel_id=1, source_target_pairs={{0,128},{128,256},{256,384},{1,129},{129,257},{257,385},{2,130},{1... | collective-permute-start | bytes 589832 | tf_op jit(solution)/shard_map/halo/ppermute | solution.py:205
  91.9 6.4 %collective-permute-start.4 = (bf16[2,192,256]{2,1,0:T(8,128)(2,1)S(1)}, bf16[2,192,256]{2,1,0:T(8,128)(2,1)S(1)}, u32[]{:S(2)}, u32[]{:S(2)}) collective-permute-start(bf16[2,192,256]{2,1,0:T(8,128)(2,1)S(1)} %get-tuple-element.11), channel_id=1, source_target_pairs={{128,0},{256,128},{384,256},{129,1},{257,129},{385,257},{130,2},{2... | collective-permute-start | bytes 589832 | tf_op jit(solution)/shard_map/halo/ppermute | solution.py:206
  131.7 17.3 %all-to-all-start.4 = ((f32[16,1,2]{2,1,0:T(1,128)}), f32[16,1,2]{2,1,0:T(1,128)S(1)}, u32[]{:S(2)}, u32[]{:S(2)}) async-start(f32[16,1,2]{2,1,0:T(1,128)} %broadcast_in_dim.14), calls=%async_computation.4 | async-start | bytes 16384 | tf_op jit(solution)/shard_map/peaks/all_to_all | solution.py:168
Sparse Core Ops, SparseCore 0:
  10.1 63.0 all-gather.1

commit v3 on v2

--- a/solution.py
+++ b/solution.py
@@ -21,6 +21,7 @@
 AXES = ("y", "x", "z", "core")
 GROUP = ("x", "core")
 PEAK_ROWS = 16
+INNER = (2, 3, 4, 5)
 NEG = -1e30
 
 
@@ -48,20 +49,24 @@
     return main, extra
 
 
-def column_order(head):
+def column_order(head, y):
     d = lax.broadcasted_iota(jnp.int32, (3 * HEAD, 3 * HEAD), 1)
     r = lax.broadcasted_iota(jnp.int32, (3 * HEAD, 3 * HEAD), 0)
     natural = ((head + 2 * (d // HEAD)) % 3) * HEAD + d % HEAD
     half, m = natural // 192, natural % 192
     z, core, j = m // 12, (m % 12) // 6, m % 6
-    return ((2 * half + core) * 96 + z * 6 + j == r).astype(jnp.bfloat16)
-
-
-def project_kernel(scale_ref, x_ref, w_ref, order_ref, qkv_ref, top_ref, bottom_ref, w_scr):
+    away = (2 * half + core + 4 - y) % 4
+    place = jnp.where(away == 3, 1, jnp.where(away == 0, 0, away + 1))
+    return (place * 96 + z * 6 + j == r).astype(jnp.bfloat16)
+
+
+def project_kernel(scale_ref, x_ref, w0_ref, w1_ref, w2_ref, w3_ref, order_ref, qkv_ref, top_ref, bottom_ref, w_cat, w_scr):
     scale = scale_ref[0]
     inverse = 1.0 / scale
+    for part, ref in enumerate((w0_ref, w1_ref, w2_ref, w3_ref)):
+        w_cat[96 * part : 96 * (part + 1)] = ref[...]
     w_scr[...] = lax.dot_general(
-        order_ref[...], w_ref[...], (((0,), (0,)), ((), ())), preferred_element_type=jnp.float32
+        order_ref[...], w_cat[...], (((0,), (0,)), ((), ())), preferred_element_type=jnp.float32
     ).astype(jnp.bfloat16)
     for part in range(4):
         tokens = x_ref[2 * part : 2 * part + 2].reshape(2 * SET, D)
@@ -84,18 +89,18 @@
     return pl.pallas_call(
         project_kernel,
         out_shape=(jax.ShapeDtypeStruct((8, SET, 3 * HEAD), jnp.bfloat16), halo, halo),
-        in_specs=[pl.BlockSpec(memory_space=pltpu.SMEM), vmem, vmem, vmem],
+        in_specs=[pl.BlockSpec(memory_space=pltpu.SMEM)] + [vmem] * 6,
         out_specs=(vmem, vmem, vmem),
-        scratch_shapes=[pltpu.VMEM((3 * HEAD, D), jnp.bfloat16)],
+        scratch_shapes=[pltpu.VMEM((3 * HEAD, D), jnp.bfloat16)] * 2,
         compiler_params=pltpu.CompilerParams(vmem_limit_bytes=24 * 2**20),
         cost_estimate=pl.CostEstimate(
             flops=2 * 8 * SET * D * 3 * HEAD, bytes_accessed=12 * 2**20, transcendentals=0
         ),
         name="project",
-    )(scale, tokens, weights, order)
-
-
-def attend_kernel(place_ref, peak_ref, qkv_ref, above_ref, below_ref, out_ref, kv):
+    )(scale, tokens, *weights, order)
+
+
+def attend_rows(pairs, place_ref, qkv_ref, out_ref, kv):
     base = place_ref[0]
     scaling = float(HEAD) ** -0.5
     shape = (2 * COLS, 8 * COLS)
@@ -111,12 +116,7 @@
     highest = jnp.zeros((2 * COLS, HEAD), jnp.float32)
     for image in range(2):
         ext_rows, ext_cols = place_ref[1 + 2 * image], place_ref[2 + 2 * image]
-        kv[image, : HALO * COLS] = above_ref[image]
-        for part in range(4):
-            start = HALO * COLS + part * SET
-            kv[image, start : start + SET] = qkv_ref[2 * part + image, :, HEAD:]
-        kv[image, KV_ROWS - HALO * COLS :] = below_ref[image]
-        for pair in range(BLOCK // 2):
+        for pair in pairs:
             part, inner = pair // 2, (pair % 2) * 2 * COLS
             query = qkv_ref[2 * part + image, inner : inner + 2 * COLS, :HEAD]
             start = 2 * pair * COLS
@@ -139,27 +139,72 @@
             result = jnp.where(inside, result, 0.0).astype(jnp.bfloat16)
             highest = jnp.maximum(highest, jnp.abs(result.astype(jnp.float32)))
             out_ref[2 * part + image, inner : inner + 2 * COLS, :] = result
+    return highest
+
+
+def fill_keys(qkv_ref, kv):
+    for image in range(2):
+        for part in range(4):
+            start = HALO * COLS + part * SET
+            kv[image, start : start + SET] = qkv_ref[2 * part + image, :, HEAD:]
+
+
+def attend_inner_kernel(place_ref, qkv_ref, out_ref, highest_ref, kv):
+    fill_keys(qkv_ref, kv)
+    highest_ref[...] = attend_rows(INNER, place_ref, qkv_ref, out_ref, kv)
+
+
+def attend_outer_kernel(place_ref, peak_ref, qkv_ref, above_ref, below_ref, inner_ref, highest_ref, out_ref, kv):
+    for image in range(2):
+        kv[image, : HALO * COLS] = above_ref[image]
+        kv[image, KV_ROWS - HALO * COLS :] = below_ref[image]
+    fill_keys(qkv_ref, kv)
+    for image in range(2):
+        for pair in INNER:
+            place = 2 * (pair // 2) + image, slice((pair % 2) * 2 * COLS, (pair % 2 + 1) * 2 * COLS)
+            out_ref[place] = inner_ref[place]
+    outer = [pair for pair in range(BLOCK // 2) if pair not in INNER]
+    highest = jnp.maximum(attend_rows(outer, place_ref, qkv_ref, out_ref, kv), highest_ref[...])
     lines = lax.broadcasted_iota(jnp.int32, (PEAK_ROWS, HEAD), 0)
     peaks = jnp.where(lines < PEAK_ROWS // 2, peak_ref[0], jnp.max(highest)).astype(jnp.bfloat16)
     for group in range(8):
         out_ref[group, SET:, :] = peaks
 
 
-def attend(place, peak_in, qkv, above, below):
+def attend_inner(place, qkv):
+    vmem = pl.BlockSpec(memory_space=pltpu.VMEM)
+    return pl.pallas_call(
+        attend_inner_kernel,
+        out_shape=(
+            jax.ShapeDtypeStruct((8, SET, HEAD), jnp.bfloat16),
+            jax.ShapeDtypeStruct((2 * COLS, HEAD), jnp.float32),
+        ),
+        in_specs=[pl.BlockSpec(memory_space=pltpu.SMEM), vmem],
+        out_specs=(vmem, vmem),
+        scratch_shapes=[pltpu.VMEM((2, KV_ROWS, 2 * HEAD), jnp.bfloat16)],
+        compiler_params=pltpu.CompilerParams(vmem_limit_bytes=24 * 2**20),
+        cost_estimate=pl.CostEstimate(
+            flops=4 * 8 * 128 * 512 * HEAD, bytes_accessed=2 * 2**20, transcendentals=8 * 128 * 512
+        ),
+        name="attend_inner",
+    )(place, qkv)
+
+
+def attend_outer(place, peak_in, qkv, above, below, inner, highest):
     vmem = pl.BlockSpec(memory_space=pltpu.VMEM)
     smem = pl.BlockSpec(memory_space=pltpu.SMEM)
     return pl.pallas_call(
-        attend_kernel,
+        attend_outer_kernel,
         out_shape=jax.ShapeDtypeStruct((8, SET + PEAK_ROWS, HEAD), jnp.bfloat16),
-        in_specs=[smem, smem, vmem, vmem, vmem],
+        in_specs=[smem, smem] + [vmem] * 5,
         out_specs=vmem,
         scratch_shapes=[pltpu.VMEM((2, KV_ROWS, 2 * HEAD), jnp.bfloat16)],
         compiler_params=pltpu.CompilerParams(vmem_limit_bytes=24 * 2**20),
         cost_estimate=pl.CostEstimate(
-            flops=4 * 16 * 128 * 512 * HEAD, bytes_accessed=3 * 2**20, transcendentals=16 * 128 * 512
-        ),
-        name="attend",
-    )(place, peak_in, qkv, above, below)
+            flops=4 * 8 * 128 * 512 * HEAD, bytes_accessed=3 * 2**20, transcendentals=8 * 128 * 512
+        ),
+        name="attend_outer",
+    )(place, peak_in, qkv, above, below, inner, highest)
 
 
 def spread(value, axis):
@@ -187,7 +232,7 @@
         over_z = spread(merged.reshape(96, 128), "z").reshape(96, D)
     over_z, late = lax.optimization_barrier((over_z, images))
     with jax.named_scope("weights_over_y"):
-        return spread(over_z, "y").reshape(3 * HEAD, D), late
+        return [over_z] + [shift(over_z, "y", step) for step in (1, -1, 2)], late
 
 
 def local(images, w_qkv, prev_scale, extent):
@@ -196,7 +241,7 @@
     weights, late = head_weights(w_qkv, images)
     peak_in = jnp.max(jnp.abs(late)).astype(jnp.float32).reshape(1)
     core = lax.axis_index("core")
-    order = column_order(2 * lax.axis_index("x") + core)
+    order = column_order(2 * lax.axis_index("x") + core, lax.axis_index("y"))
     other = shift(extent, "core", 1)
     extents = jnp.where(core == 0, jnp.concatenate([extent, other]), jnp.concatenate([other, extent]))
     place = jnp.stack([lax.axis_index("y") * BLOCK, *extents.reshape(4)]).astype(jnp.int32)
@@ -204,7 +249,8 @@
     with jax.named_scope("halo"):
         above = lax.ppermute(bottom, "y", [(i, i + 1) for i in range(3)])
         below = lax.ppermute(top, "y", [(i + 1, i) for i in range(3)])
-    mixed = attend(place, peak_in, qkv, above, below)
+    inner, highest = attend_inner(place, qkv)
+    mixed = attend_outer(place, peak_in, qkv, above, below, inner, highest)
     with jax.named_scope("heads"):
         mixed = lax.all_to_all(mixed, GROUP, 0, 0, tiled=True)
     attended = mixed[:, :SET].transpose(1, 0, 2).reshape(1, ROWS, COLS, HEADS * HEAD)

time: 158 us -> 154 us (0.975)
  blocking collectives: 62.5 us -> 22.2 us
  starting transfers between devices: 26.2 us -> 48.7 us
  waiting for transfers between devices: 31.1 us -> 44.2 us
    all_to_all x2 -> x1, blocking collectives: 43.4 us -> 7.27 us  [spread(): return lax.all_to_all(copies, axis, 0, 0, tiled=True)]
    all_to_all x2, starting transfers between devices: 13.1 us -> 23.7 us  [spread(): return lax.all_to_all(copies, axis, 0, 0, tiled=True)]
    ppermute x1 -> x4, starting transfers between devices: 4.37 us -> 14.8 us  [shift(): lax.ppermute(value, axis, [(i, (i + step) % size) for i in range(size)])]
    ppermute x1 -> x4, waiting for transfers between devices: 0.01 us -> 9.84 us  [shift(): lax.ppermute(value, axis, [(i, (i + step) % size) for i in range(size)])]
    all_to_all x2, waiting for transfers between devices: 22.6 us -> 28.1 us  [spread(): return lax.all_to_all(copies, axis, 0, 0, tiled=True)]
    all_to_all x1, blocking collectives: 19.1 us -> 14.9 us  [local(): mixed = lax.all_to_all(mixed, GROUP, 0, 0, tiled=True)]
    ppermute x1, waiting for transfers between devices: 3.62 us -> 1.35 us  [local(): below = lax.ppermute(top, 'y', [(i + 1, i) for i in range(3)])]
    pallas_call x1 -> x2, Pallas kernels: 6.34 us -> 7.12 us  [the longest x1 3.64 us: attend_outer(): pl.pallas_call(attend_outer_kernel, out_shape=jax.ShapeDtypeStruct((8, SE...]
  transfers between devices with their start and end apart: 8 -> 11, of which waited for: 4 -> 7; matrix products, arithmetic and copies ran while one was open for 3% -> 3% of each run, Pallas kernels for 0% -> 2%
where the time goes in v3:
time: 154 us; the launch traced here: 152 us
  starting transfers between devices  48.7 us (32%)
  waiting for transfers between devices  44.2 us (29%)
  blocking collectives  22.2 us (14%)
  between operations  15.6 us (10%)
  Pallas kernels  12.5 us (8%)
  local copies, waits for them, and re-layouts  6.58 us (4%)
  other arithmetic  2.79 us (2%)
    all_to_all x2, waiting for transfers between devices, spread(): return lax.all_to_all(copies, axis, 0, 0, tiled=True)  28.1 us
    all_to_all x2, starting transfers between devices, spread(): return lax.all_to_all(copies, axis, 0, 0, tiled=True)  23.7 us
    all_to_all x1, blocking collectives, local(): mixed = lax.all_to_all(mixed, GROUP, 0, 0, tiled=True)  14.9 us
    ppermute x4, starting transfers between devices, shift(): lax.ppermute(value, axis, [(i, (i + step) % size) for i in range(size)])  14.8 us
    ppermute x4, waiting for transfers between devices, shift(): lax.ppermute(value, axis, [(i, (i + step) % size) for i in range(size)])  9.84 us
    all_to_all x1, blocking collectives, spread(): return lax.all_to_all(copies, axis, 0, 0, tiled=True)  7.27 us
    pallas_call x1, Pallas kernels, project(): pl.pallas_call(project_kernel, out_shape=(jax.ShapeDtypeStruct((8, SET, 3...  5.34 us
    ppermute x1, starting transfers between devices, head_weights(): first = lax.ppermute(mine, AXES, main)  4.59 us
  transfers between devices with their start and end apart: 11, of which 7 were waited for; matrix products, arithmetic and copies ran while one was open for 3% of the time, Pallas kernels for 2%

profile of v3, /device:TPU:1, one launch (start us, length us, event | category | flops | bytes accessed | tf_op | source)
XLA Modules:
  0.0 152.4 jit_solution(9128521682826118484)
XLA Ops:
  8.6 4.6 %collective-permute-start.1 = (bf16[6,2048]{1,0:T(8,128)(2,1)}, bf16[6,2048]{1,0:T(8,128)(2,1)S(1)}, u32[]{:S(2)}, u32[]{:S(2)}) collective-permute-start(bf16[6,2048]{1,0:T(8,128)(2,1)} %bitcast.9), channel_id=1, source_target_pairs={{0,0},{1,128},{2,2},{3,130},{4,4},{5,132},{6,6},{7,134},{8,8},{9,1... | collective-permute-start | bytes 73736 | tf_op jit(solution)/shard_map/ppermute | solution.py:224
  13.2 4.2 %collective-permute-done.1 = bf16[6,2048]{1,0:T(8,128)(2,1)S(1)} collective-permute-done((bf16[6,2048]{1,0:T(8,128)(2,1)}, bf16[6,2048]{1,0:T(8,128)(2,1)S(1)}, u32[]{:S(2)}, u32[]{:S(2)}) %collective-permute-start.1) | collective-permute-done | bytes 24608 | tf_op jit(solution)/shard_map/ppermute | solution.py:224
  17.6 0.8 broadcast_in_dim.12
  18.4 16.4 %all-to-all-start = ((bf16[16,96,128]{2,1,0:T(8,128)(2,1)}), bf16[16,96,128]{2,1,0:T(8,128)(2,1)S(1)}, u32[]{:S(2)}, u32[]{:S(2)}) async-start(bf16[16,96,128]{2,1,0:T(8,128)(2,1)} %broadcast_in_dim.12), calls=%async_computation | async-start | bytes 786432 | tf_op jit(solution)/shard_map/weights_over_z/all_to_all | solution.py:213
  34.8 2.0 %collective-permute-start = (s32[1,2]{1,0:T(1,128)}, s32[1,2]{1,0:T(1,128)S(1)}, u32[]{:S(2)}, u32[]{:S(2)}) collective-permute-start(s32[1,2]{1,0:T(1,128)} %param.7), channel_id=1, source_target_pairs={{0,1},{1,0},{2,3},{3,2},{4,5},{5,4},{6,7},{7,6},{8,9},{9,8},{10,11... | collective-permute-start | bytes 32 | tf_op jit(solution)/shard_map/ppermute | solution.py:218
  36.8 18.2 %all-to-all-done = bf16[16,96,128]{2,1,0:T(8,128)(2,1)S(1)} async-done(((bf16[16,96,128]{2,1,0:T(8,128)(2,1)}), bf16[16,96,128]{2,1,0:T(8,128)(2,1)S(1)}, u32[]{:S(2)}, u32[]{:S(2)}) %all-to-all-start) | async-done | bytes 393248 | tf_op jit(solution)/shard_map/weights_over_z/all_to_all | solution.py:213
  55.2 7.5 %collective-permute-start.5 = (bf16[96,2048]{1,0:T(8,128)(2,1)S(1)}, bf16[96,2048]{1,0:T(8,128)(2,1)S(1)}, u32[]{:S(2)}, u32[]{:S(2)}) collective-permute-start(bf16[96,2048]{1,0:T(8,128)(2,1)S(1)} %reshape.40.w0_ref), channel_id=1, source_target_pairs={{0,256},{128,384},{256,0},{384,128},{1,257},{129,385},{257,1},{385... | collective-permute-start | bytes 1179656 | tf_op jit(solution)/shard_map/weights_over_y/ppermute | solution.py:218
  62.7 2.1 %collective-permute-start.4 = (bf16[96,2048]{1,0:T(8,128)(2,1)S(1)}, bf16[96,2048]{1,0:T(8,128)(2,1)S(1)}, u32[]{:S(2)}, u32[]{:S(2)}) collective-permute-start(bf16[96,2048]{1,0:T(8,128)(2,1)S(1)} %reshape.40.w0_ref), channel_id=1, source_target_pairs={{0,384},{128,0},{256,128},{384,256},{1,385},{129,1},{257,129},{385... | collective-permute-start | bytes 1179656 | tf_op jit(solution)/shard_map/weights_over_y/ppermute | solution.py:218
  64.8 3.2 %collective-permute-start.3 = (bf16[96,2048]{1,0:T(8,128)(2,1)S(1)}, bf16[96,2048]{1,0:T(8,128)(2,1)S(1)}, u32[]{:S(2)}, u32[]{:S(2)}) collective-permute-start(bf16[96,2048]{1,0:T(8,128)(2,1)S(1)} %reshape.40.w0_ref), channel_id=1, source_target_pairs={{0,128},{128,256},{256,384},{384,0},{1,129},{129,257},{257,385},{3... | collective-permute-start | bytes 1179656 | tf_op jit(solution)/shard_map/weights_over_y/ppermute | solution.py:218
  69.9 1.2 collective-permute-done.5.w3_ref
  71.1 5.2 %collective-permute-done.4.w2_ref = bf16[96,2048]{1,0:T(8,128)(2,1)S(1)} collective-permute-done((bf16[96,2048]{1,0:T(8,128)(2,1)S(1)}, bf16[96,2048]{1,0:T(8,128)(2,1)S(1)}, u32[]{:S(2)}, u32[]{:S(2)}) %collective-permute-start.4) | collective-permute-done | bytes 393248 | tf_op jit(solution)/shard_map/weights_over_y/ppermute | solution.py:218
  76.3 3.4 %collective-permute-done.3.w1_ref = bf16[96,2048]{1,0:T(8,128)(2,1)S(1)} collective-permute-done((bf16[96,2048]{1,0:T(8,128)(2,1)S(1)}, bf16[96,2048]{1,0:T(8,128)(2,1)S(1)}, u32[]{:S(2)}, u32[]{:S(2)}) %collective-permute-start.3) | collective-permute-done | bytes 393248 | tf_op jit(solution)/shard_map/weights_over_y/ppermute | solution.py:218
  79.7 3.4 %copy-done = bf16[8,256,2048]{2,1,0:T(8,128)(2,1)S(1)} copy-done((bf16[8,256,2048]{2,1,0:T(8,128)(2,1)S(1)}, bf16[8,256,2048]{2,1,0:T(8,128)(2,1)}, u32[]{:S(2)}) %copy-start) | copy-done | bytes 8388632
  83.1 5.3 %project.1 = (bf16[8,256,384]{2,1,0:T(8,128)(2,1)S(1)}, bf16[2,192,256]{2,1,0:T(8,128)(2,1)S(1)}, bf16[2,192,256]{2,1,0:T(8,128)(2,1)S(1)}) custom-call(f32[1]{0:T(128)S(6)} %copy.14.scale_ref, bf16[8,256,2048]{2,1,0:T(8,128)(2,1)S(1)} %copy-done, bf16[96,2048]{1,0:T(8,128)(2,1)S(1)} %reshape.40.w0_ref, bf16[96,2048]{1,0:T(8,128)(2,1)S(1)} %collective-permute-done.3.w1_ref, ...), custom_call_target="tpu_custom_call" | custom-call | flops 3221225472 | bytes 12582912 | tf_op jit(solution)/shard_map/project/pallas_call | solution.py:89
  88.5 3.7 %collective-permute-start.6 = (bf16[2,192,256]{2,1,0:T(8,128)(2,1)S(1)}, bf16[2,192,256]{2,1,0:T(8,128)(2,1)S(1)}, u32[]{:S(2)}, u32[]{:S(2)}) collective-permute-start(bf16[2,192,256]{2,1,0:T(8,128)(2,1)S(1)} %get-tuple-element.12), channel_id=1, source_target_pairs={{0,128},{128,256},{256,384},{1,129},{129,257},{257,385},{2,130},{1... | collective-permute-start | bytes 589832 | tf_op jit(solution)/shard_map/halo/ppermute | solution.py:250
  92.1 1.3 collective-permute-start.7
  94.9 3.5 %attend_inner.1 = (bf16[8,256,128]{2,1,0:T(8,128)(2,1)S(1)}, f32[128,128]{1,0:T(8,128)S(1)}) custom-call(s32[5]{0:T(128)S(1)} %pad_add_fusion.place_ref, bf16[8,256,384]{2,1,0:T(8,128)(2,1)S(1)} %get-tuple-element.11.qkv_ref), custom_call_target="tpu_custom_call" | custom-call | flops 268435456 | bytes 2097152 | tf_op jit(solution)/shard_map/attend_inner/pallas_call | solution.py:176
  98.4 1.4 collective-permute-done.7.below_ref
  99.7 3.6 %attend_outer.1 = bf16[8,272,128]{2,1,0:T(8,128)(2,1)S(1)} custom-call(s32[5]{0:T(128)S(1)} %pad_add_fusion.place_ref, f32[1]{0:T(128)S(6)} %convert.6.peak_ref, bf16[8,256,384]{2,1,0:T(8,128)(2,1)S(1)} %get-tuple-element.11.qkv_ref, bf16[2,192,256]{2,1,0:T(8,128)(2,1)S(1)} %collective-permute-done.6.above_ref, ...), custom_call_target="tpu_custom_call" | custom-call | flops 268435456 | bytes 3145728 | tf_op jit(solution)/shard_map/attend_outer/pallas_call | solution.py:196
  103.4 14.9 %all_to_all.22 = bf16[8,272,128]{2,1,0:T(8,128)(2,1)S(1)} all-to-all(bf16[8,272,128]{2,1,0:T(8,128)(2,1)S(1)} %attend_outer.1), channel_id=1, replica_groups=mesh['y'=4,'x'=4,'z'=16,'core'=2] {'x','core'}, dimensions={0} | all-to-all | bytes 1114112 | tf_op jit(solution)/shard_map/heads/all_to_all | solution.py:255
  118.6 7.3 %all_to_all.23 = f32[4,1,2]{2,1,0:T(1,128)S(1)} all-to-all(f32[4,1,2]{2,1,0:T(1,128)S(1)} %broadcast_in_dim.24), channel_id=1, replica_groups=mesh['y'=4,'x'=4,'z'=16,'core'=2] {'y'}, dimensions={0} | all-to-all | bytes 64 | tf_op jit(solution)/shard_map/peaks/all_to_all | solution.py:213
  126.5 7.3 %all-to-all-start.3 = ((f32[16,1,2]{2,1,0:T(1,128)}), f32[16,1,2]{2,1,0:T(1,128)S(1)}, u32[]{:S(2)}, u32[]{:S(2)}) async-start(f32[16,1,2]{2,1,0:T(1,128)} %broadcast_in_dim.25), calls=%async_computation.3 | async-start | bytes 16384 | tf_op jit(solution)/shard_map/peaks/all_to_all | solution.py:213
  134.2 1.0 reshape.44
  135.2 9.8 %all-to-all-done.3 = f32[16,1,2]{2,1,0:T(1,128)S(1)} async-done(((f32[16,1,2]{2,1,0:T(1,128)}), f32[16,1,2]{2,1,0:T(1,128)S(1)}, u32[]{:S(2)}, u32[]{:S(2)}) %all-to-all-start.3) | async-done | bytes 160 | tf_op jit(solution)/shard_map/peaks/all_to_all | solution.py:213
  (32 shorter events, 5.6 us)
Async XLA Ops:
  7.2 86.3 %copy-start.1 = (bf16[1,4,64,2048]{3,2,1,0:T(8,128)(2,1)S(1)}, bf16[1,4,64,2048]{3,2,1,0:T(8,128)(2,1)}, u32[]{:S(2)}) copy-start(bf16[1,4,64,2048]{3,2,1,0:T(8,128)(2,1)} %param.4) | copy-start | bytes 3145732
  7.2 72.6 %all-gather.2.cloned.1.call-start = ((), (), s32[]{:S(2)}) async-start(), calls=%async_computation.4 | async-start | bytes 9437184 | tf_op jit(solution)/shard_map/tokens/all_gather | solution.py:240
  7.9 5.3 %collective-permute-start.2 = (bf16[6,2048]{1,0:T(8,128)(2,1)}, bf16[6,2048]{1,0:T(8,128)(2,1)S(1)}, u32[]{:S(2)}, u32[]{:S(2)}) collective-permute-start(bf16[6,2048]{1,0:T(8,128)(2,1)} %bitcast.8), channel_id=1, source_target_pairs={{21,149},{42,298},{85,212},{106,331},{149,245},{170,266},{213,180}... | collective-permute-start | bytes 73736 | tf_op jit(solution)/shard_map/ppermute | solution.py:225
  8.6 8.9 %collective-permute-start.1 = (bf16[6,2048]{1,0:T(8,128)(2,1)}, bf16[6,2048]{1,0:T(8,128)(2,1)S(1)}, u32[]{:S(2)}, u32[]{:S(2)}) collective-permute-start(bf16[6,2048]{1,0:T(8,128)(2,1)} %bitcast.9), channel_id=1, source_target_pairs={{0,0},{1,128},{2,2},{3,130},{4,4},{5,132},{6,6},{7,134},{8,8},{9,1... | collective-permute-start | bytes 73736 | tf_op jit(solution)/shard_map/ppermute | solution.py:224
  18.4 36.7 %all-to-all-start = ((bf16[16,96,128]{2,1,0:T(8,128)(2,1)}), bf16[16,96,128]{2,1,0:T(8,128)(2,1)S(1)}, u32[]{:S(2)}, u32[]{:S(2)}) async-start(bf16[16,96,128]{2,1,0:T(8,128)(2,1)} %broadcast_in_dim.12), calls=%async_computation | async-start | bytes 786432 | tf_op jit(solution)/shard_map/weights_over_z/all_to_all | solution.py:213
  34.8 34.2 %collective-permute-start = (s32[1,2]{1,0:T(1,128)}, s32[1,2]{1,0:T(1,128)S(1)}, u32[]{:S(2)}, u32[]{:S(2)}) collective-permute-start(s32[1,2]{1,0:T(1,128)} %param.7), channel_id=1, source_target_pairs={{0,1},{1,0},{2,3},{3,2},{4,5},{5,4},{6,7},{7,6},{8,9},{9,8},{10,11... | collective-permute-start | bytes 32 | tf_op jit(solution)/shard_map/ppermute | solution.py:218
  55.2 15.9 %collective-permute-start.5 = (bf16[96,2048]{1,0:T(8,128)(2,1)S(1)}, bf16[96,2048]{1,0:T(8,128)(2,1)S(1)}, u32[]{:S(2)}, u32[]{:S(2)}) collective-permute-start(bf16[96,2048]{1,0:T(8,128)(2,1)S(1)} %reshape.40.w0_ref), channel_id=1, source_target_pairs={{0,256},{128,384},{256,0},{384,128},{1,257},{129,385},{257,1},{385... | collective-permute-start | bytes 1179656 | tf_op jit(solution)/shard_map/weights_over_y/ppermute | solution.py:218
  62.7 13.6 %collective-permute-start.4 = (bf16[96,2048]{1,0:T(8,128)(2,1)S(1)}, bf16[96,2048]{1,0:T(8,128)(2,1)S(1)}, u32[]{:S(2)}, u32[]{:S(2)}) collective-permute-start(bf16[96,2048]{1,0:T(8,128)(2,1)S(1)} %reshape.40.w0_ref), channel_id=1, source_target_pairs={{0,384},{128,0},{256,128},{384,256},{1,385},{129,1},{257,129},{385... | collective-permute-start | bytes 1179656 | tf_op jit(solution)/shard_map/weights_over_y/ppermute | solution.py:218
  64.8 14.9 %collective-permute-start.3 = (bf16[96,2048]{1,0:T(8,128)(2,1)S(1)}, bf16[96,2048]{1,0:T(8,128)(2,1)S(1)}, u32[]{:S(2)}, u32[]{:S(2)}) collective-permute-start(bf16[96,2048]{1,0:T(8,128)(2,1)S(1)} %reshape.40.w0_ref), channel_id=1, source_target_pairs={{0,128},{128,256},{256,384},{384,0},{1,129},{129,257},{257,385},{3... | collective-permute-start | bytes 1179656 | tf_op jit(solution)/shard_map/weights_over_y/ppermute | solution.py:218
  79.7 3.4 %copy-start = (bf16[8,256,2048]{2,1,0:T(8,128)(2,1)S(1)}, bf16[8,256,2048]{2,1,0:T(8,128)(2,1)}, u32[]{:S(2)}) copy-start(bf16[8,256,2048]{2,1,0:T(8,128)(2,1)} %all-gather.2.cloned.1.call-done.x_ref) | copy-start | bytes 25165828
  88.5 9.9 %collective-permute-start.6 = (bf16[2,192,256]{2,1,0:T(8,128)(2,1)S(1)}, bf16[2,192,256]{2,1,0:T(8,128)(2,1)S(1)}, u32[]{:S(2)}, u32[]{:S(2)}) collective-permute-start(bf16[2,192,256]{2,1,0:T(8,128)(2,1)S(1)} %get-tuple-element.12), channel_id=1, source_target_pairs={{0,128},{128,256},{256,384},{1,129},{129,257},{257,385},{2,130},{1... | collective-permute-start | bytes 589832 | tf_op jit(solution)/shard_map/halo/ppermute | solution.py:250
  92.1 7.6 %collective-permute-start.7 = (bf16[2,192,256]{2,1,0:T(8,128)(2,1)S(1)}, bf16[2,192,256]{2,1,0:T(8,128)(2,1)S(1)}, u32[]{:S(2)}, u32[]{:S(2)}) collective-permute-start(bf16[2,192,256]{2,1,0:T(8,128)(2,1)S(1)} %get-tuple-element.13), channel_id=1, source_target_pairs={{128,0},{256,128},{384,256},{129,1},{257,129},{385,257},{130,2},{2... | collective-permute-start | bytes 589832 | tf_op jit(solution)/shard_map/halo/ppermute | solution.py:251
  126.5 18.5 %all-to-all-start.3 = ((f32[16,1,2]{2,1,0:T(1,128)}), f32[16,1,2]{2,1,0:T(1,128)S(1)}, u32[]{:S(2)}, u32[]{:S(2)}) async-start(f32[16,1,2]{2,1,0:T(1,128)} %broadcast_in_dim.25), calls=%async_computation.3 | async-start | bytes 16384 | tf_op jit(solution)/shard_map/peaks/all_to_all | solution.py:213
Sparse Core Ops, SparseCore 0:
  10.2 63.0 all-gather.1

commit v4 on v3

--- a/solution.py
+++ b/solution.py
@@ -21,7 +21,7 @@
 AXES = ("y", "x", "z", "core")
 GROUP = ("x", "core")
 PEAK_ROWS = 16
-INNER = (2, 3, 4, 5)
+KEYS = (ROWS + 2 * HALO) * COLS
 NEG = -1e30
 
 
@@ -100,10 +100,10 @@
     )(scale, tokens, *weights, order)
 
 
-def attend_rows(pairs, place_ref, qkv_ref, out_ref, kv):
+def attend_rows(units, place_ref, qkv_ref, out_ref, kv):
     base = place_ref[0]
-    scaling = float(HEAD) ** -0.5
-    shape = (2 * COLS, 8 * COLS)
+    scaling = float(HEAD) ** -0.5 * math.log2(math.e)
+    shape = (SET, KEYS)
     q_row = lax.broadcasted_iota(jnp.int32, shape, 0)
     k_row = lax.broadcasted_iota(jnp.int32, shape, 1)
     row_step = k_row // COLS - q_row // COLS
@@ -111,34 +111,33 @@
     window = (row_step >= 0) & (row_step <= 2 * HALO) & (col_step >= -HALO) & (col_step <= HALO)
     window = jnp.where(window, 0.0, NEG)
     centre = jnp.where((row_step == HALO) & (col_step == 0), 0.0, NEG)
-    key_at = lax.broadcasted_iota(jnp.int32, (1, 8 * COLS), 1)
-    query_at = lax.broadcasted_iota(jnp.int32, (2 * COLS, 1), 0)
-    highest = jnp.zeros((2 * COLS, HEAD), jnp.float32)
+    key_at = lax.broadcasted_iota(jnp.int32, (1, KEYS), 1)
+    query_at = lax.broadcasted_iota(jnp.int32, (SET, 1), 0)
+    highest = jnp.zeros((SET, HEAD), jnp.float32)
     for image in range(2):
         ext_rows, ext_cols = place_ref[1 + 2 * image], place_ref[2 + 2 * image]
-        for pair in pairs:
-            part, inner = pair // 2, (pair % 2) * 2 * COLS
-            query = qkv_ref[2 * part + image, inner : inner + 2 * COLS, :HEAD]
-            start = 2 * pair * COLS
-            keys = kv[image, start : start + 8 * COLS, :HEAD]
-            values = kv[image, start : start + 8 * COLS, HEAD:]
+        for unit in units:
+            query = qkv_ref[2 * unit + image, :, :HEAD]
+            start = unit * SET
+            keys = kv[image, start : start + KEYS, :HEAD]
+            values = kv[image, start : start + KEYS, HEAD:]
             scores = lax.dot_general(
                 query, keys, (((1,), (1,)), ((), ())), preferred_element_type=jnp.float32
             )
-            key_rows = base + (2 * pair - HALO) + key_at // COLS
+            key_rows = base + (ROWS * unit - HALO) + key_at // COLS
             key_cols = key_at % COLS
             valid = (key_rows >= 0) & (key_rows < ext_rows) & (key_cols < ext_cols)
             bias = jnp.where(valid, window, centre)
             scores = scores * scaling + bias
-            weights = jnp.exp(scores - jnp.max(scores, axis=1, keepdims=True))
+            weights = jnp.exp2(scores - jnp.max(scores, axis=1, keepdims=True))
             weights = weights * (1.0 / jnp.sum(weights, axis=1, keepdims=True))
             result = jnp.dot(
                 weights.astype(jnp.bfloat16), values, preferred_element_type=jnp.float32
             )
-            inside = (base + 2 * pair + query_at // COLS < ext_rows) & (query_at % COLS < ext_cols)
+            inside = (base + ROWS * unit + query_at // COLS < ext_rows) & (query_at % COLS < ext_cols)
             result = jnp.where(inside, result, 0.0).astype(jnp.bfloat16)
             highest = jnp.maximum(highest, jnp.abs(result.astype(jnp.float32)))
-            out_ref[2 * part + image, inner : inner + 2 * COLS, :] = result
+            out_ref[2 * unit + image, :SET] = result
     return highest
 
 
@@ -151,7 +150,7 @@
 
 def attend_inner_kernel(place_ref, qkv_ref, out_ref, highest_ref, kv):
     fill_keys(qkv_ref, kv)
-    highest_ref[...] = attend_rows(INNER, place_ref, qkv_ref, out_ref, kv)
+    highest_ref[...] = attend_rows((1, 2), place_ref, qkv_ref, out_ref, kv)
 
 
 def attend_outer_kernel(place_ref, peak_ref, qkv_ref, above_ref, below_ref, inner_ref, highest_ref, out_ref, kv):
@@ -159,12 +158,9 @@
         kv[image, : HALO * COLS] = above_ref[image]
         kv[image, KV_ROWS - HALO * COLS :] = below_ref[image]
     fill_keys(qkv_ref, kv)
-    for image in range(2):
-        for pair in INNER:
-            place = 2 * (pair // 2) + image, slice((pair % 2) * 2 * COLS, (pair % 2 + 1) * 2 * COLS)
-            out_ref[place] = inner_ref[place]
-    outer = [pair for pair in range(BLOCK // 2) if pair not in INNER]
-    highest = jnp.maximum(attend_rows(outer, place_ref, qkv_ref, out_ref, kv), highest_ref[...])
+    for group in range(2, 6):
+        out_ref[group, :SET] = inner_ref[group]
+    highest = jnp.maximum(attend_rows((0, 3), place_ref, qkv_ref, out_ref, kv), highest_ref[...])
     lines = lax.broadcasted_iota(jnp.int32, (PEAK_ROWS, HEAD), 0)
     peaks = jnp.where(lines < PEAK_ROWS // 2, peak_ref[0], jnp.max(highest)).astype(jnp.bfloat16)
     for group in range(8):
@@ -177,14 +173,14 @@
         attend_inner_kernel,
         out_shape=(
             jax.ShapeDtypeStruct((8, SET, HEAD), jnp.bfloat16),
-            jax.ShapeDtypeStruct((2 * COLS, HEAD), jnp.float32),
+            jax.ShapeDtypeStruct((SET, HEAD), jnp.float32),
         ),
         in_specs=[pl.BlockSpec(memory_space=pltpu.SMEM), vmem],
         out_specs=(vmem, vmem),
         scratch_shapes=[pltpu.VMEM((2, KV_ROWS, 2 * HEAD), jnp.bfloat16)],
         compiler_params=pltpu.CompilerParams(vmem_limit_bytes=24 * 2**20),
         cost_estimate=pl.CostEstimate(
-            flops=4 * 8 * 128 * 512 * HEAD, bytes_accessed=2 * 2**20, transcendentals=8 * 128 * 512
+            flops=4 * 4 * SET * KEYS * HEAD, bytes_accessed=2 * 2**20, transcendentals=4 * SET * KEYS
         ),
         name="attend_inner",
     )(place, qkv)
@@ -201,7 +197,7 @@
         scratch_shapes=[pltpu.VMEM((2, KV_ROWS, 2 * HEAD), jnp.bfloat16)],
         compiler_params=pltpu.CompilerParams(vmem_limit_bytes=24 * 2**20),
         cost_estimate=pl.CostEstimate(
-            flops=4 * 8 * 128 * 512 * HEAD, bytes_accessed=3 * 2**20, transcendentals=8 * 128 * 512
+            flops=4 * 4 * SET * KEYS * HEAD, bytes_accessed=3 * 2**20, transcendentals=4 * SET * KEYS
         ),
         name="attend_outer",
     )(place, peak_in, qkv, above, below, inner, highest)
@@ -239,12 +235,13 @@
     with jax.named_scope("tokens"):
         tokens = lax.all_gather(images.reshape(SET, D), GROUP, axis=0, tiled=False)
     weights, late = head_weights(w_qkv, images)
-    peak_in = jnp.max(jnp.abs(late)).astype(jnp.float32).reshape(1)
     core = lax.axis_index("core")
     order = column_order(2 * lax.axis_index("x") + core, lax.axis_index("y"))
     other = shift(extent, "core", 1)
+    peak_in = jnp.max(jnp.abs(late)).astype(jnp.float32).reshape(1)
     extents = jnp.where(core == 0, jnp.concatenate([extent, other]), jnp.concatenate([other, extent]))
     place = jnp.stack([lax.axis_index("y") * BLOCK, *extents.reshape(4)]).astype(jnp.int32)
+    order, peak_in, place = lax.optimization_barrier((order, peak_in, place))
     qkv, top, bottom = project(prev_scale, tokens, weights, order)
     with jax.named_scope("halo"):
         above = lax.ppermute(bottom, "y", [(i, i + 1) for i in range(3)])

time: 154 us -> 153 us (level)
    ppermute x1, waiting for transfers between devices: 1.35 us -> 3.33 us  [local(): below = lax.ppermute(top, 'y', [(i + 1, i) for i in range(3)])]
    ppermute x4, waiting for transfers between devices: 9.84 us -> 8.17 us  [shift(): lax.ppermute(value, axis, [(i, (i + step) % size) for i in range(size)])]
    unnamed x4 -> x2, local copies, waits for them, and re-layouts: 3.39 us -> 3.38 us
  transfers between devices with their start and end apart: 11 -> 11, of which waited for: 7 -> 6; matrix products, arithmetic and copies ran while one was open for 3% -> 4% of each run, Pallas kernels for 2% -> 2%
where the time goes in v4:
time: 153 us; the launch traced here: 152 us
  starting transfers between devices  48.7 us (32%)
  waiting for transfers between devices  43.6 us (28%)
  blocking collectives  22.2 us (15%)
  between operations  15.6 us (10%)
  Pallas kernels  11.3 us (7%)
  local copies, waits for them, and re-layouts  6.58 us (4%)
  other arithmetic  4.02 us (3%)
    all_to_all x2, waiting for transfers between devices, spread(): return lax.all_to_all(copies, axis, 0, 0, tiled=True)  27.2 us
    all_to_all x2, starting transfers between devices, spread(): return lax.all_to_all(copies, axis, 0, 0, tiled=True)  23.7 us
    all_to_all x1, blocking collectives, local(): mixed = lax.all_to_all(mixed, GROUP, 0, 0, tiled=True)  14.9 us
    ppermute x4, starting transfers between devices, shift(): lax.ppermute(value, axis, [(i, (i + step) % size) for i in range(size)])  14.8 us
    ppermute x4, waiting for transfers between devices, shift(): lax.ppermute(value, axis, [(i, (i + step) % size) for i in range(size)])  8.17 us
    all_to_all x1, blocking collectives, spread(): return lax.all_to_all(copies, axis, 0, 0, tiled=True)  7.26 us
    pallas_call x1, Pallas kernels, project(): pl.pallas_call(project_kernel, out_shape=(jax.ShapeDtypeStruct((8, SET, 3...  5.34 us
    ppermute x1, starting transfers between devices, head_weights(): first = lax.ppermute(mine, AXES, main)  4.59 us
  transfers between devices with their start and end apart: 11, of which 6 were waited for; matrix products, arithmetic and copies ran while one was open for 4% of the time, Pallas kernels for 2%

profile of v4, /device:TPU:1, one launch (start us, length us, event | category | flops | bytes accessed | tf_op | source)
XLA Modules:
  0.0 151.9 jit_solution(1165266191925642862)
XLA Ops:
  8.6 4.6 %collective-permute-start = (bf16[6,2048]{1,0:T(8,128)(2,1)}, bf16[6,2048]{1,0:T(8,128)(2,1)S(1)}, u32[]{:S(2)}, u32[]{:S(2)}) collective-permute-start(bf16[6,2048]{1,0:T(8,128)(2,1)} %bitcast.9), channel_id=1, source_target_pairs={{0,0},{1,128},{2,2},{3,130},{4,4},{5,132},{6,6},{7,134},{8,8},{9,1... | collective-permute-start | bytes 73736 | tf_op jit(solution)/shard_map/ppermute | solution.py:220
  13.2 4.2 %collective-permute-done = bf16[6,2048]{1,0:T(8,128)(2,1)S(1)} collective-permute-done((bf16[6,2048]{1,0:T(8,128)(2,1)}, bf16[6,2048]{1,0:T(8,128)(2,1)S(1)}, u32[]{:S(2)}, u32[]{:S(2)}) %collective-permute-start) | collective-permute-done | bytes 24608 | tf_op jit(solution)/shard_map/ppermute | solution.py:220
  17.6 0.8 broadcast_in_dim.12
  18.4 16.4 %all-to-all-start = ((bf16[16,96,128]{2,1,0:T(8,128)(2,1)}), bf16[16,96,128]{2,1,0:T(8,128)(2,1)S(1)}, u32[]{:S(2)}, u32[]{:S(2)}) async-start(bf16[16,96,128]{2,1,0:T(8,128)(2,1)} %broadcast_in_dim.12), calls=%async_computation | async-start | bytes 786432 | tf_op jit(solution)/shard_map/weights_over_z/all_to_all | solution.py:209
  34.7 2.0 %collective-permute-start.2 = (s32[1,2]{1,0:T(1,128)}, s32[1,2]{1,0:T(1,128)S(1)}, u32[]{:S(2)}, u32[]{:S(2)}) collective-permute-start(s32[1,2]{1,0:T(1,128)} %param.7), channel_id=1, source_target_pairs={{0,1},{1,0},{2,3},{3,2},{4,5},{5,4},{6,7},{7,6},{8,9},{9,8},{10,11... | collective-permute-start | bytes 32 | tf_op jit(solution)/shard_map/ppermute | solution.py:214
  37.7 17.3 %all-to-all-done = bf16[16,96,128]{2,1,0:T(8,128)(2,1)S(1)} async-done(((bf16[16,96,128]{2,1,0:T(8,128)(2,1)}), bf16[16,96,128]{2,1,0:T(8,128)(2,1)S(1)}, u32[]{:S(2)}, u32[]{:S(2)}) %all-to-all-start) | async-done | bytes 393248 | tf_op jit(solution)/shard_map/weights_over_z/all_to_all | solution.py:209
  55.2 7.5 %collective-permute-start.5 = (bf16[96,2048]{1,0:T(8,128)(2,1)S(1)}, bf16[96,2048]{1,0:T(8,128)(2,1)S(1)}, u32[]{:S(2)}, u32[]{:S(2)}) collective-permute-start(bf16[96,2048]{1,0:T(8,128)(2,1)S(1)} %reshape.41.w0_ref), channel_id=1, source_target_pairs={{0,256},{128,384},{256,0},{384,128},{1,257},{129,385},{257,1},{385... | collective-permute-start | bytes 1179656 | tf_op jit(solution)/shard_map/weights_over_y/ppermute | solution.py:214
  62.7 2.1 %collective-permute-start.4 = (bf16[96,2048]{1,0:T(8,128)(2,1)S(1)}, bf16[96,2048]{1,0:T(8,128)(2,1)S(1)}, u32[]{:S(2)}, u32[]{:S(2)}) collective-permute-start(bf16[96,2048]{1,0:T(8,128)(2,1)S(1)} %reshape.41.w0_ref), channel_id=1, source_target_pairs={{0,384},{128,0},{256,128},{384,256},{1,385},{129,1},{257,129},{385... | collective-permute-start | bytes 1179656 | tf_op jit(solution)/shard_map/weights_over_y/ppermute | solution.py:214
  64.8 3.2 %collective-permute-start.3 = (bf16[96,2048]{1,0:T(8,128)(2,1)S(1)}, bf16[96,2048]{1,0:T(8,128)(2,1)S(1)}, u32[]{:S(2)}, u32[]{:S(2)}) collective-permute-start(bf16[96,2048]{1,0:T(8,128)(2,1)S(1)} %reshape.41.w0_ref), channel_id=1, source_target_pairs={{0,128},{128,256},{256,384},{384,0},{1,129},{129,257},{257,385},{3... | collective-permute-start | bytes 1179656 | tf_op jit(solution)/shard_map/weights_over_y/ppermute | solution.py:214
  68.9 2.0 %abs_reduce_fusion = bf16[]{:T(256)} fusion(bf16[1,4,64,2048]{3,2,1,0:T(8,128)(2,1)} %param.4), kind=kLoop, calls=%fused_computation | loop fusion | flops 1048575 | bytes 1048578 | tf_op jit(solution)/shard_map/reduce_max | solution.py:241
  71.6 4.8 %collective-permute-done.4.w2_ref = bf16[96,2048]{1,0:T(8,128)(2,1)S(1)} collective-permute-done((bf16[96,2048]{1,0:T(8,128)(2,1)S(1)}, bf16[96,2048]{1,0:T(8,128)(2,1)S(1)}, u32[]{:S(2)}, u32[]{:S(2)}) %collective-permute-start.4) | collective-permute-done | bytes 393248 | tf_op jit(solution)/shard_map/weights_over_y/ppermute | solution.py:214
  76.3 3.4 %collective-permute-done.3.w1_ref = bf16[96,2048]{1,0:T(8,128)(2,1)S(1)} collective-permute-done((bf16[96,2048]{1,0:T(8,128)(2,1)S(1)}, bf16[96,2048]{1,0:T(8,128)(2,1)S(1)}, u32[]{:S(2)}, u32[]{:S(2)}) %collective-permute-start.3) | collective-permute-done | bytes 393248 | tf_op jit(solution)/shard_map/weights_over_y/ppermute | solution.py:214
  79.7 3.4 %copy-done = bf16[8,256,2048]{2,1,0:T(8,128)(2,1)S(1)} copy-done((bf16[8,256,2048]{2,1,0:T(8,128)(2,1)S(1)}, bf16[8,256,2048]{2,1,0:T(8,128)(2,1)}, u32[]{:S(2)}) %copy-start) | copy-done | bytes 8388632
  83.1 5.3 %project.1 = (bf16[8,256,384]{2,1,0:T(8,128)(2,1)S(1)}, bf16[2,192,256]{2,1,0:T(8,128)(2,1)S(1)}, bf16[2,192,256]{2,1,0:T(8,128)(2,1)S(1)}) custom-call(f32[1]{0:T(128)S(6)} %copy.14.scale_ref, bf16[8,256,2048]{2,1,0:T(8,128)(2,1)S(1)} %copy-done, bf16[96,2048]{1,0:T(8,128)(2,1)S(1)} %reshape.41.w0_ref, bf16[96,2048]{1,0:T(8,128)(2,1)S(1)} %collective-permute-done.3.w1_ref, ...), custom_call_target="tpu_custom_call" | custom-call | flops 3221225472 | bytes 12582912 | tf_op jit(solution)/shard_map/project/pallas_call | solution.py:89
  88.5 3.7 %collective-permute-start.6 = (bf16[2,192,256]{2,1,0:T(8,128)(2,1)S(1)}, bf16[2,192,256]{2,1,0:T(8,128)(2,1)S(1)}, u32[]{:S(2)}, u32[]{:S(2)}) collective-permute-start(bf16[2,192,256]{2,1,0:T(8,128)(2,1)S(1)} %get-tuple-element.18), channel_id=1, source_target_pairs={{0,128},{128,256},{256,384},{1,129},{129,257},{257,385},{2,130},{1... | collective-permute-start | bytes 589832 | tf_op jit(solution)/shard_map/halo/ppermute | solution.py:247
  92.1 1.3 collective-permute-start.7
  93.4 2.9 %attend_inner.1 = (bf16[8,256,128]{2,1,0:T(8,128)(2,1)S(1)}, f32[256,128]{1,0:T(8,128)S(1)}) custom-call(s32[5]{0:T(128)S(1)} %pad_add_fusion.place_ref, bf16[8,256,384]{2,1,0:T(8,128)(2,1)S(1)} %get-tuple-element.17.qkv_ref), custom_call_target="tpu_custom_call" | custom-call | flops 335544320 | bytes 2097152 | tf_op jit(solution)/shard_map/attend_inner/pallas_call | solution.py:172
  96.4 3.3 %collective-permute-done.7.below_ref = bf16[2,192,256]{2,1,0:T(8,128)(2,1)S(1)} collective-permute-done((bf16[2,192,256]{2,1,0:T(8,128)(2,1)S(1)}, bf16[2,192,256]{2,1,0:T(8,128)(2,1)S(1)}, u32[]{:S(2)}, u32[]{:S(2)}) %collective-permute-start.7) | collective-permute-done | bytes 196640 | tf_op jit(solution)/shard_map/halo/ppermute | solution.py:248
  99.7 3.1 %attend_outer.1 = bf16[8,272,128]{2,1,0:T(8,128)(2,1)S(1)} custom-call(s32[5]{0:T(128)S(1)} %pad_add_fusion.place_ref, f32[1]{0:T(128)S(6)} %convert.6.peak_ref, bf16[8,256,384]{2,1,0:T(8,128)(2,1)S(1)} %get-tuple-element.17.qkv_ref, bf16[2,192,256]{2,1,0:T(8,128)(2,1)S(1)} %collective-permute-done.6.above_ref, ...), custom_call_target="tpu_custom_call" | custom-call | flops 335544320 | bytes 3145728 | tf_op jit(solution)/shard_map/attend_outer/pallas_call | solution.py:192
  102.8 14.9 %all_to_all.22 = bf16[8,272,128]{2,1,0:T(8,128)(2,1)S(1)} all-to-all(bf16[8,272,128]{2,1,0:T(8,128)(2,1)S(1)} %attend_outer.1), channel_id=1, replica_groups=mesh['y'=4,'x'=4,'z'=16,'core'=2] {'x','core'}, dimensions={0} | all-to-all | bytes 1114112 | tf_op jit(solution)/shard_map/heads/all_to_all | solution.py:252
  118.0 7.3 %all_to_all.23 = f32[4,1,2]{2,1,0:T(1,128)S(1)} all-to-all(f32[4,1,2]{2,1,0:T(1,128)S(1)} %broadcast_in_dim.24), channel_id=1, replica_groups=mesh['y'=4,'x'=4,'z'=16,'core'=2] {'y'}, dimensions={0} | all-to-all | bytes 64 | tf_op jit(solution)/shard_map/peaks/all_to_all | solution.py:209
  125.9 7.3 %all-to-all-start.3 = ((f32[16,1,2]{2,1,0:T(1,128)}), f32[16,1,2]{2,1,0:T(1,128)S(1)}, u32[]{:S(2)}, u32[]{:S(2)}) async-start(f32[16,1,2]{2,1,0:T(1,128)} %broadcast_in_dim.25), calls=%async_computation.3 | async-start | bytes 16384 | tf_op jit(solution)/shard_map/peaks/all_to_all | solution.py:209
  133.6 1.0 reshape.45
  134.6 9.9 %all-to-all-done.3 = f32[16,1,2]{2,1,0:T(1,128)S(1)} async-done(((f32[16,1,2]{2,1,0:T(1,128)}), f32[16,1,2]{2,1,0:T(1,128)S(1)}, u32[]{:S(2)}, u32[]{:S(2)}) %all-to-all-start.3) | async-done | bytes 160 | tf_op jit(solution)/shard_map/peaks/all_to_all | solution.py:209
  (30 shorter events, 4.8 us)
Async XLA Ops:
  7.2 72.6 %all-gather.2.cloned.1.call-start = ((), (), s32[]{:S(2)}) async-start(), calls=%async_computation.4 | async-start | bytes 9437184 | tf_op jit(solution)/shard_map/tokens/all_gather | solution.py:236
  7.9 5.3 %collective-permute-start.1 = (bf16[6,2048]{1,0:T(8,128)(2,1)}, bf16[6,2048]{1,0:T(8,128)(2,1)S(1)}, u32[]{:S(2)}, u32[]{:S(2)}) collective-permute-start(bf16[6,2048]{1,0:T(8,128)(2,1)} %bitcast.8), channel_id=1, source_target_pairs={{21,149},{42,298},{85,212},{106,331},{149,245},{170,266},{213,180}... | collective-permute-start | bytes 73736 | tf_op jit(solution)/shard_map/ppermute | solution.py:221
  8.6 8.9 %collective-permute-start = (bf16[6,2048]{1,0:T(8,128)(2,1)}, bf16[6,2048]{1,0:T(8,128)(2,1)S(1)}, u32[]{:S(2)}, u32[]{:S(2)}) collective-permute-start(bf16[6,2048]{1,0:T(8,128)(2,1)} %bitcast.9), channel_id=1, source_target_pairs={{0,0},{1,128},{2,2},{3,130},{4,4},{5,132},{6,6},{7,134},{8,8},{9,1... | collective-permute-start | bytes 73736 | tf_op jit(solution)/shard_map/ppermute | solution.py:220
  18.4 36.7 %all-to-all-start = ((bf16[16,96,128]{2,1,0:T(8,128)(2,1)}), bf16[16,96,128]{2,1,0:T(8,128)(2,1)S(1)}, u32[]{:S(2)}, u32[]{:S(2)}) async-start(bf16[16,96,128]{2,1,0:T(8,128)(2,1)} %broadcast_in_dim.12), calls=%async_computation | async-start | bytes 786432 | tf_op jit(solution)/shard_map/weights_over_z/all_to_all | solution.py:209
  34.7 33.3 %collective-permute-start.2 = (s32[1,2]{1,0:T(1,128)}, s32[1,2]{1,0:T(1,128)S(1)}, u32[]{:S(2)}, u32[]{:S(2)}) collective-permute-start(s32[1,2]{1,0:T(1,128)} %param.7), channel_id=1, source_target_pairs={{0,1},{1,0},{2,3},{3,2},{4,5},{5,4},{6,7},{7,6},{8,9},{9,8},{10,11... | collective-permute-start | bytes 32 | tf_op jit(solution)/shard_map/ppermute | solution.py:214
  55.2 16.4 %collective-permute-start.5 = (bf16[96,2048]{1,0:T(8,128)(2,1)S(1)}, bf16[96,2048]{1,0:T(8,128)(2,1)S(1)}, u32[]{:S(2)}, u32[]{:S(2)}) collective-permute-start(bf16[96,2048]{1,0:T(8,128)(2,1)S(1)} %reshape.41.w0_ref), channel_id=1, source_target_pairs={{0,256},{128,384},{256,0},{384,128},{1,257},{129,385},{257,1},{385... | collective-permute-start | bytes 1179656 | tf_op jit(solution)/shard_map/weights_over_y/ppermute | solution.py:214
  62.7 13.6 %collective-permute-start.4 = (bf16[96,2048]{1,0:T(8,128)(2,1)S(1)}, bf16[96,2048]{1,0:T(8,128)(2,1)S(1)}, u32[]{:S(2)}, u32[]{:S(2)}) collective-permute-start(bf16[96,2048]{1,0:T(8,128)(2,1)S(1)} %reshape.41.w0_ref), channel_id=1, source_target_pairs={{0,384},{128,0},{256,128},{384,256},{1,385},{129,1},{257,129},{385... | collective-permute-start | bytes 1179656 | tf_op jit(solution)/shard_map/weights_over_y/ppermute | solution.py:214
  64.8 14.9 %collective-permute-start.3 = (bf16[96,2048]{1,0:T(8,128)(2,1)S(1)}, bf16[96,2048]{1,0:T(8,128)(2,1)S(1)}, u32[]{:S(2)}, u32[]{:S(2)}) collective-permute-start(bf16[96,2048]{1,0:T(8,128)(2,1)S(1)} %reshape.41.w0_ref), channel_id=1, source_target_pairs={{0,128},{128,256},{256,384},{384,0},{1,129},{129,257},{257,385},{3... | collective-permute-start | bytes 1179656 | tf_op jit(solution)/shard_map/weights_over_y/ppermute | solution.py:214
  79.7 3.4 %copy-start = (bf16[8,256,2048]{2,1,0:T(8,128)(2,1)S(1)}, bf16[8,256,2048]{2,1,0:T(8,128)(2,1)}, u32[]{:S(2)}) copy-start(bf16[8,256,2048]{2,1,0:T(8,128)(2,1)} %all-gather.2.cloned.1.call-done.x_ref) | copy-start | bytes 25165828
  88.5 7.9 %collective-permute-start.6 = (bf16[2,192,256]{2,1,0:T(8,128)(2,1)S(1)}, bf16[2,192,256]{2,1,0:T(8,128)(2,1)S(1)}, u32[]{:S(2)}, u32[]{:S(2)}) collective-permute-start(bf16[2,192,256]{2,1,0:T(8,128)(2,1)S(1)} %get-tuple-element.18), channel_id=1, source_target_pairs={{0,128},{128,256},{256,384},{1,129},{129,257},{257,385},{2,130},{1... | collective-permute-start | bytes 589832 | tf_op jit(solution)/shard_map/halo/ppermute | solution.py:247
  92.1 7.6 %collective-permute-start.7 = (bf16[2,192,256]{2,1,0:T(8,128)(2,1)S(1)}, bf16[2,192,256]{2,1,0:T(8,128)(2,1)S(1)}, u32[]{:S(2)}, u32[]{:S(2)}) collective-permute-start(bf16[2,192,256]{2,1,0:T(8,128)(2,1)S(1)} %get-tuple-element.19), channel_id=1, source_target_pairs={{128,0},{256,128},{384,256},{129,1},{257,129},{385,257},{130,2},{2... | collective-permute-start | bytes 589832 | tf_op jit(solution)/shard_map/halo/ppermute | solution.py:248
  125.9 18.6 %all-to-all-start.3 = ((f32[16,1,2]{2,1,0:T(1,128)}), f32[16,1,2]{2,1,0:T(1,128)S(1)}, u32[]{:S(2)}, u32[]{:S(2)}) async-start(f32[16,1,2]{2,1,0:T(1,128)} %broadcast_in_dim.25), calls=%async_computation.3 | async-start | bytes 16384 | tf_op jit(solution)/shard_map/peaks/all_to_all | solution.py:209
Sparse Core Ops, SparseCore 0:
  10.1 63.0 all-gather.1

commit v5 on v4

--- a/solution.py
+++ b/solution.py
@@ -22,6 +22,7 @@
 GROUP = ("x", "core")
 PEAK_ROWS = 16
 KEYS = (ROWS + 2 * HALO) * COLS
+OUTER, INNER = (0, 3), (1, 2)
 NEG = -1e30
 
 
@@ -60,15 +61,10 @@
     return (place * 96 + z * 6 + j == r).astype(jnp.bfloat16)
 
 
-def project_kernel(scale_ref, x_ref, w0_ref, w1_ref, w2_ref, w3_ref, order_ref, qkv_ref, top_ref, bottom_ref, w_cat, w_scr):
+def project_rows(scale_ref, x_ref, w_scr, qkv_ref, parts):
     scale = scale_ref[0]
     inverse = 1.0 / scale
-    for part, ref in enumerate((w0_ref, w1_ref, w2_ref, w3_ref)):
-        w_cat[96 * part : 96 * (part + 1)] = ref[...]
-    w_scr[...] = lax.dot_general(
-        order_ref[...], w_cat[...], (((0,), (0,)), ((), ())), preferred_element_type=jnp.float32
-    ).astype(jnp.bfloat16)
-    for part in range(4):
+    for place, part in enumerate(parts):
         tokens = x_ref[2 * part : 2 * part + 2].reshape(2 * SET, D)
         tokens = (tokens.astype(jnp.float32) * inverse).astype(jnp.bfloat16)
         tokens = jnp.clip(tokens, -FP_TOP, FP_TOP)
@@ -76,31 +72,67 @@
             tokens, w_scr[...], (((1,), (1,)), ((), ())), preferred_element_type=jnp.float32
         )
         out = (out * scale).astype(jnp.bfloat16).reshape(2, SET, 3 * HEAD)
-        qkv_ref[2 * part : 2 * part + 2] = out
-        if part == 0:
-            top_ref[...] = out[:, : HALO * COLS, HEAD:]
-        if part == 3:
-            bottom_ref[...] = out[:, SET - HALO * COLS :, HEAD:]
-
-
-def project(scale, tokens, weights, order):
+        qkv_ref[2 * place : 2 * place + 2] = out
+
+
+def project_outer_kernel(scale_ref, x_ref, w0_ref, w1_ref, w2_ref, w3_ref, order_ref, qkv_ref, top_ref, bottom_ref, w_ref, w_cat):
+    for part, ref in enumerate((w0_ref, w1_ref, w2_ref, w3_ref)):
+        w_cat[96 * part : 96 * (part + 1)] = ref[...]
+    w_ref[...] = lax.dot_general(
+        order_ref[...], w_cat[...], (((0,), (0,)), ((), ())), preferred_element_type=jnp.float32
+    ).astype(jnp.bfloat16)
+    project_rows(scale_ref, x_ref, w_ref, qkv_ref, OUTER)
+    top_ref[...] = qkv_ref[:2, : HALO * COLS, HEAD:]
+    bottom_ref[...] = qkv_ref[2:, SET - HALO * COLS :, HEAD:]
+
+
+def project_inner_kernel(scale_ref, x_ref, w_ref, qkv_ref):
+    project_rows(scale_ref, x_ref, w_ref, qkv_ref, INNER)
+
+
+def project_outer(scale, tokens, weights, order):
     halo = jax.ShapeDtypeStruct((2, HALO * COLS, 2 * HEAD), jnp.bfloat16)
     vmem = pl.BlockSpec(memory_space=pltpu.VMEM)
     return pl.pallas_call(
-        project_kernel,
-        out_shape=(jax.ShapeDtypeStruct((8, SET, 3 * HEAD), jnp.bfloat16), halo, halo),
+        project_outer_kernel,
+        out_shape=(
+            jax.ShapeDtypeStruct((4, SET, 3 * HEAD), jnp.bfloat16),
+            halo,
+            halo,
+            jax.ShapeDtypeStruct((3 * HEAD, D), jnp.bfloat16),
+        ),
         in_specs=[pl.BlockSpec(memory_space=pltpu.SMEM)] + [vmem] * 6,
-        out_specs=(vmem, vmem, vmem),
-        scratch_shapes=[pltpu.VMEM((3 * HEAD, D), jnp.bfloat16)] * 2,
+        out_specs=(vmem,) * 4,
+        scratch_shapes=[pltpu.VMEM((3 * HEAD, D), jnp.bfloat16)],
         compiler_params=pltpu.CompilerParams(vmem_limit_bytes=24 * 2**20),
         cost_estimate=pl.CostEstimate(
-            flops=2 * 8 * SET * D * 3 * HEAD, bytes_accessed=12 * 2**20, transcendentals=0
-        ),
-        name="project",
+            flops=2 * 4 * SET * D * 3 * HEAD, bytes_accessed=8 * 2**20, transcendentals=0
+        ),
+        name="project_outer",
     )(scale, tokens, *weights, order)
 
 
-def attend_rows(units, place_ref, qkv_ref, out_ref, kv):
+def project_inner(scale, tokens, weights):
+    vmem = pl.BlockSpec(memory_space=pltpu.VMEM)
+    return pl.pallas_call(
+        project_inner_kernel,
+        out_shape=jax.ShapeDtypeStruct((4, SET, 3 * HEAD), jnp.bfloat16),
+        in_specs=[pl.BlockSpec(memory_space=pltpu.SMEM), vmem, vmem],
+        out_specs=vmem,
+        compiler_params=pltpu.CompilerParams(vmem_limit_bytes=24 * 2**20),
+        cost_estimate=pl.CostEstimate(
+            flops=2 * 4 * SET * D * 3 * HEAD, bytes_accessed=6 * 2**20, transcendentals=0
+        ),
+        name="project_inner",
+    )(scale, tokens, weights)
+
+
+def tile_column(outer_ref, inner_ref, part, image):
+    ref, parts = (outer_ref, OUTER) if part in OUTER else (inner_ref, INNER)
+    return ref.at[2 * parts.index(part) + image]
+
+
+def attend_rows(units, place_ref, outer_ref, inner_ref, out_ref, kv):
     base = place_ref[0]
     scaling = float(HEAD) ** -0.5 * math.log2(math.e)
     shape = (SET, KEYS)
@@ -117,7 +149,7 @@
     for image in range(2):
         ext_rows, ext_cols = place_ref[1 + 2 * image], place_ref[2 + 2 * image]
         for unit in units:
-            query = qkv_ref[2 * unit + image, :, :HEAD]
+            query = tile_column(outer_ref, inner_ref, unit, image)[:, :HEAD]
             start = unit * SET
             keys = kv[image, start : start + KEYS, :HEAD]
             values = kv[image, start : start + KEYS, HEAD:]
@@ -141,33 +173,33 @@
     return highest
 
 
-def fill_keys(qkv_ref, kv):
+def fill_keys(outer_ref, inner_ref, kv):
     for image in range(2):
         for part in range(4):
             start = HALO * COLS + part * SET
-            kv[image, start : start + SET] = qkv_ref[2 * part + image, :, HEAD:]
-
-
-def attend_inner_kernel(place_ref, qkv_ref, out_ref, highest_ref, kv):
-    fill_keys(qkv_ref, kv)
-    highest_ref[...] = attend_rows((1, 2), place_ref, qkv_ref, out_ref, kv)
-
-
-def attend_outer_kernel(place_ref, peak_ref, qkv_ref, above_ref, below_ref, inner_ref, highest_ref, out_ref, kv):
+            kv[image, start : start + SET] = tile_column(outer_ref, inner_ref, part, image)[:, HEAD:]
+
+
+def attend_inner_kernel(place_ref, outer_ref, inner_ref, out_ref, highest_ref, kv):
+    fill_keys(outer_ref, inner_ref, kv)
+    highest_ref[...] = attend_rows(INNER, place_ref, outer_ref, inner_ref, out_ref, kv)
+
+
+def attend_outer_kernel(place_ref, peak_ref, outer_ref, inner_ref, above_ref, below_ref, done_ref, highest_ref, out_ref, kv):
     for image in range(2):
         kv[image, : HALO * COLS] = above_ref[image]
         kv[image, KV_ROWS - HALO * COLS :] = below_ref[image]
-    fill_keys(qkv_ref, kv)
+    fill_keys(outer_ref, inner_ref, kv)
     for group in range(2, 6):
-        out_ref[group, :SET] = inner_ref[group]
-    highest = jnp.maximum(attend_rows((0, 3), place_ref, qkv_ref, out_ref, kv), highest_ref[...])
+        out_ref[group, :SET] = done_ref[group]
+    highest = jnp.maximum(attend_rows(OUTER, place_ref, outer_ref, inner_ref, out_ref, kv), highest_ref[...])
     lines = lax.broadcasted_iota(jnp.int32, (PEAK_ROWS, HEAD), 0)
     peaks = jnp.where(lines < PEAK_ROWS // 2, peak_ref[0], jnp.max(highest)).astype(jnp.bfloat16)
     for group in range(8):
         out_ref[group, SET:, :] = peaks
 
 
-def attend_inner(place, qkv):
+def attend_inner(place, outer, inner):
     vmem = pl.BlockSpec(memory_space=pltpu.VMEM)
     return pl.pallas_call(
         attend_inner_kernel,
@@ -175,7 +207,7 @@
             jax.ShapeDtypeStruct((8, SET, HEAD), jnp.bfloat16),
             jax.ShapeDtypeStruct((SET, HEAD), jnp.float32),
         ),
-        in_specs=[pl.BlockSpec(memory_space=pltpu.SMEM), vmem],
+        in_specs=[pl.BlockSpec(memory_space=pltpu.SMEM), vmem, vmem],
         out_specs=(vmem, vmem),
         scratch_shapes=[pltpu.VMEM((2, KV_ROWS, 2 * HEAD), jnp.bfloat16)],
         compiler_params=pltpu.CompilerParams(vmem_limit_bytes=24 * 2**20),
@@ -183,16 +215,16 @@
             flops=4 * 4 * SET * KEYS * HEAD, bytes_accessed=2 * 2**20, transcendentals=4 * SET * KEYS
         ),
         name="attend_inner",
-    )(place, qkv)
-
-
-def attend_outer(place, peak_in, qkv, above, below, inner, highest):
+    )(place, outer, inner)
+
+
+def attend_outer(place, peak_in, outer, inner, above, below, done, highest):
     vmem = pl.BlockSpec(memory_space=pltpu.VMEM)
     smem = pl.BlockSpec(memory_space=pltpu.SMEM)
     return pl.pallas_call(
         attend_outer_kernel,
         out_shape=jax.ShapeDtypeStruct((8, SET + PEAK_ROWS, HEAD), jnp.bfloat16),
-        in_specs=[smem, smem] + [vmem] * 5,
+        in_specs=[smem, smem] + [vmem] * 6,
         out_specs=vmem,
         scratch_shapes=[pltpu.VMEM((2, KV_ROWS, 2 * HEAD), jnp.bfloat16)],
         compiler_params=pltpu.CompilerParams(vmem_limit_bytes=24 * 2**20),
@@ -200,7 +232,7 @@
             flops=4 * 4 * SET * KEYS * HEAD, bytes_accessed=3 * 2**20, transcendentals=4 * SET * KEYS
         ),
         name="attend_outer",
-    )(place, peak_in, qkv, above, below, inner, highest)
+    )(place, peak_in, outer, inner, above, below, done, highest)
 
 
 def spread(value, axis):
@@ -242,12 +274,13 @@
     extents = jnp.where(core == 0, jnp.concatenate([extent, other]), jnp.concatenate([other, extent]))
     place = jnp.stack([lax.axis_index("y") * BLOCK, *extents.reshape(4)]).astype(jnp.int32)
     order, peak_in, place = lax.optimization_barrier((order, peak_in, place))
-    qkv, top, bottom = project(prev_scale, tokens, weights, order)
+    outer, top, bottom, weights = project_outer(prev_scale, tokens, weights, order)
     with jax.named_scope("halo"):
         above = lax.ppermute(bottom, "y", [(i, i + 1) for i in range(3)])
         below = lax.ppermute(top, "y", [(i + 1, i) for i in range(3)])
-    inner, highest = attend_inner(place, qkv)
-    mixed = attend_outer(place, peak_in, qkv, above, below, inner, highest)
+    inner = project_inner(prev_scale, tokens, weights)
+    done, highest = attend_inner(place, outer, inner)
+    mixed = attend_outer(place, peak_in, outer, inner, above, below, done, highest)
     with jax.named_scope("heads"):
         mixed = lax.all_to_all(mixed, GROUP, 0, 0, tiled=True)
     attended = mixed[:, :SET].transpose(1, 0, 2).reshape(1, ROWS, COLS, HEADS * HEAD)

time: 153 us -> 152 us (level)
  waiting for transfers between devices: 43.6 us -> 41.2 us
    ppermute x1, waiting for transfers between devices: 3.33 us -> 0.98 us  [local(): below = lax.ppermute(top, 'y', [(i + 1, i) for i in range(3)])]
    pallas_call x1 -> x2, Pallas kernels: 5.34 us -> 5.61 us  [the longest x1 3.26 us: project_outer(): pl.pallas_call(project_outer_kernel, out_shape=(jax.ShapeDtypeStruct((4,...]
  transfers between devices with their start and end apart: 11 -> 11, of which waited for: 6 -> 6; matrix products, arithmetic and copies ran while one was open for 4% -> 4% of each run, Pallas kernels for 2% -> 4%
where the time goes in v5:
time: 152 us; the launch traced here: 150 us
  starting transfers between devices  49 us (32%)
  waiting for transfers between devices  41.2 us (27%)
  blocking collectives  22.2 us (15%)
  between operations  15.6 us (10%)
  Pallas kernels  11.6 us (8%)
  local copies, waits for them, and re-layouts  6.58 us (4%)
  other arithmetic  4.02 us (3%)
    all_to_all x2, waiting for transfers between devices, spread(): return lax.all_to_all(copies, axis, 0, 0, tiled=True)  27.2 us
    all_to_all x2, starting transfers between devices, spread(): return lax.all_to_all(copies, axis, 0, 0, tiled=True)  24 us
    all_to_all x1, blocking collectives, local(): mixed = lax.all_to_all(mixed, GROUP, 0, 0, tiled=True)  14.9 us
    ppermute x4, starting transfers between devices, shift(): lax.ppermute(value, axis, [(i, (i + step) % size) for i in range(size)])  14.8 us
    ppermute x4, waiting for transfers between devices, shift(): lax.ppermute(value, axis, [(i, (i + step) % size) for i in range(size)])  8.17 us
    all_to_all x1, blocking collectives, spread(): return lax.all_to_all(copies, axis, 0, 0, tiled=True)  7.33 us
    ppermute x1, starting transfers between devices, head_weights(): first = lax.ppermute(mine, AXES, main)  4.59 us
    ppermute x1, waiting for transfers between devices, head_weights(): first = lax.ppermute(mine, AXES, main)  4.2 us
  transfers between devices with their start and end apart: 11, of which 6 were waited for; matrix products, arithmetic and copies ran while one was open for 4% of the time, Pallas kernels for 4%

profile of v5, /device:TPU:1, one launch (start us, length us, event | category | flops | bytes accessed | tf_op | source)
XLA Modules:
  0.0 150.2 jit_solution(314662402012867114)
XLA Ops:
  8.6 4.6 %collective-permute-start = (bf16[6,2048]{1,0:T(8,128)(2,1)}, bf16[6,2048]{1,0:T(8,128)(2,1)S(1)}, u32[]{:S(2)}, u32[]{:S(2)}) collective-permute-start(bf16[6,2048]{1,0:T(8,128)(2,1)} %bitcast.9), channel_id=1, source_target_pairs={{0,0},{1,128},{2,2},{3,130},{4,4},{5,132},{6,6},{7,134},{8,8},{9,1... | collective-permute-start | bytes 73736 | tf_op jit(solution)/shard_map/ppermute | solution.py:252
  13.2 4.2 %collective-permute-done = bf16[6,2048]{1,0:T(8,128)(2,1)S(1)} collective-permute-done((bf16[6,2048]{1,0:T(8,128)(2,1)}, bf16[6,2048]{1,0:T(8,128)(2,1)S(1)}, u32[]{:S(2)}, u32[]{:S(2)}) %collective-permute-start) | collective-permute-done | bytes 24608 | tf_op jit(solution)/shard_map/ppermute | solution.py:252
  18.4 16.4 %all-to-all-start = ((bf16[16,96,128]{2,1,0:T(8,128)(2,1)}), bf16[16,96,128]{2,1,0:T(8,128)(2,1)S(1)}, u32[]{:S(2)}, u32[]{:S(2)}) async-start(bf16[16,96,128]{2,1,0:T(8,128)(2,1)} %broadcast_in_dim.12), calls=%async_computation | async-start | bytes 786432 | tf_op jit(solution)/shard_map/weights_over_z/all_to_all | solution.py:241
  34.7 2.0 %collective-permute-start.2 = (s32[1,2]{1,0:T(1,128)}, s32[1,2]{1,0:T(1,128)S(1)}, u32[]{:S(2)}, u32[]{:S(2)}) collective-permute-start(s32[1,2]{1,0:T(1,128)} %param.7), channel_id=1, source_target_pairs={{0,1},{1,0},{2,3},{3,2},{4,5},{5,4},{6,7},{7,6},{8,9},{9,8},{10,11... | collective-permute-start | bytes 32 | tf_op jit(solution)/shard_map/ppermute | solution.py:246
  37.7 17.3 %all-to-all-done = bf16[16,96,128]{2,1,0:T(8,128)(2,1)S(1)} async-done(((bf16[16,96,128]{2,1,0:T(8,128)(2,1)}), bf16[16,96,128]{2,1,0:T(8,128)(2,1)S(1)}, u32[]{:S(2)}, u32[]{:S(2)}) %all-to-all-start) | async-done | bytes 393248 | tf_op jit(solution)/shard_map/weights_over_z/all_to_all | solution.py:241
  55.2 7.5 %collective-permute-start.5 = (bf16[96,2048]{1,0:T(8,128)(2,1)S(1)}, bf16[96,2048]{1,0:T(8,128)(2,1)S(1)}, u32[]{:S(2)}, u32[]{:S(2)}) collective-permute-start(bf16[96,2048]{1,0:T(8,128)(2,1)S(1)} %reshape.41.w0_ref), channel_id=1, source_target_pairs={{0,256},{128,384},{256,0},{384,128},{1,257},{129,385},{257,1},{385... | collective-permute-start | bytes 1179656 | tf_op jit(solution)/shard_map/weights_over_y/ppermute | solution.py:246
  62.7 2.1 %collective-permute-start.4 = (bf16[96,2048]{1,0:T(8,128)(2,1)S(1)}, bf16[96,2048]{1,0:T(8,128)(2,1)S(1)}, u32[]{:S(2)}, u32[]{:S(2)}) collective-permute-start(bf16[96,2048]{1,0:T(8,128)(2,1)S(1)} %reshape.41.w0_ref), channel_id=1, source_target_pairs={{0,384},{128,0},{256,128},{384,256},{1,385},{129,1},{257,129},{385... | collective-permute-start | bytes 1179656 | tf_op jit(solution)/shard_map/weights_over_y/ppermute | solution.py:246
  64.8 3.2 %collective-permute-start.3 = (bf16[96,2048]{1,0:T(8,128)(2,1)S(1)}, bf16[96,2048]{1,0:T(8,128)(2,1)S(1)}, u32[]{:S(2)}, u32[]{:S(2)}) collective-permute-start(bf16[96,2048]{1,0:T(8,128)(2,1)S(1)} %reshape.41.w0_ref), channel_id=1, source_target_pairs={{0,128},{128,256},{256,384},{384,0},{1,129},{129,257},{257,385},{3... | collective-permute-start | bytes 1179656 | tf_op jit(solution)/shard_map/weights_over_y/ppermute | solution.py:246
  68.9 2.0 %abs_reduce_fusion = bf16[]{:T(256)} fusion(bf16[1,4,64,2048]{3,2,1,0:T(8,128)(2,1)} %param.4), kind=kLoop, calls=%fused_computation | loop fusion | flops 1048575 | bytes 1048578 | tf_op jit(solution)/shard_map/reduce_max | solution.py:273
  71.6 4.8 %collective-permute-done.4.w2_ref = bf16[96,2048]{1,0:T(8,128)(2,1)S(1)} collective-permute-done((bf16[96,2048]{1,0:T(8,128)(2,1)S(1)}, bf16[96,2048]{1,0:T(8,128)(2,1)S(1)}, u32[]{:S(2)}, u32[]{:S(2)}) %collective-permute-start.4) | collective-permute-done | bytes 393248 | tf_op jit(solution)/shard_map/weights_over_y/ppermute | solution.py:246
  76.3 3.4 %collective-permute-done.3.w1_ref = bf16[96,2048]{1,0:T(8,128)(2,1)S(1)} collective-permute-done((bf16[96,2048]{1,0:T(8,128)(2,1)S(1)}, bf16[96,2048]{1,0:T(8,128)(2,1)S(1)}, u32[]{:S(2)}, u32[]{:S(2)}) %collective-permute-start.3) | collective-permute-done | bytes 393248 | tf_op jit(solution)/shard_map/weights_over_y/ppermute | solution.py:246
  79.7 3.4 %copy-done = bf16[8,256,2048]{2,1,0:T(8,128)(2,1)S(1)} copy-done((bf16[8,256,2048]{2,1,0:T(8,128)(2,1)S(1)}, bf16[8,256,2048]{2,1,0:T(8,128)(2,1)}, u32[]{:S(2)}) %copy-start) | copy-done | bytes 8388632
  83.1 3.3 %project_outer.1 = (bf16[4,256,384]{2,1,0:T(8,128)(2,1)S(1)}, bf16[2,192,256]{2,1,0:T(8,128)(2,1)S(1)}, bf16[2,192,256]{2,1,0:T(8,128)(2,1)S(1)}, bf16[384,2048]{1,0:T(8,128)(2,1)S(1)}) custom-call(f32[1]{0:T(128)S(6)} %copy.14.scale_ref, bf16[8,256,2048]{2,1,0:T(8,128)(2,1)S(1)} %copy-done, bf16[96,2048]{1,0:T(8,128)(2,1)S(1)} %reshape.41.w0_ref, ...), custom_call_target="tpu_custom_call" | custom-call | flops 1610612736 | bytes 8388608 | tf_op jit(solution)/shard_map/project_outer/pallas_call | solution.py:96
  86.4 3.7 %collective-permute-start.6 = (bf16[2,192,256]{2,1,0:T(8,128)(2,1)S(1)}, bf16[2,192,256]{2,1,0:T(8,128)(2,1)S(1)}, u32[]{:S(2)}, u32[]{:S(2)}) collective-permute-start(bf16[2,192,256]{2,1,0:T(8,128)(2,1)S(1)} %get-tuple-element.20), channel_id=1, source_target_pairs={{0,128},{128,256},{256,384},{1,129},{129,257},{257,385},{2,130},{1... | collective-permute-start | bytes 589832 | tf_op jit(solution)/shard_map/halo/ppermute | solution.py:279
  90.0 1.3 collective-permute-start.7
  91.3 2.3 %project_inner.1.inner_ref = bf16[4,256,384]{2,1,0:T(8,128)(2,1)S(1)} custom-call(f32[1]{0:T(128)S(6)} %copy.14.scale_ref, bf16[8,256,2048]{2,1,0:T(8,128)(2,1)S(1)} %copy-done, bf16[384,2048]{1,0:T(8,128)(2,1)S(1)} %get-tuple-element.19.w_ref), custom_call_target="tpu_custom_call" | custom-call | flops 1610612736 | bytes 6291456 | tf_op jit(solution)/shard_map/project_inner/pallas_call | solution.py:117
  93.7 2.9 %attend_inner.1 = (bf16[8,256,128]{2,1,0:T(8,128)(2,1)S(1)}, f32[256,128]{1,0:T(8,128)S(1)}) custom-call(s32[5]{0:T(128)S(1)} %pad_add_fusion.place_ref, bf16[4,256,384]{2,1,0:T(8,128)(2,1)S(1)} %get-tuple-element.18.outer_ref, bf16[4,256,384]{2,1,0:T(8,128)(2,1)S(1)} %project_inner.1.inner_ref), custom_call_target="tpu_custom_call" | custom-call | flops 335544320 | bytes 2097152 | tf_op jit(solution)/shard_map/attend_inner/pallas_call | solution.py:204
  96.6 1.0 collective-permute-done.7.below_ref
  97.6 3.1 %attend_outer.1 = bf16[8,272,128]{2,1,0:T(8,128)(2,1)S(1)} custom-call(s32[5]{0:T(128)S(1)} %pad_add_fusion.place_ref, f32[1]{0:T(128)S(6)} %convert.6.peak_ref, bf16[4,256,384]{2,1,0:T(8,128)(2,1)S(1)} %get-tuple-element.18.outer_ref, bf16[4,256,384]{2,1,0:T(8,128)(2,1)S(1)} %project_inner.1.inner_ref, ...), custom_call_target="tpu_custom_call" | custom-call | flops 335544320 | bytes 3145728 | tf_op jit(solution)/shard_map/attend_outer/pallas_call | solution.py:224
  100.7 14.9 %all_to_all.22 = bf16[8,272,128]{2,1,0:T(8,128)(2,1)S(1)} all-to-all(bf16[8,272,128]{2,1,0:T(8,128)(2,1)S(1)} %attend_outer.1), channel_id=1, replica_groups=mesh['y'=4,'x'=4,'z'=16,'core'=2] {'x','core'}, dimensions={0} | all-to-all | bytes 1114112 | tf_op jit(solution)/shard_map/heads/all_to_all | solution.py:285
  116.0 7.3 %all_to_all.23 = f32[4,1,2]{2,1,0:T(1,128)S(1)} all-to-all(f32[4,1,2]{2,1,0:T(1,128)S(1)} %broadcast_in_dim.24), channel_id=1, replica_groups=mesh['y'=4,'x'=4,'z'=16,'core'=2] {'y'}, dimensions={0} | all-to-all | bytes 64 | tf_op jit(solution)/shard_map/peaks/all_to_all | solution.py:241
  123.9 7.6 %all-to-all-start.3 = ((f32[16,1,2]{2,1,0:T(1,128)}), f32[16,1,2]{2,1,0:T(1,128)S(1)}, u32[]{:S(2)}, u32[]{:S(2)}) async-start(f32[16,1,2]{2,1,0:T(1,128)} %broadcast_in_dim.25), calls=%async_computation.3 | async-start | bytes 16384 | tf_op jit(solution)/shard_map/peaks/all_to_all | solution.py:241
  131.9 1.0 reshape.45
  132.9 9.9 %all-to-all-done.3 = f32[16,1,2]{2,1,0:T(1,128)S(1)} async-done(((f32[16,1,2]{2,1,0:T(1,128)}), f32[16,1,2]{2,1,0:T(1,128)S(1)}, u32[]{:S(2)}, u32[]{:S(2)}) %all-to-all-start.3) | async-done | bytes 160 | tf_op jit(solution)/shard_map/peaks/all_to_all | solution.py:241
  (31 shorter events, 5.6 us)
Async XLA Ops:
  7.2 72.6 %all-gather.2.cloned.1.call-start = ((), (), s32[]{:S(2)}) async-start(), calls=%async_computation.4 | async-start | bytes 9437184 | tf_op jit(solution)/shard_map/tokens/all_gather | solution.py:268
  7.9 5.3 %collective-permute-start.1 = (bf16[6,2048]{1,0:T(8,128)(2,1)}, bf16[6,2048]{1,0:T(8,128)(2,1)S(1)}, u32[]{:S(2)}, u32[]{:S(2)}) collective-permute-start(bf16[6,2048]{1,0:T(8,128)(2,1)} %bitcast.8), channel_id=1, source_target_pairs={{21,149},{42,298},{85,212},{106,331},{149,245},{170,266},{213,180}... | collective-permute-start | bytes 73736 | tf_op jit(solution)/shard_map/ppermute | solution.py:253
  8.6 8.9 %collective-permute-start = (bf16[6,2048]{1,0:T(8,128)(2,1)}, bf16[6,2048]{1,0:T(8,128)(2,1)S(1)}, u32[]{:S(2)}, u32[]{:S(2)}) collective-permute-start(bf16[6,2048]{1,0:T(8,128)(2,1)} %bitcast.9), channel_id=1, source_target_pairs={{0,0},{1,128},{2,2},{3,130},{4,4},{5,132},{6,6},{7,134},{8,8},{9,1... | collective-permute-start | bytes 73736 | tf_op jit(solution)/shard_map/ppermute | solution.py:252
  18.4 36.7 %all-to-all-start = ((bf16[16,96,128]{2,1,0:T(8,128)(2,1)}), bf16[16,96,128]{2,1,0:T(8,128)(2,1)S(1)}, u32[]{:S(2)}, u32[]{:S(2)}) async-start(bf16[16,96,128]{2,1,0:T(8,128)(2,1)} %broadcast_in_dim.12), calls=%async_computation | async-start | bytes 786432 | tf_op jit(solution)/shard_map/weights_over_z/all_to_all | solution.py:241
  34.7 33.3 %collective-permute-start.2 = (s32[1,2]{1,0:T(1,128)}, s32[1,2]{1,0:T(1,128)S(1)}, u32[]{:S(2)}, u32[]{:S(2)}) collective-permute-start(s32[1,2]{1,0:T(1,128)} %param.7), channel_id=1, source_target_pairs={{0,1},{1,0},{2,3},{3,2},{4,5},{5,4},{6,7},{7,6},{8,9},{9,8},{10,11... | collective-permute-start | bytes 32 | tf_op jit(solution)/shard_map/ppermute | solution.py:246
  55.2 16.4 %collective-permute-start.5 = (bf16[96,2048]{1,0:T(8,128)(2,1)S(1)}, bf16[96,2048]{1,0:T(8,128)(2,1)S(1)}, u32[]{:S(2)}, u32[]{:S(2)}) collective-permute-start(bf16[96,2048]{1,0:T(8,128)(2,1)S(1)} %reshape.41.w0_ref), channel_id=1, source_target_pairs={{0,256},{128,384},{256,0},{384,128},{1,257},{129,385},{257,1},{385... | collective-permute-start | bytes 1179656 | tf_op jit(solution)/shard_map/weights_over_y/ppermute | solution.py:246
  62.7 13.6 %collective-permute-start.4 = (bf16[96,2048]{1,0:T(8,128)(2,1)S(1)}, bf16[96,2048]{1,0:T(8,128)(2,1)S(1)}, u32[]{:S(2)}, u32[]{:S(2)}) collective-permute-start(bf16[96,2048]{1,0:T(8,128)(2,1)S(1)} %reshape.41.w0_ref), channel_id=1, source_target_pairs={{0,384},{128,0},{256,128},{384,256},{1,385},{129,1},{257,129},{385... | collective-permute-start | bytes 1179656 | tf_op jit(solution)/shard_map/weights_over_y/ppermute | solution.py:246
  64.8 14.9 %collective-permute-start.3 = (bf16[96,2048]{1,0:T(8,128)(2,1)S(1)}, bf16[96,2048]{1,0:T(8,128)(2,1)S(1)}, u32[]{:S(2)}, u32[]{:S(2)}) collective-permute-start(bf16[96,2048]{1,0:T(8,128)(2,1)S(1)} %reshape.41.w0_ref), channel_id=1, source_target_pairs={{0,128},{128,256},{256,384},{384,0},{1,129},{129,257},{257,385},{3... | collective-permute-start | bytes 1179656 | tf_op jit(solution)/shard_map/weights_over_y/ppermute | solution.py:246
  79.7 3.4 %copy-start = (bf16[8,256,2048]{2,1,0:T(8,128)(2,1)S(1)}, bf16[8,256,2048]{2,1,0:T(8,128)(2,1)}, u32[]{:S(2)}) copy-start(bf16[8,256,2048]{2,1,0:T(8,128)(2,1)} %all-gather.2.cloned.1.call-done.x_ref) | copy-start | bytes 25165828
  86.4 10.3 %collective-permute-start.6 = (bf16[2,192,256]{2,1,0:T(8,128)(2,1)S(1)}, bf16[2,192,256]{2,1,0:T(8,128)(2,1)S(1)}, u32[]{:S(2)}, u32[]{:S(2)}) collective-permute-start(bf16[2,192,256]{2,1,0:T(8,128)(2,1)S(1)} %get-tuple-element.20), channel_id=1, source_target_pairs={{0,128},{128,256},{256,384},{1,129},{129,257},{257,385},{2,130},{1... | collective-permute-start | bytes 589832 | tf_op jit(solution)/shard_map/halo/ppermute | solution.py:279
  90.0 7.6 %collective-permute-start.7 = (bf16[2,192,256]{2,1,0:T(8,128)(2,1)S(1)}, bf16[2,192,256]{2,1,0:T(8,128)(2,1)S(1)}, u32[]{:S(2)}, u32[]{:S(2)}) collective-permute-start(bf16[2,192,256]{2,1,0:T(8,128)(2,1)S(1)} %get-tuple-element.21), channel_id=1, source_target_pairs={{128,0},{256,128},{384,256},{129,1},{257,129},{385,257},{130,2},{2... | collective-permute-start | bytes 589832 | tf_op jit(solution)/shard_map/halo/ppermute | solution.py:280
  123.9 18.9 %all-to-all-start.3 = ((f32[16,1,2]{2,1,0:T(1,128)}), f32[16,1,2]{2,1,0:T(1,128)S(1)}, u32[]{:S(2)}, u32[]{:S(2)}) async-start(f32[16,1,2]{2,1,0:T(1,128)} %broadcast_in_dim.25), calls=%async_computation.3 | async-start | bytes 16384 | tf_op jit(solution)/shard_map/peaks/all_to_all | solution.py:241
Sparse Core Ops, SparseCore 0:
  10.1 63.0 all-gather.1

commit v6 on v5

--- a/solution.py
+++ b/solution.py
@@ -61,11 +61,11 @@
     return (place * 96 + z * 6 + j == r).astype(jnp.bfloat16)
 
 
-def project_rows(scale_ref, x_ref, w_scr, qkv_ref, parts):
+def project_rows(scale_ref, x_refs, w_scr, qkv_ref):
     scale = scale_ref[0]
     inverse = 1.0 / scale
-    for place, part in enumerate(parts):
-        tokens = x_ref[2 * part : 2 * part + 2].reshape(2 * SET, D)
+    for place, x_ref in enumerate(x_refs):
+        tokens = x_ref[...].reshape(2 * SET, D)
         tokens = (tokens.astype(jnp.float32) * inverse).astype(jnp.bfloat16)
         tokens = jnp.clip(tokens, -FP_TOP, FP_TOP)
         out = lax.dot_general(
@@ -75,19 +75,19 @@
         qkv_ref[2 * place : 2 * place + 2] = out
 
 
-def project_outer_kernel(scale_ref, x_ref, w0_ref, w1_ref, w2_ref, w3_ref, order_ref, qkv_ref, top_ref, bottom_ref, w_ref, w_cat):
+def project_outer_kernel(scale_ref, x0_ref, x3_ref, w0_ref, w1_ref, w2_ref, w3_ref, order_ref, qkv_ref, top_ref, bottom_ref, w_ref, w_cat):
     for part, ref in enumerate((w0_ref, w1_ref, w2_ref, w3_ref)):
         w_cat[96 * part : 96 * (part + 1)] = ref[...]
     w_ref[...] = lax.dot_general(
         order_ref[...], w_cat[...], (((0,), (0,)), ((), ())), preferred_element_type=jnp.float32
     ).astype(jnp.bfloat16)
-    project_rows(scale_ref, x_ref, w_ref, qkv_ref, OUTER)
+    project_rows(scale_ref, (x0_ref, x3_ref), w_ref, qkv_ref)
     top_ref[...] = qkv_ref[:2, : HALO * COLS, HEAD:]
     bottom_ref[...] = qkv_ref[2:, SET - HALO * COLS :, HEAD:]
 
 
-def project_inner_kernel(scale_ref, x_ref, w_ref, qkv_ref):
-    project_rows(scale_ref, x_ref, w_ref, qkv_ref, INNER)
+def project_inner_kernel(scale_ref, x1_ref, x2_ref, w_ref, qkv_ref):
+    project_rows(scale_ref, (x1_ref, x2_ref), w_ref, qkv_ref)
 
 
 def project_outer(scale, tokens, weights, order):
@@ -101,7 +101,7 @@
             halo,
             jax.ShapeDtypeStruct((3 * HEAD, D), jnp.bfloat16),
         ),
-        in_specs=[pl.BlockSpec(memory_space=pltpu.SMEM)] + [vmem] * 6,
+        in_specs=[pl.BlockSpec(memory_space=pltpu.SMEM)] + [vmem] * 7,
         out_specs=(vmem,) * 4,
         scratch_shapes=[pltpu.VMEM((3 * HEAD, D), jnp.bfloat16)],
         compiler_params=pltpu.CompilerParams(vmem_limit_bytes=24 * 2**20),
@@ -109,7 +109,7 @@
             flops=2 * 4 * SET * D * 3 * HEAD, bytes_accessed=8 * 2**20, transcendentals=0
         ),
         name="project_outer",
-    )(scale, tokens, *weights, order)
+    )(scale, *tokens, *weights, order)
 
 
 def project_inner(scale, tokens, weights):
@@ -117,14 +117,14 @@
     return pl.pallas_call(
         project_inner_kernel,
         out_shape=jax.ShapeDtypeStruct((4, SET, 3 * HEAD), jnp.bfloat16),
-        in_specs=[pl.BlockSpec(memory_space=pltpu.SMEM), vmem, vmem],
+        in_specs=[pl.BlockSpec(memory_space=pltpu.SMEM), vmem, vmem, vmem],
         out_specs=vmem,
         compiler_params=pltpu.CompilerParams(vmem_limit_bytes=24 * 2**20),
         cost_estimate=pl.CostEstimate(
             flops=2 * 4 * SET * D * 3 * HEAD, bytes_accessed=6 * 2**20, transcendentals=0
         ),
         name="project_inner",
-    )(scale, tokens, weights)
+    )(scale, *tokens, weights)
 
 
 def tile_column(outer_ref, inner_ref, part, image):
@@ -266,6 +266,7 @@
 def local(images, w_qkv, prev_scale, extent):
     with jax.named_scope("tokens"):
         tokens = lax.all_gather(images.reshape(SET, D), GROUP, axis=0, tiled=False)
+    tokens = [tokens[2 * part : 2 * part + 2] for part in range(4)]
     weights, late = head_weights(w_qkv, images)
     core = lax.axis_index("core")
     order = column_order(2 * lax.axis_index("x") + core, lax.axis_index("y"))
@@ -274,11 +275,11 @@
     extents = jnp.where(core == 0, jnp.concatenate([extent, other]), jnp.concatenate([other, extent]))
     place = jnp.stack([lax.axis_index("y") * BLOCK, *extents.reshape(4)]).astype(jnp.int32)
     order, peak_in, place = lax.optimization_barrier((order, peak_in, place))
-    outer, top, bottom, weights = project_outer(prev_scale, tokens, weights, order)
+    outer, top, bottom, weights = project_outer(prev_scale, [tokens[part] for part in OUTER], weights, order)
     with jax.named_scope("halo"):
         above = lax.ppermute(bottom, "y", [(i, i + 1) for i in range(3)])
         below = lax.ppermute(top, "y", [(i + 1, i) for i in range(3)])
-    inner = project_inner(prev_scale, tokens, weights)
+    inner = project_inner(prev_scale, [tokens[part] for part in INNER], weights)
     done, highest = attend_inner(place, outer, inner)
     mixed = attend_outer(place, peak_in, outer, inner, above, below, done, highest)
     with jax.named_scope("heads"):

time: 152 us -> 150 us (0.987)
  waiting for transfers between devices: 41.2 us -> 39.1 us
  other arithmetic: 4.02 us -> 2.06 us
  starting transfers between devices: 49 us -> 50.6 us
    ppermute x4, waiting for transfers between devices: 8.17 us -> 2.46 us  [shift(): lax.ppermute(value, axis, [(i, (i + step) % size) for i in range(size)])]
    slice x0 -> x1, local copies, waits for them, and re-layouts: none -> 4 us  [local(): tokens = [tokens[2 * part:2 * part + 2] for part in range(4)]]
    all_gather x1, waiting for transfers between devices: 0.01 us -> 3.85 us  [local(): tokens = lax.all_gather(images.reshape(SET, D), GROUP, axis=0, tiled=False)]
    unnamed x2 -> x4, local copies, waits for them, and re-layouts: 3.38 us -> 0.01 us
    all_to_all x2, starting transfers between devices: 24 us -> 25.6 us  [spread(): return lax.all_to_all(copies, axis, 0, 0, tiled=True)]
  transfers between devices with their start and end apart: 11 -> 11, of which waited for: 6 -> 6; matrix products, arithmetic and copies ran while one was open for 4% -> 5% of each run, Pallas kernels for 4% -> 4%
where the time goes in v6:
time: 150 us; the launch traced here: 148 us
  starting transfers between devices  50.6 us (34%)
  waiting for transfers between devices  39.1 us (26%)
  blocking collectives  22.3 us (15%)
  between operations  15.6 us (10%)
  Pallas kernels  11.6 us (8%)
  local copies, waits for them, and re-layouts  7.2 us (5%)
  other arithmetic  2.06 us (1%)
    all_to_all x2, waiting for transfers between devices, spread(): return lax.all_to_all(copies, axis, 0, 0, tiled=True)  27 us
    all_to_all x2, starting transfers between devices, spread(): return lax.all_to_all(copies, axis, 0, 0, tiled=True)  25.6 us
    all_to_all x1, blocking collectives, local(): mixed = lax.all_to_all(mixed, GROUP, 0, 0, tiled=True)  14.9 us
    ppermute x4, starting transfers between devices, shift(): lax.ppermute(value, axis, [(i, (i + step) % size) for i in range(size)])  14.8 us
    all_to_all x1, blocking collectives, spread(): return lax.all_to_all(copies, axis, 0, 0, tiled=True)  7.34 us
    ppermute x1, starting transfers between devices, head_weights(): first = lax.ppermute(mine, AXES, main)  4.59 us
    ppermute x1, waiting for transfers between devices, head_weights(): first = lax.ppermute(mine, AXES, main)  4.2 us
    slice x1, local copies, waits for them, and re-layouts, local(): tokens = [tokens[2 * part:2 * part + 2] for part in range(4)]  4 us
  transfers between devices with their start and end apart: 11, of which 6 were waited for; matrix products, arithmetic and copies ran while one was open for 5% of the time, Pallas kernels for 4%

profile of v6, /device:TPU:1, one launch (start us, length us, event | category | flops | bytes accessed | tf_op | source)
XLA Modules:
  0.0 148.5 jit_solution(7782724217881665173)
XLA Ops:
  8.6 4.6 %collective-permute-start = (bf16[6,2048]{1,0:T(8,128)(2,1)}, bf16[6,2048]{1,0:T(8,128)(2,1)S(1)}, u32[]{:S(2)}, u32[]{:S(2)}) collective-permute-start(bf16[6,2048]{1,0:T(8,128)(2,1)} %bitcast.9), channel_id=1, source_target_pairs={{0,0},{1,128},{2,2},{3,130},{4,4},{5,132},{6,6},{7,134},{8,8},{9,1... | collective-permute-start | bytes 73736 | tf_op jit(solution)/shard_map/ppermute | solution.py:252
  13.2 4.2 %collective-permute-done = bf16[6,2048]{1,0:T(8,128)(2,1)S(1)} collective-permute-done((bf16[6,2048]{1,0:T(8,128)(2,1)}, bf16[6,2048]{1,0:T(8,128)(2,1)S(1)}, u32[]{:S(2)}, u32[]{:S(2)}) %collective-permute-start) | collective-permute-done | bytes 24608 | tf_op jit(solution)/shard_map/ppermute | solution.py:252
  17.6 0.8 broadcast_in_dim.12
  18.4 16.4 %all-to-all-start = ((bf16[16,96,128]{2,1,0:T(8,128)(2,1)}), bf16[16,96,128]{2,1,0:T(8,128)(2,1)S(1)}, u32[]{:S(2)}, u32[]{:S(2)}) async-start(bf16[16,96,128]{2,1,0:T(8,128)(2,1)} %broadcast_in_dim.12), calls=%async_computation | async-start | bytes 786432 | tf_op jit(solution)/shard_map/weights_over_z/all_to_all | solution.py:241
  34.8 2.0 %collective-permute-start.2 = (s32[1,2]{1,0:T(1,128)S(1)}, s32[1,2]{1,0:T(1,128)S(1)}, u32[]{:S(2)}, u32[]{:S(2)}) collective-permute-start(s32[1,2]{1,0:T(1,128)S(1)} %copy-done.1), channel_id=1, source_target_pairs={{0,1},{1,0},{2,3},{3,2},{4,5},{5,4},{6,7},{7,6},{8,9},{9,8},{10,11... | collective-permute-start | bytes 32 | tf_op jit(solution)/shard_map/ppermute | solution.py:246
  38.0 17.1 %all-to-all-done = bf16[16,96,128]{2,1,0:T(8,128)(2,1)S(1)} async-done(((bf16[16,96,128]{2,1,0:T(8,128)(2,1)}), bf16[16,96,128]{2,1,0:T(8,128)(2,1)S(1)}, u32[]{:S(2)}, u32[]{:S(2)}) %all-to-all-start) | async-done | bytes 393248 | tf_op jit(solution)/shard_map/weights_over_z/all_to_all | solution.py:241
  55.2 7.5 %collective-permute-start.5 = (bf16[96,2048]{1,0:T(8,128)(2,1)S(1)}, bf16[96,2048]{1,0:T(8,128)(2,1)S(1)}, u32[]{:S(2)}, u32[]{:S(2)}) collective-permute-start(bf16[96,2048]{1,0:T(8,128)(2,1)S(1)} %reshape.41.w0_ref), channel_id=1, source_target_pairs={{0,256},{128,384},{256,0},{384,128},{1,257},{129,385},{257,1},{385... | collective-permute-start | bytes 1179656 | tf_op jit(solution)/shard_map/weights_over_y/ppermute | solution.py:246
  62.7 2.1 %collective-permute-start.4 = (bf16[96,2048]{1,0:T(8,128)(2,1)S(1)}, bf16[96,2048]{1,0:T(8,128)(2,1)S(1)}, u32[]{:S(2)}, u32[]{:S(2)}) collective-permute-start(bf16[96,2048]{1,0:T(8,128)(2,1)S(1)} %reshape.41.w0_ref), channel_id=1, source_target_pairs={{0,384},{128,0},{256,128},{384,256},{1,385},{129,1},{257,129},{385... | collective-permute-start | bytes 1179656 | tf_op jit(solution)/shard_map/weights_over_y/ppermute | solution.py:246
  64.8 3.2 %collective-permute-start.3 = (bf16[96,2048]{1,0:T(8,128)(2,1)S(1)}, bf16[96,2048]{1,0:T(8,128)(2,1)S(1)}, u32[]{:S(2)}, u32[]{:S(2)}) collective-permute-start(bf16[96,2048]{1,0:T(8,128)(2,1)S(1)} %reshape.41.w0_ref), channel_id=1, source_target_pairs={{0,128},{128,256},{256,384},{384,0},{1,129},{129,257},{257,385},{3... | collective-permute-start | bytes 1179656 | tf_op jit(solution)/shard_map/weights_over_y/ppermute | solution.py:246
  69.4 3.9 %all-gather.2.cloned.1.call-done = bf16[8,256,2048]{2,1,0:T(8,128)(2,1)} async-done(((bf16[1,256,2048]{2,1,0:T(8,128)(2,1)}), bf16[8,256,2048]{2,1,0:T(8,128)(2,1)}) %all-gather.2.cloned.1.call-update) | async-done | bytes 8388624 | tf_op jit(solution)/shard_map/tokens/all_gather | solution.py:268
  73.3 4.0 %fusion.24 = (bf16[2,256,2048]{2,1,0:T(8,128)(2,1)S(1)}, bf16[2,256,2048]{2,1,0:T(8,128)(2,1)S(1)}, bf16[2,256,2048]{2,1,0:T(8,128)(2,1)S(1)}, bf16[2,256,2048]{2,1,0:T(8,128)(2,1)S(1)}) fusion(bf16[8,256,2048]{2,1,0:T(8,128)(2,1)} %all-gather.2.cloned.1.call-done), kind=kLoop, calls=%fused_computation.54 | loop fusion | bytes 16777216 | tf_op jit(solution)/shard_map/slice | solution.py:269
  77.3 2.4 %collective-permute-done.3.w1_ref = bf16[96,2048]{1,0:T(8,128)(2,1)S(1)} collective-permute-done((bf16[96,2048]{1,0:T(8,128)(2,1)S(1)}, bf16[96,2048]{1,0:T(8,128)(2,1)S(1)}, u32[]{:S(2)}, u32[]{:S(2)}) %collective-permute-start.3) | collective-permute-done | bytes 393248 | tf_op jit(solution)/shard_map/weights_over_y/ppermute | solution.py:246
  79.7 3.3 %project_outer.1 = (bf16[4,256,384]{2,1,0:T(8,128)(2,1)S(1)}, bf16[2,192,256]{2,1,0:T(8,128)(2,1)S(1)}, bf16[2,192,256]{2,1,0:T(8,128)(2,1)S(1)}, bf16[384,2048]{1,0:T(8,128)(2,1)S(1)}) custom-call(f32[1]{0:T(128)S(6)} %copy.14.scale_ref, bf16[2,256,2048]{2,1,0:T(8,128)(2,1)S(1)} %get-tuple-element.27.x0_ref, ...), custom_call_target="tpu_custom_call" | custom-call | flops 1610612736 | bytes 8388608 | tf_op jit(solution)/shard_map/project_outer/pallas_call | solution.py:96
  83.0 3.7 %collective-permute-start.6 = (bf16[2,192,256]{2,1,0:T(8,128)(2,1)S(1)}, bf16[2,192,256]{2,1,0:T(8,128)(2,1)S(1)}, u32[]{:S(2)}, u32[]{:S(2)}) collective-permute-start(bf16[2,192,256]{2,1,0:T(8,128)(2,1)S(1)} %get-tuple-element.20), channel_id=1, source_target_pairs={{0,128},{128,256},{256,384},{1,129},{129,257},{257,385},{2,130},{1... | collective-permute-start | bytes 589832 | tf_op jit(solution)/shard_map/halo/ppermute | solution.py:280
  86.7 1.3 collective-permute-start.7
  88.0 2.3 %project_inner.1.inner_ref = bf16[4,256,384]{2,1,0:T(8,128)(2,1)S(1)} custom-call(f32[1]{0:T(128)S(6)} %copy.14.scale_ref, bf16[2,256,2048]{2,1,0:T(8,128)(2,1)S(1)} %get-tuple-element.25.x1_ref, bf16[2,256,2048]{2,1,0:T(8,128)(2,1)S(1)} %get-tuple-element.24.x2_ref, bf16[384,2048]{1,0:T(8,128)(2,1)S(1)} %get-tuple-element.19.w_ref), custom_call_target="tpu_custom_call" | custom-call | flops 1610612736 | bytes 6291456 | tf_op jit(solution)/shard_map/project_inner/pallas_call | solution.py:117
  90.3 2.9 %attend_inner.1 = (bf16[8,256,128]{2,1,0:T(8,128)(2,1)S(1)}, f32[256,128]{1,0:T(8,128)S(1)}) custom-call(s32[5]{0:T(128)S(1)} %pad_add_fusion.place_ref, bf16[4,256,384]{2,1,0:T(8,128)(2,1)S(1)} %get-tuple-element.18.outer_ref, bf16[4,256,384]{2,1,0:T(8,128)(2,1)S(1)} %project_inner.1.inner_ref), custom_call_target="tpu_custom_call" | custom-call | flops 335544320 | bytes 2097152 | tf_op jit(solution)/shard_map/attend_inner/pallas_call | solution.py:204
  93.3 1.0 collective-permute-done.7.below_ref
  94.2 3.1 %attend_outer.1 = bf16[8,272,128]{2,1,0:T(8,128)(2,1)S(1)} custom-call(s32[5]{0:T(128)S(1)} %pad_add_fusion.place_ref, f32[1]{0:T(128)S(6)} %convert.6.peak_ref, bf16[4,256,384]{2,1,0:T(8,128)(2,1)S(1)} %get-tuple-element.18.outer_ref, bf16[4,256,384]{2,1,0:T(8,128)(2,1)S(1)} %project_inner.1.inner_ref, ...), custom_call_target="tpu_custom_call" | custom-call | flops 335544320 | bytes 3145728 | tf_op jit(solution)/shard_map/attend_outer/pallas_call | solution.py:224
  97.3 14.9 %all_to_all.22 = bf16[8,272,128]{2,1,0:T(8,128)(2,1)S(1)} all-to-all(bf16[8,272,128]{2,1,0:T(8,128)(2,1)S(1)} %attend_outer.1), channel_id=1, replica_groups=mesh['y'=4,'x'=4,'z'=16,'core'=2] {'x','core'}, dimensions={0} | all-to-all | bytes 1114112 | tf_op jit(solution)/shard_map/heads/all_to_all | solution.py:286
  112.6 7.3 %all_to_all.23 = f32[4,1,2]{2,1,0:T(1,128)S(1)} all-to-all(f32[4,1,2]{2,1,0:T(1,128)S(1)} %broadcast_in_dim.24), channel_id=1, replica_groups=mesh['y'=4,'x'=4,'z'=16,'core'=2] {'y'}, dimensions={0} | all-to-all | bytes 64 | tf_op jit(solution)/shard_map/peaks/all_to_all | solution.py:241
  120.5 9.2 %all-to-all-start.3 = ((f32[16,1,2]{2,1,0:T(1,128)}), f32[16,1,2]{2,1,0:T(1,128)S(1)}, u32[]{:S(2)}, u32[]{:S(2)}) async-start(f32[16,1,2]{2,1,0:T(1,128)} %broadcast_in_dim.25), calls=%async_computation.3 | async-start | bytes 16384 | tf_op jit(solution)/shard_map/peaks/all_to_all | solution.py:241
  130.2 1.0 reshape.45
  131.2 9.9 %all-to-all-done.3 = f32[16,1,2]{2,1,0:T(1,128)S(1)} async-done(((f32[16,1,2]{2,1,0:T(1,128)}), f32[16,1,2]{2,1,0:T(1,128)S(1)}, u32[]{:S(2)}, u32[]{:S(2)}) %all-to-all-start.3) | async-done | bytes 160 | tf_op jit(solution)/shard_map/peaks/all_to_all | solution.py:241
  (34 shorter events, 4.9 us)
Async XLA Ops:
  7.2 60.9 %copy-start = (bf16[1,4,64,2048]{3,2,1,0:T(8,128)(2,1)S(1)}, bf16[1,4,64,2048]{3,2,1,0:T(8,128)(2,1)}, u32[]{:S(2)}) copy-start(bf16[1,4,64,2048]{3,2,1,0:T(8,128)(2,1)} %param.4) | copy-start | bytes 3145732
  7.2 27.6 %copy-start.1 = (s32[1,2]{1,0:T(1,128)S(1)}, s32[1,2]{1,0:T(1,128)}, u32[]{:S(2)}) copy-start(s32[1,2]{1,0:T(1,128)} %param.7) | copy-start | bytes 28
  7.2 66.1 %all-gather.2.cloned.1.call-start = ((), (), s32[]{:S(2)}) async-start(), calls=%async_computation.4 | async-start | bytes 9437184 | tf_op jit(solution)/shard_map/tokens/all_gather | solution.py:268
  7.9 5.3 %collective-permute-start.1 = (bf16[6,2048]{1,0:T(8,128)(2,1)}, bf16[6,2048]{1,0:T(8,128)(2,1)S(1)}, u32[]{:S(2)}, u32[]{:S(2)}) collective-permute-start(bf16[6,2048]{1,0:T(8,128)(2,1)} %bitcast.8), channel_id=1, source_target_pairs={{21,149},{42,298},{85,212},{106,331},{149,245},{170,266},{213,180}... | collective-permute-start | bytes 73736 | tf_op jit(solution)/shard_map/ppermute | solution.py:253
  8.6 8.9 %collective-permute-start = (bf16[6,2048]{1,0:T(8,128)(2,1)}, bf16[6,2048]{1,0:T(8,128)(2,1)S(1)}, u32[]{:S(2)}, u32[]{:S(2)}) collective-permute-start(bf16[6,2048]{1,0:T(8,128)(2,1)} %bitcast.9), channel_id=1, source_target_pairs={{0,0},{1,128},{2,2},{3,130},{4,4},{5,132},{6,6},{7,134},{8,8},{9,1... | collective-permute-start | bytes 73736 | tf_op jit(solution)/shard_map/ppermute | solution.py:252
  18.4 36.7 %all-to-all-start = ((bf16[16,96,128]{2,1,0:T(8,128)(2,1)}), bf16[16,96,128]{2,1,0:T(8,128)(2,1)S(1)}, u32[]{:S(2)}, u32[]{:S(2)}) async-start(bf16[16,96,128]{2,1,0:T(8,128)(2,1)} %broadcast_in_dim.12), calls=%async_computation | async-start | bytes 786432 | tf_op jit(solution)/shard_map/weights_over_z/all_to_all | solution.py:241
  34.8 3.0 %collective-permute-start.2 = (s32[1,2]{1,0:T(1,128)S(1)}, s32[1,2]{1,0:T(1,128)S(1)}, u32[]{:S(2)}, u32[]{:S(2)}) collective-permute-start(s32[1,2]{1,0:T(1,128)S(1)} %copy-done.1), channel_id=1, source_target_pairs={{0,1},{1,0},{2,3},{3,2},{4,5},{5,4},{6,7},{7,6},{8,9},{9,8},{10,11... | collective-permute-start | bytes 32 | tf_op jit(solution)/shard_map/ppermute | solution.py:246
  55.2 22.1 %collective-permute-start.5 = (bf16[96,2048]{1,0:T(8,128)(2,1)S(1)}, bf16[96,2048]{1,0:T(8,128)(2,1)S(1)}, u32[]{:S(2)}, u32[]{:S(2)}) collective-permute-start(bf16[96,2048]{1,0:T(8,128)(2,1)S(1)} %reshape.41.w0_ref), channel_id=1, source_target_pairs={{0,256},{128,384},{256,0},{384,128},{1,257},{129,385},{257,1},{385... | collective-permute-start | bytes 1179656 | tf_op jit(solution)/shard_map/weights_over_y/ppermute | solution.py:246
  62.7 14.6 %collective-permute-start.4 = (bf16[96,2048]{1,0:T(8,128)(2,1)S(1)}, bf16[96,2048]{1,0:T(8,128)(2,1)S(1)}, u32[]{:S(2)}, u32[]{:S(2)}) collective-permute-start(bf16[96,2048]{1,0:T(8,128)(2,1)S(1)} %reshape.41.w0_ref), channel_id=1, source_target_pairs={{0,384},{128,0},{256,128},{384,256},{1,385},{129,1},{257,129},{385... | collective-permute-start | bytes 1179656 | tf_op jit(solution)/shard_map/weights_over_y/ppermute | solution.py:246
  64.8 14.9 %collective-permute-start.3 = (bf16[96,2048]{1,0:T(8,128)(2,1)S(1)}, bf16[96,2048]{1,0:T(8,128)(2,1)S(1)}, u32[]{:S(2)}, u32[]{:S(2)}) collective-permute-start(bf16[96,2048]{1,0:T(8,128)(2,1)S(1)} %reshape.41.w0_ref), channel_id=1, source_target_pairs={{0,128},{128,256},{256,384},{384,0},{1,129},{129,257},{257,385},{3... | collective-permute-start | bytes 1179656 | tf_op jit(solution)/shard_map/weights_over_y/ppermute | solution.py:246
  83.0 10.2 %collective-permute-start.6 = (bf16[2,192,256]{2,1,0:T(8,128)(2,1)S(1)}, bf16[2,192,256]{2,1,0:T(8,128)(2,1)S(1)}, u32[]{:S(2)}, u32[]{:S(2)}) collective-permute-start(bf16[2,192,256]{2,1,0:T(8,128)(2,1)S(1)} %get-tuple-element.20), channel_id=1, source_target_pairs={{0,128},{128,256},{256,384},{1,129},{129,257},{257,385},{2,130},{1... | collective-permute-start | bytes 589832 | tf_op jit(solution)/shard_map/halo/ppermute | solution.py:280
  86.7 7.6 %collective-permute-start.7 = (bf16[2,192,256]{2,1,0:T(8,128)(2,1)S(1)}, bf16[2,192,256]{2,1,0:T(8,128)(2,1)S(1)}, u32[]{:S(2)}, u32[]{:S(2)}) collective-permute-start(bf16[2,192,256]{2,1,0:T(8,128)(2,1)S(1)} %get-tuple-element.21), channel_id=1, source_target_pairs={{128,0},{256,128},{384,256},{129,1},{257,129},{385,257},{130,2},{2... | collective-permute-start | bytes 589832 | tf_op jit(solution)/shard_map/halo/ppermute | solution.py:281
  120.5 20.5 %all-to-all-start.3 = ((f32[16,1,2]{2,1,0:T(1,128)}), f32[16,1,2]{2,1,0:T(1,128)S(1)}, u32[]{:S(2)}, u32[]{:S(2)}) async-start(f32[16,1,2]{2,1,0:T(1,128)} %broadcast_in_dim.25), calls=%async_computation.3 | async-start | bytes 16384 | tf_op jit(solution)/shard_map/peaks/all_to_all | solution.py:241
Sparse Core Ops, SparseCore 0:
  10.2 63.0 all-gather.1

commit v7 on v6

--- a/solution.py
+++ b/solution.py
@@ -146,26 +146,28 @@
     key_at = lax.broadcasted_iota(jnp.int32, (1, KEYS), 1)
     query_at = lax.broadcasted_iota(jnp.int32, (SET, 1), 0)
     highest = jnp.zeros((SET, HEAD), jnp.float32)
-    for image in range(2):
-        ext_rows, ext_cols = place_ref[1 + 2 * image], place_ref[2 + 2 * image]
-        for unit in units:
+    for unit in units:
+        start = unit * SET
+        scores, weights = [], []
+        for image in range(2):
             query = tile_column(outer_ref, inner_ref, unit, image)[:, :HEAD]
-            start = unit * SET
             keys = kv[image, start : start + KEYS, :HEAD]
-            values = kv[image, start : start + KEYS, HEAD:]
-            scores = lax.dot_general(
-                query, keys, (((1,), (1,)), ((), ())), preferred_element_type=jnp.float32
+            scores.append(
+                lax.dot_general(query, keys, (((1,), (1,)), ((), ())), preferred_element_type=jnp.float32)
             )
+        for image in range(2):
+            ext_rows, ext_cols = place_ref[1 + 2 * image], place_ref[2 + 2 * image]
             key_rows = base + (ROWS * unit - HALO) + key_at // COLS
             key_cols = key_at % COLS
             valid = (key_rows >= 0) & (key_rows < ext_rows) & (key_cols < ext_cols)
-            bias = jnp.where(valid, window, centre)
-            scores = scores * scaling + bias
-            weights = jnp.exp2(scores - jnp.max(scores, axis=1, keepdims=True))
-            weights = weights * (1.0 / jnp.sum(weights, axis=1, keepdims=True))
-            result = jnp.dot(
-                weights.astype(jnp.bfloat16), values, preferred_element_type=jnp.float32
-            )
+            biased = scores[image] * scaling + jnp.where(valid, window, centre)
+            part = jnp.exp2(biased - jnp.max(biased, axis=1, keepdims=True))
+            part = part * (1.0 / jnp.sum(part, axis=1, keepdims=True))
+            weights.append(part.astype(jnp.bfloat16))
+        for image in range(2):
+            ext_rows, ext_cols = place_ref[1 + 2 * image], place_ref[2 + 2 * image]
+            values = kv[image, start : start + KEYS, HEAD:]
+            result = jnp.dot(weights[image], values, preferred_element_type=jnp.float32)
             inside = (base + ROWS * unit + query_at // COLS < ext_rows) & (query_at % COLS < ext_cols)
             result = jnp.where(inside, result, 0.0).astype(jnp.bfloat16)
             highest = jnp.maximum(highest, jnp.abs(result.astype(jnp.float32)))

time: 150 us -> 149 us (level)
  transfers between devices with their start and end apart: 11 -> 11, of which waited for: 6 -> 6; matrix products, arithmetic and copies ran while one was open for 5% -> 5% of each run, Pallas kernels for 4% -> 3%
where the time goes in v7:
time: 149 us; the launch traced here: 148 us
  starting transfers between devices  50.7 us (34%)
  waiting for transfers between devices  39.8 us (27%)
  blocking collectives  22.2 us (15%)
  between operations  15.6 us (10%)
  Pallas kernels  10.3 us (7%)
  local copies, waits for them, and re-layouts  7.2 us (5%)
  other arithmetic  2.06 us (1%)
    all_to_all x2, waiting for transfers between devices, spread(): return lax.all_to_all(copies, axis, 0, 0, tiled=True)  27 us
    all_to_all x2, starting transfers between devices, spread(): return lax.all_to_all(copies, axis, 0, 0, tiled=True)  25.7 us
    all_to_all x1, blocking collectives, local(): mixed = lax.all_to_all(mixed, GROUP, 0, 0, tiled=True)  14.9 us
    ppermute x4, starting transfers between devices, shift(): lax.ppermute(value, axis, [(i, (i + step) % size) for i in range(size)])  14.8 us
    all_to_all x1, blocking collectives, spread(): return lax.all_to_all(copies, axis, 0, 0, tiled=True)  7.26 us
    ppermute x1, starting transfers between devices, head_weights(): first = lax.ppermute(mine, AXES, main)  4.59 us
    ppermute x1, waiting for transfers between devices, head_weights(): first = lax.ppermute(mine, AXES, main)  4.2 us
    slice x1, local copies, waits for them, and re-layouts, local(): tokens = [tokens[2 * part:2 * part + 2] for part in range(4)]  4 us
  transfers between devices with their start and end apart: 11, of which 6 were waited for; matrix products, arithmetic and copies ran while one was open for 5% of the time, Pallas kernels for 3%

profile of v7, /device:TPU:1, one launch (start us, length us, event | category | flops | bytes accessed | tf_op | source)
XLA Modules:
  0.0 147.8 jit_solution(3432148803117116184)
XLA Ops:
  8.6 4.6 %collective-permute-start = (bf16[6,2048]{1,0:T(8,128)(2,1)}, bf16[6,2048]{1,0:T(8,128)(2,1)S(1)}, u32[]{:S(2)}, u32[]{:S(2)}) collective-permute-start(bf16[6,2048]{1,0:T(8,128)(2,1)} %bitcast.9), channel_id=1, source_target_pairs={{0,0},{1,128},{2,2},{3,130},{4,4},{5,132},{6,6},{7,134},{8,8},{9,1... | collective-permute-start | bytes 73736 | tf_op jit(solution)/shard_map/ppermute | solution.py:254
  13.2 4.2 %collective-permute-done = bf16[6,2048]{1,0:T(8,128)(2,1)S(1)} collective-permute-done((bf16[6,2048]{1,0:T(8,128)(2,1)}, bf16[6,2048]{1,0:T(8,128)(2,1)S(1)}, u32[]{:S(2)}, u32[]{:S(2)}) %collective-permute-start) | collective-permute-done | bytes 24608 | tf_op jit(solution)/shard_map/ppermute | solution.py:254
  17.6 0.8 broadcast_in_dim.12
  18.4 16.4 %all-to-all-start = ((bf16[16,96,128]{2,1,0:T(8,128)(2,1)}), bf16[16,96,128]{2,1,0:T(8,128)(2,1)S(1)}, u32[]{:S(2)}, u32[]{:S(2)}) async-start(bf16[16,96,128]{2,1,0:T(8,128)(2,1)} %broadcast_in_dim.12), calls=%async_computation | async-start | bytes 786432 | tf_op jit(solution)/shard_map/weights_over_z/all_to_all | solution.py:243
  34.8 2.0 %collective-permute-start.2 = (s32[1,2]{1,0:T(1,128)S(1)}, s32[1,2]{1,0:T(1,128)S(1)}, u32[]{:S(2)}, u32[]{:S(2)}) collective-permute-start(s32[1,2]{1,0:T(1,128)S(1)} %copy-done.1), channel_id=1, source_target_pairs={{0,1},{1,0},{2,3},{3,2},{4,5},{5,4},{6,7},{7,6},{8,9},{9,8},{10,11... | collective-permute-start | bytes 32 | tf_op jit(solution)/shard_map/ppermute | solution.py:248
  38.0 17.1 %all-to-all-done = bf16[16,96,128]{2,1,0:T(8,128)(2,1)S(1)} async-done(((bf16[16,96,128]{2,1,0:T(8,128)(2,1)}), bf16[16,96,128]{2,1,0:T(8,128)(2,1)S(1)}, u32[]{:S(2)}, u32[]{:S(2)}) %all-to-all-start) | async-done | bytes 393248 | tf_op jit(solution)/shard_map/weights_over_z/all_to_all | solution.py:243
  55.2 7.5 %collective-permute-start.5 = (bf16[96,2048]{1,0:T(8,128)(2,1)S(1)}, bf16[96,2048]{1,0:T(8,128)(2,1)S(1)}, u32[]{:S(2)}, u32[]{:S(2)}) collective-permute-start(bf16[96,2048]{1,0:T(8,128)(2,1)S(1)} %reshape.41.w0_ref), channel_id=1, source_target_pairs={{0,256},{128,384},{256,0},{384,128},{1,257},{129,385},{257,1},{385... | collective-permute-start | bytes 1179656 | tf_op jit(solution)/shard_map/weights_over_y/ppermute | solution.py:248
  62.7 2.1 %collective-permute-start.4 = (bf16[96,2048]{1,0:T(8,128)(2,1)S(1)}, bf16[96,2048]{1,0:T(8,128)(2,1)S(1)}, u32[]{:S(2)}, u32[]{:S(2)}) collective-permute-start(bf16[96,2048]{1,0:T(8,128)(2,1)S(1)} %reshape.41.w0_ref), channel_id=1, source_target_pairs={{0,384},{128,0},{256,128},{384,256},{1,385},{129,1},{257,129},{385... | collective-permute-start | bytes 1179656 | tf_op jit(solution)/shard_map/weights_over_y/ppermute | solution.py:248
  64.8 3.2 %collective-permute-start.3 = (bf16[96,2048]{1,0:T(8,128)(2,1)S(1)}, bf16[96,2048]{1,0:T(8,128)(2,1)S(1)}, u32[]{:S(2)}, u32[]{:S(2)}) collective-permute-start(bf16[96,2048]{1,0:T(8,128)(2,1)S(1)} %reshape.41.w0_ref), channel_id=1, source_target_pairs={{0,128},{128,256},{256,384},{384,0},{1,129},{129,257},{257,385},{3... | collective-permute-start | bytes 1179656 | tf_op jit(solution)/shard_map/weights_over_y/ppermute | solution.py:248
  69.4 3.9 %all-gather.2.cloned.1.call-done = bf16[8,256,2048]{2,1,0:T(8,128)(2,1)} async-done(((bf16[1,256,2048]{2,1,0:T(8,128)(2,1)}), bf16[8,256,2048]{2,1,0:T(8,128)(2,1)}) %all-gather.2.cloned.1.call-update) | async-done | bytes 8388624 | tf_op jit(solution)/shard_map/tokens/all_gather | solution.py:270
  73.3 4.0 %fusion.24 = (bf16[2,256,2048]{2,1,0:T(8,128)(2,1)S(1)}, bf16[2,256,2048]{2,1,0:T(8,128)(2,1)S(1)}, bf16[2,256,2048]{2,1,0:T(8,128)(2,1)S(1)}, bf16[2,256,2048]{2,1,0:T(8,128)(2,1)S(1)}) fusion(bf16[8,256,2048]{2,1,0:T(8,128)(2,1)} %all-gather.2.cloned.1.call-done), kind=kLoop, calls=%fused_computation.54 | loop fusion | bytes 16777216 | tf_op jit(solution)/shard_map/slice | solution.py:271
  77.3 2.4 %collective-permute-done.3.w1_ref = bf16[96,2048]{1,0:T(8,128)(2,1)S(1)} collective-permute-done((bf16[96,2048]{1,0:T(8,128)(2,1)S(1)}, bf16[96,2048]{1,0:T(8,128)(2,1)S(1)}, u32[]{:S(2)}, u32[]{:S(2)}) %collective-permute-start.3) | collective-permute-done | bytes 393248 | tf_op jit(solution)/shard_map/weights_over_y/ppermute | solution.py:248
  79.7 3.3 %project_outer.1 = (bf16[4,256,384]{2,1,0:T(8,128)(2,1)S(1)}, bf16[2,192,256]{2,1,0:T(8,128)(2,1)S(1)}, bf16[2,192,256]{2,1,0:T(8,128)(2,1)S(1)}, bf16[384,2048]{1,0:T(8,128)(2,1)S(1)}) custom-call(f32[1]{0:T(128)S(6)} %copy.14.scale_ref, bf16[2,256,2048]{2,1,0:T(8,128)(2,1)S(1)} %get-tuple-element.27.x0_ref, ...), custom_call_target="tpu_custom_call" | custom-call | flops 1610612736 | bytes 8388608 | tf_op jit(solution)/shard_map/project_outer/pallas_call | solution.py:96
  83.0 3.7 %collective-permute-start.6 = (bf16[2,192,256]{2,1,0:T(8,128)(2,1)S(1)}, bf16[2,192,256]{2,1,0:T(8,128)(2,1)S(1)}, u32[]{:S(2)}, u32[]{:S(2)}) collective-permute-start(bf16[2,192,256]{2,1,0:T(8,128)(2,1)S(1)} %get-tuple-element.20), channel_id=1, source_target_pairs={{0,128},{128,256},{256,384},{1,129},{129,257},{257,385},{2,130},{1... | collective-permute-start | bytes 589832 | tf_op jit(solution)/shard_map/halo/ppermute | solution.py:282
  86.7 1.3 collective-permute-start.7
  88.0 2.3 %project_inner.1.inner_ref = bf16[4,256,384]{2,1,0:T(8,128)(2,1)S(1)} custom-call(f32[1]{0:T(128)S(6)} %copy.14.scale_ref, bf16[2,256,2048]{2,1,0:T(8,128)(2,1)S(1)} %get-tuple-element.25.x1_ref, bf16[2,256,2048]{2,1,0:T(8,128)(2,1)S(1)} %get-tuple-element.24.x2_ref, bf16[384,2048]{1,0:T(8,128)(2,1)S(1)} %get-tuple-element.19.w_ref), custom_call_target="tpu_custom_call" | custom-call | flops 1610612736 | bytes 6291456 | tf_op jit(solution)/shard_map/project_inner/pallas_call | solution.py:117
  90.3 2.2 %attend_inner.1 = (bf16[8,256,128]{2,1,0:T(8,128)(2,1)S(1)}, f32[256,128]{1,0:T(8,128)S(1)}) custom-call(s32[5]{0:T(128)S(1)} %pad_add_fusion.place_ref, bf16[4,256,384]{2,1,0:T(8,128)(2,1)S(1)} %get-tuple-element.18.outer_ref, bf16[4,256,384]{2,1,0:T(8,128)(2,1)S(1)} %project_inner.1.inner_ref), custom_call_target="tpu_custom_call" | custom-call | flops 335544320 | bytes 2097152 | tf_op jit(solution)/shard_map/attend_inner/pallas_call | solution.py:206
  92.6 1.7 %collective-permute-done.7.below_ref = bf16[2,192,256]{2,1,0:T(8,128)(2,1)S(1)} collective-permute-done((bf16[2,192,256]{2,1,0:T(8,128)(2,1)S(1)}, bf16[2,192,256]{2,1,0:T(8,128)(2,1)S(1)}, u32[]{:S(2)}, u32[]{:S(2)}) %collective-permute-start.7) | collective-permute-done | bytes 196640 | tf_op jit(solution)/shard_map/halo/ppermute | solution.py:283
  94.2 2.4 %attend_outer.1 = bf16[8,272,128]{2,1,0:T(8,128)(2,1)S(1)} custom-call(s32[5]{0:T(128)S(1)} %pad_add_fusion.place_ref, f32[1]{0:T(128)S(6)} %convert.6.peak_ref, bf16[4,256,384]{2,1,0:T(8,128)(2,1)S(1)} %get-tuple-element.18.outer_ref, bf16[4,256,384]{2,1,0:T(8,128)(2,1)S(1)} %project_inner.1.inner_ref, ...), custom_call_target="tpu_custom_call" | custom-call | flops 335544320 | bytes 3145728 | tf_op jit(solution)/shard_map/attend_outer/pallas_call | solution.py:226
  96.7 14.9 %all_to_all.22 = bf16[8,272,128]{2,1,0:T(8,128)(2,1)S(1)} all-to-all(bf16[8,272,128]{2,1,0:T(8,128)(2,1)S(1)} %attend_outer.1), channel_id=1, replica_groups=mesh['y'=4,'x'=4,'z'=16,'core'=2] {'x','core'}, dimensions={0} | all-to-all | bytes 1114112 | tf_op jit(solution)/shard_map/heads/all_to_all | solution.py:288
  111.9 7.3 %all_to_all.23 = f32[4,1,2]{2,1,0:T(1,128)S(1)} all-to-all(f32[4,1,2]{2,1,0:T(1,128)S(1)} %broadcast_in_dim.24), channel_id=1, replica_groups=mesh['y'=4,'x'=4,'z'=16,'core'=2] {'y'}, dimensions={0} | all-to-all | bytes 64 | tf_op jit(solution)/shard_map/peaks/all_to_all | solution.py:243
  119.8 9.3 %all-to-all-start.3 = ((f32[16,1,2]{2,1,0:T(1,128)}), f32[16,1,2]{2,1,0:T(1,128)S(1)}, u32[]{:S(2)}, u32[]{:S(2)}) async-start(f32[16,1,2]{2,1,0:T(1,128)} %broadcast_in_dim.25), calls=%async_computation.3 | async-start | bytes 16384 | tf_op jit(solution)/shard_map/peaks/all_to_all | solution.py:243
  129.5 1.0 reshape.45
  130.5 9.9 %all-to-all-done.3 = f32[16,1,2]{2,1,0:T(1,128)S(1)} async-done(((f32[16,1,2]{2,1,0:T(1,128)}), f32[16,1,2]{2,1,0:T(1,128)S(1)}, u32[]{:S(2)}, u32[]{:S(2)}) %all-to-all-start.3) | async-done | bytes 160 | tf_op jit(solution)/shard_map/peaks/all_to_all | solution.py:243
  (34 shorter events, 4.9 us)
Async XLA Ops:
  7.2 60.9 %copy-start = (bf16[1,4,64,2048]{3,2,1,0:T(8,128)(2,1)S(1)}, bf16[1,4,64,2048]{3,2,1,0:T(8,128)(2,1)}, u32[]{:S(2)}) copy-start(bf16[1,4,64,2048]{3,2,1,0:T(8,128)(2,1)} %param.4) | copy-start | bytes 3145732
  7.2 27.6 %copy-start.1 = (s32[1,2]{1,0:T(1,128)S(1)}, s32[1,2]{1,0:T(1,128)}, u32[]{:S(2)}) copy-start(s32[1,2]{1,0:T(1,128)} %param.7) | copy-start | bytes 28
  7.2 66.1 %all-gather.2.cloned.1.call-start = ((), (), s32[]{:S(2)}) async-start(), calls=%async_computation.4 | async-start | bytes 9437184 | tf_op jit(solution)/shard_map/tokens/all_gather | solution.py:270
  7.9 5.3 %collective-permute-start.1 = (bf16[6,2048]{1,0:T(8,128)(2,1)}, bf16[6,2048]{1,0:T(8,128)(2,1)S(1)}, u32[]{:S(2)}, u32[]{:S(2)}) collective-permute-start(bf16[6,2048]{1,0:T(8,128)(2,1)} %bitcast.8), channel_id=1, source_target_pairs={{21,149},{42,298},{85,212},{106,331},{149,245},{170,266},{213,180}... | collective-permute-start | bytes 73736 | tf_op jit(solution)/shard_map/ppermute | solution.py:255
  8.6 8.9 %collective-permute-start = (bf16[6,2048]{1,0:T(8,128)(2,1)}, bf16[6,2048]{1,0:T(8,128)(2,1)S(1)}, u32[]{:S(2)}, u32[]{:S(2)}) collective-permute-start(bf16[6,2048]{1,0:T(8,128)(2,1)} %bitcast.9), channel_id=1, source_target_pairs={{0,0},{1,128},{2,2},{3,130},{4,4},{5,132},{6,6},{7,134},{8,8},{9,1... | collective-permute-start | bytes 73736 | tf_op jit(solution)/shard_map/ppermute | solution.py:254
  18.4 36.7 %all-to-all-start = ((bf16[16,96,128]{2,1,0:T(8,128)(2,1)}), bf16[16,96,128]{2,1,0:T(8,128)(2,1)S(1)}, u32[]{:S(2)}, u32[]{:S(2)}) async-start(bf16[16,96,128]{2,1,0:T(8,128)(2,1)} %broadcast_in_dim.12), calls=%async_computation | async-start | bytes 786432 | tf_op jit(solution)/shard_map/weights_over_z/all_to_all | solution.py:243
  34.8 3.0 %collective-permute-start.2 = (s32[1,2]{1,0:T(1,128)S(1)}, s32[1,2]{1,0:T(1,128)S(1)}, u32[]{:S(2)}, u32[]{:S(2)}) collective-permute-start(s32[1,2]{1,0:T(1,128)S(1)} %copy-done.1), channel_id=1, source_target_pairs={{0,1},{1,0},{2,3},{3,2},{4,5},{5,4},{6,7},{7,6},{8,9},{9,8},{10,11... | collective-permute-start | bytes 32 | tf_op jit(solution)/shard_map/ppermute | solution.py:248
  55.2 22.1 %collective-permute-start.5 = (bf16[96,2048]{1,0:T(8,128)(2,1)S(1)}, bf16[96,2048]{1,0:T(8,128)(2,1)S(1)}, u32[]{:S(2)}, u32[]{:S(2)}) collective-permute-start(bf16[96,2048]{1,0:T(8,128)(2,1)S(1)} %reshape.41.w0_ref), channel_id=1, source_target_pairs={{0,256},{128,384},{256,0},{384,128},{1,257},{129,385},{257,1},{385... | collective-permute-start | bytes 1179656 | tf_op jit(solution)/shard_map/weights_over_y/ppermute | solution.py:248
  62.7 14.6 %collective-permute-start.4 = (bf16[96,2048]{1,0:T(8,128)(2,1)S(1)}, bf16[96,2048]{1,0:T(8,128)(2,1)S(1)}, u32[]{:S(2)}, u32[]{:S(2)}) collective-permute-start(bf16[96,2048]{1,0:T(8,128)(2,1)S(1)} %reshape.41.w0_ref), channel_id=1, source_target_pairs={{0,384},{128,0},{256,128},{384,256},{1,385},{129,1},{257,129},{385... | collective-permute-start | bytes 1179656 | tf_op jit(solution)/shard_map/weights_over_y/ppermute | solution.py:248
  64.8 14.9 %collective-permute-start.3 = (bf16[96,2048]{1,0:T(8,128)(2,1)S(1)}, bf16[96,2048]{1,0:T(8,128)(2,1)S(1)}, u32[]{:S(2)}, u32[]{:S(2)}) collective-permute-start(bf16[96,2048]{1,0:T(8,128)(2,1)S(1)} %reshape.41.w0_ref), channel_id=1, source_target_pairs={{0,128},{128,256},{256,384},{384,0},{1,129},{129,257},{257,385},{3... | collective-permute-start | bytes 1179656 | tf_op jit(solution)/shard_map/weights_over_y/ppermute | solution.py:248
  83.0 9.6 %collective-permute-start.6 = (bf16[2,192,256]{2,1,0:T(8,128)(2,1)S(1)}, bf16[2,192,256]{2,1,0:T(8,128)(2,1)S(1)}, u32[]{:S(2)}, u32[]{:S(2)}) collective-permute-start(bf16[2,192,256]{2,1,0:T(8,128)(2,1)S(1)} %get-tuple-element.20), channel_id=1, source_target_pairs={{0,128},{128,256},{256,384},{1,129},{129,257},{257,385},{2,130},{1... | collective-permute-start | bytes 589832 | tf_op jit(solution)/shard_map/halo/ppermute | solution.py:282
  86.7 7.6 %collective-permute-start.7 = (bf16[2,192,256]{2,1,0:T(8,128)(2,1)S(1)}, bf16[2,192,256]{2,1,0:T(8,128)(2,1)S(1)}, u32[]{:S(2)}, u32[]{:S(2)}) collective-permute-start(bf16[2,192,256]{2,1,0:T(8,128)(2,1)S(1)} %get-tuple-element.21), channel_id=1, source_target_pairs={{128,0},{256,128},{384,256},{129,1},{257,129},{385,257},{130,2},{2... | collective-permute-start | bytes 589832 | tf_op jit(solution)/shard_map/halo/ppermute | solution.py:283
  119.8 20.6 %all-to-all-start.3 = ((f32[16,1,2]{2,1,0:T(1,128)}), f32[16,1,2]{2,1,0:T(1,128)S(1)}, u32[]{:S(2)}, u32[]{:S(2)}) async-start(f32[16,1,2]{2,1,0:T(1,128)} %broadcast_in_dim.25), calls=%async_computation.3 | async-start | bytes 16384 | tf_op jit(solution)/shard_map/peaks/all_to_all | solution.py:243
Sparse Core Ops, SparseCore 0:
  10.2 63.0 all-gather.1

commit v8 on v7

--- a/solution.py
+++ b/solution.py
@@ -268,7 +268,6 @@
 def local(images, w_qkv, prev_scale, extent):
     with jax.named_scope("tokens"):
         tokens = lax.all_gather(images.reshape(SET, D), GROUP, axis=0, tiled=False)
-    tokens = [tokens[2 * part : 2 * part + 2] for part in range(4)]
     weights, late = head_weights(w_qkv, images)
     core = lax.axis_index("core")
     order = column_order(2 * lax.axis_index("x") + core, lax.axis_index("y"))
@@ -277,11 +276,12 @@
     extents = jnp.where(core == 0, jnp.concatenate([extent, other]), jnp.concatenate([other, extent]))
     place = jnp.stack([lax.axis_index("y") * BLOCK, *extents.reshape(4)]).astype(jnp.int32)
     order, peak_in, place = lax.optimization_barrier((order, peak_in, place))
-    outer, top, bottom, weights = project_outer(prev_scale, [tokens[part] for part in OUTER], weights, order)
+    outer, top, bottom, weights = project_outer(prev_scale, [tokens[2 * part : 2 * part + 2] for part in OUTER], weights, order)
     with jax.named_scope("halo"):
         above = lax.ppermute(bottom, "y", [(i, i + 1) for i in range(3)])
         below = lax.ppermute(top, "y", [(i + 1, i) for i in range(3)])
-    inner = project_inner(prev_scale, [tokens[part] for part in INNER], weights)
+    tokens = lax.optimization_barrier((tokens, weights))[0]
+    inner = project_inner(prev_scale, [tokens[2 * part : 2 * part + 2] for part in INNER], weights)
     done, highest = attend_inner(place, outer, inner)
     mixed = attend_outer(place, peak_in, outer, inner, above, below, done, highest)
     with jax.named_scope("heads"):

time: 149 us -> 148 us (level)
    slice x1 -> x2, local copies, waits for them, and re-layouts: 4 us -> 3.45 us  [local(): tokens[2 * part:2 * part + 2]]
  transfers between devices with their start and end apart: 11 -> 11, of which waited for: 6 -> 7; matrix products, arithmetic and copies ran while one was open for 5% -> 5% of each run, Pallas kernels for 3% -> 3%
where the time goes in v8:
time: 148 us; the launch traced here: 147 us
  starting transfers between devices  49.5 us (33%)
  waiting for transfers between devices  40.3 us (27%)
  blocking collectives  22.2 us (15%)
  between operations  15.6 us (11%)
  Pallas kernels  10.3 us (7%)
  local copies, waits for them, and re-layouts  6.66 us (4%)
  other arithmetic  2.06 us (1%)
    all_to_all x2, waiting for transfers between devices, spread(): return lax.all_to_all(copies, axis, 0, 0, tiled=True)  26.9 us
    all_to_all x2, starting transfers between devices, spread(): return lax.all_to_all(copies, axis, 0, 0, tiled=True)  24.5 us
    all_to_all x1, blocking collectives, local(): mixed = lax.all_to_all(mixed, GROUP, 0, 0, tiled=True)  14.9 us
    ppermute x4, starting transfers between devices, shift(): lax.ppermute(value, axis, [(i, (i + step) % size) for i in range(size)])  14.8 us
    all_to_all x1, blocking collectives, spread(): return lax.all_to_all(copies, axis, 0, 0, tiled=True)  7.26 us
    ppermute x1, starting transfers between devices, head_weights(): first = lax.ppermute(mine, AXES, main)  4.59 us
    ppermute x1, waiting for transfers between devices, head_weights(): first = lax.ppermute(mine, AXES, main)  4.2 us
    all_gather x1, waiting for transfers between devices, local(): tokens = lax.all_gather(images.reshape(SET, D), GROUP, axis=0, tiled=False)  3.85 us
  transfers between devices with their start and end apart: 11, of which 7 were waited for; matrix products, arithmetic and copies ran while one was open for 5% of the time, Pallas kernels for 3%

profile of v8, /device:TPU:1, one launch (start us, length us, event | category | flops | bytes accessed | tf_op | source)
XLA Modules:
  0.0 146.6 jit_solution(14679605008089025112)
XLA Ops:
  8.6 4.6 %collective-permute-start = (bf16[6,2048]{1,0:T(8,128)(2,1)}, bf16[6,2048]{1,0:T(8,128)(2,1)S(1)}, u32[]{:S(2)}, u32[]{:S(2)}) collective-permute-start(bf16[6,2048]{1,0:T(8,128)(2,1)} %bitcast.9), channel_id=1, source_target_pairs={{0,0},{1,128},{2,2},{3,130},{4,4},{5,132},{6,6},{7,134},{8,8},{9,1... | collective-permute-start | bytes 73736 | tf_op jit(solution)/shard_map/ppermute | solution.py:254
  13.2 4.2 %collective-permute-done = bf16[6,2048]{1,0:T(8,128)(2,1)S(1)} collective-permute-done((bf16[6,2048]{1,0:T(8,128)(2,1)}, bf16[6,2048]{1,0:T(8,128)(2,1)S(1)}, u32[]{:S(2)}, u32[]{:S(2)}) %collective-permute-start) | collective-permute-done | bytes 24608 | tf_op jit(solution)/shard_map/ppermute | solution.py:254
  17.6 0.8 broadcast_in_dim.12
  18.4 16.4 %all-to-all-start = ((bf16[16,96,128]{2,1,0:T(8,128)(2,1)}), bf16[16,96,128]{2,1,0:T(8,128)(2,1)S(1)}, u32[]{:S(2)}, u32[]{:S(2)}) async-start(bf16[16,96,128]{2,1,0:T(8,128)(2,1)} %broadcast_in_dim.12), calls=%async_computation | async-start | bytes 786432 | tf_op jit(solution)/shard_map/weights_over_z/all_to_all | solution.py:243
  34.8 2.0 %collective-permute-start.2 = (s32[1,2]{1,0:T(1,128)S(1)}, s32[1,2]{1,0:T(1,128)S(1)}, u32[]{:S(2)}, u32[]{:S(2)}) collective-permute-start(s32[1,2]{1,0:T(1,128)S(1)} %copy-done.2), channel_id=1, source_target_pairs={{0,1},{1,0},{2,3},{3,2},{4,5},{5,4},{6,7},{7,6},{8,9},{9,8},{10,11... | collective-permute-start | bytes 32 | tf_op jit(solution)/shard_map/ppermute | solution.py:248
  38.0 17.1 %all-to-all-done = bf16[16,96,128]{2,1,0:T(8,128)(2,1)S(1)} async-done(((bf16[16,96,128]{2,1,0:T(8,128)(2,1)}), bf16[16,96,128]{2,1,0:T(8,128)(2,1)S(1)}, u32[]{:S(2)}, u32[]{:S(2)}) %all-to-all-start) | async-done | bytes 393248 | tf_op jit(solution)/shard_map/weights_over_z/all_to_all | solution.py:243
  55.2 7.5 %collective-permute-start.5 = (bf16[96,2048]{1,0:T(8,128)(2,1)S(1)}, bf16[96,2048]{1,0:T(8,128)(2,1)S(1)}, u32[]{:S(2)}, u32[]{:S(2)}) collective-permute-start(bf16[96,2048]{1,0:T(8,128)(2,1)S(1)} %reshape.41.w0_ref), channel_id=1, source_target_pairs={{0,256},{128,384},{256,0},{384,128},{1,257},{129,385},{257,1},{385... | collective-permute-start | bytes 1179656 | tf_op jit(solution)/shard_map/weights_over_y/ppermute | solution.py:248
  62.7 2.1 %collective-permute-start.4 = (bf16[96,2048]{1,0:T(8,128)(2,1)S(1)}, bf16[96,2048]{1,0:T(8,128)(2,1)S(1)}, u32[]{:S(2)}, u32[]{:S(2)}) collective-permute-start(bf16[96,2048]{1,0:T(8,128)(2,1)S(1)} %reshape.41.w0_ref), channel_id=1, source_target_pairs={{0,384},{128,0},{256,128},{384,256},{1,385},{129,1},{257,129},{385... | collective-permute-start | bytes 1179656 | tf_op jit(solution)/shard_map/weights_over_y/ppermute | solution.py:248
  64.8 3.2 %collective-permute-start.3 = (bf16[96,2048]{1,0:T(8,128)(2,1)S(1)}, bf16[96,2048]{1,0:T(8,128)(2,1)S(1)}, u32[]{:S(2)}, u32[]{:S(2)}) collective-permute-start(bf16[96,2048]{1,0:T(8,128)(2,1)S(1)} %reshape.41.w0_ref), channel_id=1, source_target_pairs={{0,128},{128,256},{256,384},{384,0},{1,129},{129,257},{257,385},{3... | collective-permute-start | bytes 1179656 | tf_op jit(solution)/shard_map/weights_over_y/ppermute | solution.py:248
  69.4 3.9 %all-gather.2.cloned.1.call-done = bf16[8,256,2048]{2,1,0:T(8,128)(2,1)} async-done(((bf16[1,256,2048]{2,1,0:T(8,128)(2,1)}), bf16[8,256,2048]{2,1,0:T(8,128)(2,1)}) %all-gather.2.cloned.1.call-update) | async-done | bytes 8388624 | tf_op jit(solution)/shard_map/tokens/all_gather | solution.py:270
  73.3 2.9 %fusion.25 = (bf16[2,256,2048]{2,1,0:T(8,128)(2,1)S(1)}, bf16[2,256,2048]{2,1,0:T(8,128)(2,1)S(1)}) fusion(bf16[8,256,2048]{2,1,0:T(8,128)(2,1)} %all-gather.2.cloned.1.call-done), kind=kLoop, calls=%fused_computation.55 | loop fusion | bytes 8388608 | tf_op jit(solution)/shard_map/slice | solution.py:279
  76.3 3.4 %collective-permute-done.3.w1_ref = bf16[96,2048]{1,0:T(8,128)(2,1)S(1)} collective-permute-done((bf16[96,2048]{1,0:T(8,128)(2,1)S(1)}, bf16[96,2048]{1,0:T(8,128)(2,1)S(1)}, u32[]{:S(2)}, u32[]{:S(2)}) %collective-permute-start.3) | collective-permute-done | bytes 393248 | tf_op jit(solution)/shard_map/weights_over_y/ppermute | solution.py:248
  79.7 3.3 %project_outer.1 = (bf16[4,256,384]{2,1,0:T(8,128)(2,1)S(1)}, bf16[2,192,256]{2,1,0:T(8,128)(2,1)S(1)}, bf16[2,192,256]{2,1,0:T(8,128)(2,1)S(1)}, bf16[384,2048]{1,0:T(8,128)(2,1)S(1)}) custom-call(f32[1]{0:T(128)S(6)} %copy.14.scale_ref, bf16[2,256,2048]{2,1,0:T(8,128)(2,1)S(1)} %get-tuple-element.29.x0_ref, ...), custom_call_target="tpu_custom_call" | custom-call | flops 1610612736 | bytes 8388608 | tf_op jit(solution)/shard_map/project_outer/pallas_call | solution.py:96
  83.0 3.7 %collective-permute-start.6 = (bf16[2,192,256]{2,1,0:T(8,128)(2,1)S(1)}, bf16[2,192,256]{2,1,0:T(8,128)(2,1)S(1)}, u32[]{:S(2)}, u32[]{:S(2)}) collective-permute-start(bf16[2,192,256]{2,1,0:T(8,128)(2,1)S(1)} %get-tuple-element.22), channel_id=1, source_target_pairs={{0,128},{128,256},{256,384},{1,129},{129,257},{257,385},{2,130},{1... | collective-permute-start | bytes 589832 | tf_op jit(solution)/shard_map/halo/ppermute | solution.py:281
  86.7 1.3 collective-permute-start.7
  88.6 2.4 %project_inner.1.inner_ref = bf16[4,256,384]{2,1,0:T(8,128)(2,1)S(1)} custom-call(f32[1]{0:T(128)S(6)} %copy.14.scale_ref, bf16[2,256,2048]{2,1,0:T(8,128)(2,1)S(1)} %get-tuple-element.27.x1_ref, bf16[2,256,2048]{2,1,0:T(8,128)(2,1)S(1)} %get-tuple-element.26.x2_ref, bf16[384,2048]{1,0:T(8,128)(2,1)S(1)} %get-tuple-element.20.w_ref), custom_call_target="tpu_custom_call" | custom-call | flops 1610612736 | bytes 6291456 | tf_op jit(solution)/shard_map/project_inner/pallas_call | solution.py:117
  90.9 2.2 %attend_inner.1 = (bf16[8,256,128]{2,1,0:T(8,128)(2,1)S(1)}, f32[256,128]{1,0:T(8,128)S(1)}) custom-call(s32[5]{0:T(128)S(1)} %pad_add_fusion.place_ref, bf16[4,256,384]{2,1,0:T(8,128)(2,1)S(1)} %get-tuple-element.19.outer_ref, bf16[4,256,384]{2,1,0:T(8,128)(2,1)S(1)} %project_inner.1.inner_ref), custom_call_target="tpu_custom_call" | custom-call | flops 335544320 | bytes 2097152 | tf_op jit(solution)/shard_map/attend_inner/pallas_call | solution.py:206
  93.2 1.1 collective-permute-done.7.below_ref
  94.2 2.4 %attend_outer.1 = bf16[8,272,128]{2,1,0:T(8,128)(2,1)S(1)} custom-call(s32[5]{0:T(128)S(1)} %pad_add_fusion.place_ref, f32[1]{0:T(128)S(6)} %convert.6.peak_ref, bf16[4,256,384]{2,1,0:T(8,128)(2,1)S(1)} %get-tuple-element.19.outer_ref, bf16[4,256,384]{2,1,0:T(8,128)(2,1)S(1)} %project_inner.1.inner_ref, ...), custom_call_target="tpu_custom_call" | custom-call | flops 335544320 | bytes 3145728 | tf_op jit(solution)/shard_map/attend_outer/pallas_call | solution.py:226
  96.7 14.9 %all_to_all.22 = bf16[8,272,128]{2,1,0:T(8,128)(2,1)S(1)} all-to-all(bf16[8,272,128]{2,1,0:T(8,128)(2,1)S(1)} %attend_outer.1), channel_id=1, replica_groups=mesh['y'=4,'x'=4,'z'=16,'core'=2] {'x','core'}, dimensions={0} | all-to-all | bytes 1114112 | tf_op jit(solution)/shard_map/heads/all_to_all | solution.py:288
  111.9 7.3 %all_to_all.23 = f32[4,1,2]{2,1,0:T(1,128)S(1)} all-to-all(f32[4,1,2]{2,1,0:T(1,128)S(1)} %broadcast_in_dim.24), channel_id=1, replica_groups=mesh['y'=4,'x'=4,'z'=16,'core'=2] {'y'}, dimensions={0} | all-to-all | bytes 64 | tf_op jit(solution)/shard_map/peaks/all_to_all | solution.py:243
  119.8 8.2 %all-to-all-start.3 = ((f32[16,1,2]{2,1,0:T(1,128)}), f32[16,1,2]{2,1,0:T(1,128)S(1)}, u32[]{:S(2)}, u32[]{:S(2)}) async-start(f32[16,1,2]{2,1,0:T(1,128)} %broadcast_in_dim.25), calls=%async_computation.3 | async-start | bytes 16384 | tf_op jit(solution)/shard_map/peaks/all_to_all | solution.py:243
  128.4 1.0 reshape.45
  129.4 9.8 %all-to-all-done.3 = f32[16,1,2]{2,1,0:T(1,128)S(1)} async-done(((f32[16,1,2]{2,1,0:T(1,128)}), f32[16,1,2]{2,1,0:T(1,128)S(1)}, u32[]{:S(2)}, u32[]{:S(2)}) %all-to-all-start.3) | async-done | bytes 160 | tf_op jit(solution)/shard_map/peaks/all_to_all | solution.py:243
  (37 shorter events, 5.6 us)
Async XLA Ops:
  7.2 60.9 %copy-start.1 = (bf16[1,4,64,2048]{3,2,1,0:T(8,128)(2,1)S(1)}, bf16[1,4,64,2048]{3,2,1,0:T(8,128)(2,1)}, u32[]{:S(2)}) copy-start(bf16[1,4,64,2048]{3,2,1,0:T(8,128)(2,1)} %param.4) | copy-start | bytes 3145732
  7.2 27.6 %copy-start.2 = (s32[1,2]{1,0:T(1,128)S(1)}, s32[1,2]{1,0:T(1,128)}, u32[]{:S(2)}) copy-start(s32[1,2]{1,0:T(1,128)} %param.7) | copy-start | bytes 28
  7.2 66.1 %all-gather.2.cloned.1.call-start = ((), (), s32[]{:S(2)}) async-start(), calls=%async_computation.4 | async-start | bytes 9437184 | tf_op jit(solution)/shard_map/tokens/all_gather | solution.py:270
  7.9 5.3 %collective-permute-start.1 = (bf16[6,2048]{1,0:T(8,128)(2,1)}, bf16[6,2048]{1,0:T(8,128)(2,1)S(1)}, u32[]{:S(2)}, u32[]{:S(2)}) collective-permute-start(bf16[6,2048]{1,0:T(8,128)(2,1)} %bitcast.8), channel_id=1, source_target_pairs={{21,149},{42,298},{85,212},{106,331},{149,245},{170,266},{213,180}... | collective-permute-start | bytes 73736 | tf_op jit(solution)/shard_map/ppermute | solution.py:255
  8.6 8.9 %collective-permute-start = (bf16[6,2048]{1,0:T(8,128)(2,1)}, bf16[6,2048]{1,0:T(8,128)(2,1)S(1)}, u32[]{:S(2)}, u32[]{:S(2)}) collective-permute-start(bf16[6,2048]{1,0:T(8,128)(2,1)} %bitcast.9), channel_id=1, source_target_pairs={{0,0},{1,128},{2,2},{3,130},{4,4},{5,132},{6,6},{7,134},{8,8},{9,1... | collective-permute-start | bytes 73736 | tf_op jit(solution)/shard_map/ppermute | solution.py:254
  18.4 36.7 %all-to-all-start = ((bf16[16,96,128]{2,1,0:T(8,128)(2,1)}), bf16[16,96,128]{2,1,0:T(8,128)(2,1)S(1)}, u32[]{:S(2)}, u32[]{:S(2)}) async-start(bf16[16,96,128]{2,1,0:T(8,128)(2,1)} %broadcast_in_dim.12), calls=%async_computation | async-start | bytes 786432 | tf_op jit(solution)/shard_map/weights_over_z/all_to_all | solution.py:243
  34.8 3.0 %collective-permute-start.2 = (s32[1,2]{1,0:T(1,128)S(1)}, s32[1,2]{1,0:T(1,128)S(1)}, u32[]{:S(2)}, u32[]{:S(2)}) collective-permute-start(s32[1,2]{1,0:T(1,128)S(1)} %copy-done.2), channel_id=1, source_target_pairs={{0,1},{1,0},{2,3},{3,2},{4,5},{5,4},{6,7},{7,6},{8,9},{9,8},{10,11... | collective-permute-start | bytes 32 | tf_op jit(solution)/shard_map/ppermute | solution.py:248
  55.2 21.0 %collective-permute-start.5 = (bf16[96,2048]{1,0:T(8,128)(2,1)S(1)}, bf16[96,2048]{1,0:T(8,128)(2,1)S(1)}, u32[]{:S(2)}, u32[]{:S(2)}) collective-permute-start(bf16[96,2048]{1,0:T(8,128)(2,1)S(1)} %reshape.41.w0_ref), channel_id=1, source_target_pairs={{0,256},{128,384},{256,0},{384,128},{1,257},{129,385},{257,1},{385... | collective-permute-start | bytes 1179656 | tf_op jit(solution)/shard_map/weights_over_y/ppermute | solution.py:248
  62.7 13.6 %collective-permute-start.4 = (bf16[96,2048]{1,0:T(8,128)(2,1)S(1)}, bf16[96,2048]{1,0:T(8,128)(2,1)S(1)}, u32[]{:S(2)}, u32[]{:S(2)}) collective-permute-start(bf16[96,2048]{1,0:T(8,128)(2,1)S(1)} %reshape.41.w0_ref), channel_id=1, source_target_pairs={{0,384},{128,0},{256,128},{384,256},{1,385},{129,1},{257,129},{385... | collective-permute-start | bytes 1179656 | tf_op jit(solution)/shard_map/weights_over_y/ppermute | solution.py:248
  64.8 14.9 %collective-permute-start.3 = (bf16[96,2048]{1,0:T(8,128)(2,1)S(1)}, bf16[96,2048]{1,0:T(8,128)(2,1)S(1)}, u32[]{:S(2)}, u32[]{:S(2)}) collective-permute-start(bf16[96,2048]{1,0:T(8,128)(2,1)S(1)} %reshape.41.w0_ref), channel_id=1, source_target_pairs={{0,128},{128,256},{256,384},{384,0},{1,129},{129,257},{257,385},{3... | collective-permute-start | bytes 1179656 | tf_op jit(solution)/shard_map/weights_over_y/ppermute | solution.py:248
  73.3 14.7 %copy-start = (bf16[8,256,2048]{2,1,0:T(8,128)(2,1)S(1)}, bf16[8,256,2048]{2,1,0:T(8,128)(2,1)}, u32[]{:S(2)}) copy-start(bf16[8,256,2048]{2,1,0:T(8,128)(2,1)} %all-gather.2.cloned.1.call-done) | copy-start | bytes 25165828
  83.0 10.2 %collective-permute-start.6 = (bf16[2,192,256]{2,1,0:T(8,128)(2,1)S(1)}, bf16[2,192,256]{2,1,0:T(8,128)(2,1)S(1)}, u32[]{:S(2)}, u32[]{:S(2)}) collective-permute-start(bf16[2,192,256]{2,1,0:T(8,128)(2,1)S(1)} %get-tuple-element.22), channel_id=1, source_target_pairs={{0,128},{128,256},{256,384},{1,129},{129,257},{257,385},{2,130},{1... | collective-permute-start | bytes 589832 | tf_op jit(solution)/shard_map/halo/ppermute | solution.py:281
  86.7 7.6 %collective-permute-start.7 = (bf16[2,192,256]{2,1,0:T(8,128)(2,1)S(1)}, bf16[2,192,256]{2,1,0:T(8,128)(2,1)S(1)}, u32[]{:S(2)}, u32[]{:S(2)}) collective-permute-start(bf16[2,192,256]{2,1,0:T(8,128)(2,1)S(1)} %get-tuple-element.23), channel_id=1, source_target_pairs={{128,0},{256,128},{384,256},{129,1},{257,129},{385,257},{130,2},{2... | collective-permute-start | bytes 589832 | tf_op jit(solution)/shard_map/halo/ppermute | solution.py:282
  119.8 19.4 %all-to-all-start.3 = ((f32[16,1,2]{2,1,0:T(1,128)}), f32[16,1,2]{2,1,0:T(1,128)S(1)}, u32[]{:S(2)}, u32[]{:S(2)}) async-start(f32[16,1,2]{2,1,0:T(1,128)} %broadcast_in_dim.25), calls=%async_computation.3 | async-start | bytes 16384 | tf_op jit(solution)/shard_map/peaks/all_to_all | solution.py:243
Sparse Core Ops, SparseCore 0:
  10.2 63.0 all-gather.1

commit v9 on v8

--- a/solution.py
+++ b/solution.py
@@ -75,11 +75,10 @@
         qkv_ref[2 * place : 2 * place + 2] = out
 
 
-def project_outer_kernel(scale_ref, x0_ref, x3_ref, w0_ref, w1_ref, w2_ref, w3_ref, order_ref, qkv_ref, top_ref, bottom_ref, w_ref, w_cat):
-    for part, ref in enumerate((w0_ref, w1_ref, w2_ref, w3_ref)):
-        w_cat[96 * part : 96 * (part + 1)] = ref[...]
+def project_outer_kernel(scale_ref, x0_ref, x3_ref, w0_ref, w1_ref, w2_ref, w3_ref, order_ref, qkv_ref, top_ref, bottom_ref, w_ref):
+    gathered = jnp.concatenate([ref[...] for ref in (w0_ref, w1_ref, w2_ref, w3_ref)])
     w_ref[...] = lax.dot_general(
-        order_ref[...], w_cat[...], (((0,), (0,)), ((), ())), preferred_element_type=jnp.float32
+        order_ref[...], gathered, (((0,), (0,)), ((), ())), preferred_element_type=jnp.float32
     ).astype(jnp.bfloat16)
     project_rows(scale_ref, (x0_ref, x3_ref), w_ref, qkv_ref)
     top_ref[...] = qkv_ref[:2, : HALO * COLS, HEAD:]
@@ -103,7 +102,6 @@
         ),
         in_specs=[pl.BlockSpec(memory_space=pltpu.SMEM)] + [vmem] * 7,
         out_specs=(vmem,) * 4,
-        scratch_shapes=[pltpu.VMEM((3 * HEAD, D), jnp.bfloat16)],
         compiler_params=pltpu.CompilerParams(vmem_limit_bytes=24 * 2**20),
         cost_estimate=pl.CostEstimate(
             flops=2 * 4 * SET * D * 3 * HEAD, bytes_accessed=8 * 2**20, transcendentals=0

time: 148 us -> 148 us (level)
  no operation moved by 1% of the time
where the time goes in v9:
time: 148 us; the launch traced here: 147 us
  starting transfers between devices  49.5 us (33%)
  waiting for transfers between devices  40.3 us (27%)
  blocking collectives  22.2 us (15%)
  between operations  15.6 us (11%)
  Pallas kernels  10.3 us (7%)
  local copies, waits for them, and re-layouts  6.66 us (4%)
  other arithmetic  2.06 us (1%)
    all_to_all x2, waiting for transfers between devices, spread(): return lax.all_to_all(copies, axis, 0, 0, tiled=True)  26.9 us
    all_to_all x2, starting transfers between devices, spread(): return lax.all_to_all(copies, axis, 0, 0, tiled=True)  24.5 us
    all_to_all x1, blocking collectives, local(): mixed = lax.all_to_all(mixed, GROUP, 0, 0, tiled=True)  14.9 us
    ppermute x4, starting transfers between devices, shift(): lax.ppermute(value, axis, [(i, (i + step) % size) for i in range(size)])  14.8 us
    all_to_all x1, blocking collectives, spread(): return lax.all_to_all(copies, axis, 0, 0, tiled=True)  7.26 us
    ppermute x1, starting transfers between devices, head_weights(): first = lax.ppermute(mine, AXES, main)  4.59 us
    ppermute x1, waiting for transfers between devices, head_weights(): first = lax.ppermute(mine, AXES, main)  4.2 us
    all_gather x1, waiting for transfers between devices, local(): tokens = lax.all_gather(images.reshape(SET, D), GROUP, axis=0, tiled=False)  3.85 us
  transfers between devices with their start and end apart: 11, of which 7 were waited for; matrix products, arithmetic and copies ran while one was open for 5% of the time, Pallas kernels for 3%

profile of v9, /device:TPU:1, one launch (start us, length us, event | category | flops | bytes accessed | tf_op | source)
XLA Modules:
  0.0 146.6 jit_solution(14679605008089025112)
XLA Ops:
  8.6 4.6 %collective-permute-start = (bf16[6,2048]{1,0:T(8,128)(2,1)}, bf16[6,2048]{1,0:T(8,128)(2,1)S(1)}, u32[]{:S(2)}, u32[]{:S(2)}) collective-permute-start(bf16[6,2048]{1,0:T(8,128)(2,1)} %bitcast.9), channel_id=1, source_target_pairs={{0,0},{1,128},{2,2},{3,130},{4,4},{5,132},{6,6},{7,134},{8,8},{9,1... | collective-permute-start | bytes 73736 | tf_op jit(solution)/shard_map/ppermute | solution.py:252
  13.2 4.2 %collective-permute-done = bf16[6,2048]{1,0:T(8,128)(2,1)S(1)} collective-permute-done((bf16[6,2048]{1,0:T(8,128)(2,1)}, bf16[6,2048]{1,0:T(8,128)(2,1)S(1)}, u32[]{:S(2)}, u32[]{:S(2)}) %collective-permute-start) | collective-permute-done | bytes 24608 | tf_op jit(solution)/shard_map/ppermute | solution.py:252
  17.6 0.8 broadcast_in_dim.12
  18.4 16.4 %all-to-all-start = ((bf16[16,96,128]{2,1,0:T(8,128)(2,1)}), bf16[16,96,128]{2,1,0:T(8,128)(2,1)S(1)}, u32[]{:S(2)}, u32[]{:S(2)}) async-start(bf16[16,96,128]{2,1,0:T(8,128)(2,1)} %broadcast_in_dim.12), calls=%async_computation | async-start | bytes 786432 | tf_op jit(solution)/shard_map/weights_over_z/all_to_all | solution.py:241
  34.8 2.0 %collective-permute-start.2 = (s32[1,2]{1,0:T(1,128)S(1)}, s32[1,2]{1,0:T(1,128)S(1)}, u32[]{:S(2)}, u32[]{:S(2)}) collective-permute-start(s32[1,2]{1,0:T(1,128)S(1)} %copy-done.2), channel_id=1, source_target_pairs={{0,1},{1,0},{2,3},{3,2},{4,5},{5,4},{6,7},{7,6},{8,9},{9,8},{10,11... | collective-permute-start | bytes 32 | tf_op jit(solution)/shard_map/ppermute | solution.py:246
  38.0 17.1 %all-to-all-done = bf16[16,96,128]{2,1,0:T(8,128)(2,1)S(1)} async-done(((bf16[16,96,128]{2,1,0:T(8,128)(2,1)}), bf16[16,96,128]{2,1,0:T(8,128)(2,1)S(1)}, u32[]{:S(2)}, u32[]{:S(2)}) %all-to-all-start) | async-done | bytes 393248 | tf_op jit(solution)/shard_map/weights_over_z/all_to_all | solution.py:241
  55.2 7.5 %collective-permute-start.5 = (bf16[96,2048]{1,0:T(8,128)(2,1)S(1)}, bf16[96,2048]{1,0:T(8,128)(2,1)S(1)}, u32[]{:S(2)}, u32[]{:S(2)}) collective-permute-start(bf16[96,2048]{1,0:T(8,128)(2,1)S(1)} %reshape.41.w0_ref), channel_id=1, source_target_pairs={{0,256},{128,384},{256,0},{384,128},{1,257},{129,385},{257,1},{385... | collective-permute-start | bytes 1179656 | tf_op jit(solution)/shard_map/weights_over_y/ppermute | solution.py:246
  62.7 2.1 %collective-permute-start.4 = (bf16[96,2048]{1,0:T(8,128)(2,1)S(1)}, bf16[96,2048]{1,0:T(8,128)(2,1)S(1)}, u32[]{:S(2)}, u32[]{:S(2)}) collective-permute-start(bf16[96,2048]{1,0:T(8,128)(2,1)S(1)} %reshape.41.w0_ref), channel_id=1, source_target_pairs={{0,384},{128,0},{256,128},{384,256},{1,385},{129,1},{257,129},{385... | collective-permute-start | bytes 1179656 | tf_op jit(solution)/shard_map/weights_over_y/ppermute | solution.py:246
  64.8 3.2 %collective-permute-start.3 = (bf16[96,2048]{1,0:T(8,128)(2,1)S(1)}, bf16[96,2048]{1,0:T(8,128)(2,1)S(1)}, u32[]{:S(2)}, u32[]{:S(2)}) collective-permute-start(bf16[96,2048]{1,0:T(8,128)(2,1)S(1)} %reshape.41.w0_ref), channel_id=1, source_target_pairs={{0,128},{128,256},{256,384},{384,0},{1,129},{129,257},{257,385},{3... | collective-permute-start | bytes 1179656 | tf_op jit(solution)/shard_map/weights_over_y/ppermute | solution.py:246
  69.4 3.9 %all-gather.2.cloned.1.call-done = bf16[8,256,2048]{2,1,0:T(8,128)(2,1)} async-done(((bf16[1,256,2048]{2,1,0:T(8,128)(2,1)}), bf16[8,256,2048]{2,1,0:T(8,128)(2,1)}) %all-gather.2.cloned.1.call-update) | async-done | bytes 8388624 | tf_op jit(solution)/shard_map/tokens/all_gather | solution.py:268
  73.3 2.9 %fusion.25 = (bf16[2,256,2048]{2,1,0:T(8,128)(2,1)S(1)}, bf16[2,256,2048]{2,1,0:T(8,128)(2,1)S(1)}) fusion(bf16[8,256,2048]{2,1,0:T(8,128)(2,1)} %all-gather.2.cloned.1.call-done), kind=kLoop, calls=%fused_computation.55 | loop fusion | bytes 8388608 | tf_op jit(solution)/shard_map/slice | solution.py:277
  76.3 3.4 %collective-permute-done.3.w1_ref = bf16[96,2048]{1,0:T(8,128)(2,1)S(1)} collective-permute-done((bf16[96,2048]{1,0:T(8,128)(2,1)S(1)}, bf16[96,2048]{1,0:T(8,128)(2,1)S(1)}, u32[]{:S(2)}, u32[]{:S(2)}) %collective-permute-start.3) | collective-permute-done | bytes 393248 | tf_op jit(solution)/shard_map/weights_over_y/ppermute | solution.py:246
  79.7 3.3 %project_outer.1 = (bf16[4,256,384]{2,1,0:T(8,128)(2,1)S(1)}, bf16[2,192,256]{2,1,0:T(8,128)(2,1)S(1)}, bf16[2,192,256]{2,1,0:T(8,128)(2,1)S(1)}, bf16[384,2048]{1,0:T(8,128)(2,1)S(1)}) custom-call(f32[1]{0:T(128)S(6)} %copy.14.scale_ref, bf16[2,256,2048]{2,1,0:T(8,128)(2,1)S(1)} %get-tuple-element.29.x0_ref, ...), custom_call_target="tpu_custom_call" | custom-call | flops 1610612736 | bytes 8388608 | tf_op jit(solution)/shard_map/project_outer/pallas_call | solution.py:95
  83.0 3.7 %collective-permute-start.6 = (bf16[2,192,256]{2,1,0:T(8,128)(2,1)S(1)}, bf16[2,192,256]{2,1,0:T(8,128)(2,1)S(1)}, u32[]{:S(2)}, u32[]{:S(2)}) collective-permute-start(bf16[2,192,256]{2,1,0:T(8,128)(2,1)S(1)} %get-tuple-element.22), channel_id=1, source_target_pairs={{0,128},{128,256},{256,384},{1,129},{129,257},{257,385},{2,130},{1... | collective-permute-start | bytes 589832 | tf_op jit(solution)/shard_map/halo/ppermute | solution.py:279
  86.7 1.3 collective-permute-start.7
  88.6 2.4 %project_inner.1.inner_ref = bf16[4,256,384]{2,1,0:T(8,128)(2,1)S(1)} custom-call(f32[1]{0:T(128)S(6)} %copy.14.scale_ref, bf16[2,256,2048]{2,1,0:T(8,128)(2,1)S(1)} %get-tuple-element.27.x1_ref, bf16[2,256,2048]{2,1,0:T(8,128)(2,1)S(1)} %get-tuple-element.26.x2_ref, bf16[384,2048]{1,0:T(8,128)(2,1)S(1)} %get-tuple-element.20.w_ref), custom_call_target="tpu_custom_call" | custom-call | flops 1610612736 | bytes 6291456 | tf_op jit(solution)/shard_map/project_inner/pallas_call | solution.py:115
  90.9 2.2 %attend_inner.1 = (bf16[8,256,128]{2,1,0:T(8,128)(2,1)S(1)}, f32[256,128]{1,0:T(8,128)S(1)}) custom-call(s32[5]{0:T(128)S(1)} %pad_add_fusion.place_ref, bf16[4,256,384]{2,1,0:T(8,128)(2,1)S(1)} %get-tuple-element.19.outer_ref, bf16[4,256,384]{2,1,0:T(8,128)(2,1)S(1)} %project_inner.1.inner_ref), custom_call_target="tpu_custom_call" | custom-call | flops 335544320 | bytes 2097152 | tf_op jit(solution)/shard_map/attend_inner/pallas_call | solution.py:204
  93.2 1.1 collective-permute-done.7.below_ref
  94.2 2.4 %attend_outer.1 = bf16[8,272,128]{2,1,0:T(8,128)(2,1)S(1)} custom-call(s32[5]{0:T(128)S(1)} %pad_add_fusion.place_ref, f32[1]{0:T(128)S(6)} %convert.6.peak_ref, bf16[4,256,384]{2,1,0:T(8,128)(2,1)S(1)} %get-tuple-element.19.outer_ref, bf16[4,256,384]{2,1,0:T(8,128)(2,1)S(1)} %project_inner.1.inner_ref, ...), custom_call_target="tpu_custom_call" | custom-call | flops 335544320 | bytes 3145728 | tf_op jit(solution)/shard_map/attend_outer/pallas_call | solution.py:224
  96.7 14.9 %all_to_all.22 = bf16[8,272,128]{2,1,0:T(8,128)(2,1)S(1)} all-to-all(bf16[8,272,128]{2,1,0:T(8,128)(2,1)S(1)} %attend_outer.1), channel_id=1, replica_groups=mesh['y'=4,'x'=4,'z'=16,'core'=2] {'x','core'}, dimensions={0} | all-to-all | bytes 1114112 | tf_op jit(solution)/shard_map/heads/all_to_all | solution.py:286
  111.9 7.3 %all_to_all.23 = f32[4,1,2]{2,1,0:T(1,128)S(1)} all-to-all(f32[4,1,2]{2,1,0:T(1,128)S(1)} %broadcast_in_dim.24), channel_id=1, replica_groups=mesh['y'=4,'x'=4,'z'=16,'core'=2] {'y'}, dimensions={0} | all-to-all | bytes 64 | tf_op jit(solution)/shard_map/peaks/all_to_all | solution.py:241
  119.8 8.2 %all-to-all-start.3 = ((f32[16,1,2]{2,1,0:T(1,128)}), f32[16,1,2]{2,1,0:T(1,128)S(1)}, u32[]{:S(2)}, u32[]{:S(2)}) async-start(f32[16,1,2]{2,1,0:T(1,128)} %broadcast_in_dim.25), calls=%async_computation.3 | async-start | bytes 16384 | tf_op jit(solution)/shard_map/peaks/all_to_all | solution.py:241
  128.4 1.0 reshape.45
  129.4 9.8 %all-to-all-done.3 = f32[16,1,2]{2,1,0:T(1,128)S(1)} async-done(((f32[16,1,2]{2,1,0:T(1,128)}), f32[16,1,2]{2,1,0:T(1,128)S(1)}, u32[]{:S(2)}, u32[]{:S(2)}) %all-to-all-start.3) | async-done | bytes 160 | tf_op jit(solution)/shard_map/peaks/all_to_all | solution.py:241
  (37 shorter events, 5.6 us)
Async XLA Ops:
  7.2 60.9 %copy-start.1 = (bf16[1,4,64,2048]{3,2,1,0:T(8,128)(2,1)S(1)}, bf16[1,4,64,2048]{3,2,1,0:T(8,128)(2,1)}, u32[]{:S(2)}) copy-start(bf16[1,4,64,2048]{3,2,1,0:T(8,128)(2,1)} %param.4) | copy-start | bytes 3145732
  7.2 27.6 %copy-start.2 = (s32[1,2]{1,0:T(1,128)S(1)}, s32[1,2]{1,0:T(1,128)}, u32[]{:S(2)}) copy-start(s32[1,2]{1,0:T(1,128)} %param.7) | copy-start | bytes 28
  7.2 66.1 %all-gather.2.cloned.1.call-start = ((), (), s32[]{:S(2)}) async-start(), calls=%async_computation.4 | async-start | bytes 9437184 | tf_op jit(solution)/shard_map/tokens/all_gather | solution.py:268
  7.9 5.3 %collective-permute-start.1 = (bf16[6,2048]{1,0:T(8,128)(2,1)}, bf16[6,2048]{1,0:T(8,128)(2,1)S(1)}, u32[]{:S(2)}, u32[]{:S(2)}) collective-permute-start(bf16[6,2048]{1,0:T(8,128)(2,1)} %bitcast.8), channel_id=1, source_target_pairs={{21,149},{42,298},{85,212},{106,331},{149,245},{170,266},{213,180}... | collective-permute-start | bytes 73736 | tf_op jit(solution)/shard_map/ppermute | solution.py:253
  8.6 8.9 %collective-permute-start = (bf16[6,2048]{1,0:T(8,128)(2,1)}, bf16[6,2048]{1,0:T(8,128)(2,1)S(1)}, u32[]{:S(2)}, u32[]{:S(2)}) collective-permute-start(bf16[6,2048]{1,0:T(8,128)(2,1)} %bitcast.9), channel_id=1, source_target_pairs={{0,0},{1,128},{2,2},{3,130},{4,4},{5,132},{6,6},{7,134},{8,8},{9,1... | collective-permute-start | bytes 73736 | tf_op jit(solution)/shard_map/ppermute | solution.py:252
  18.4 36.7 %all-to-all-start = ((bf16[16,96,128]{2,1,0:T(8,128)(2,1)}), bf16[16,96,128]{2,1,0:T(8,128)(2,1)S(1)}, u32[]{:S(2)}, u32[]{:S(2)}) async-start(bf16[16,96,128]{2,1,0:T(8,128)(2,1)} %broadcast_in_dim.12), calls=%async_computation | async-start | bytes 786432 | tf_op jit(solution)/shard_map/weights_over_z/all_to_all | solution.py:241
  34.8 3.0 %collective-permute-start.2 = (s32[1,2]{1,0:T(1,128)S(1)}, s32[1,2]{1,0:T(1,128)S(1)}, u32[]{:S(2)}, u32[]{:S(2)}) collective-permute-start(s32[1,2]{1,0:T(1,128)S(1)} %copy-done.2), channel_id=1, source_target_pairs={{0,1},{1,0},{2,3},{3,2},{4,5},{5,4},{6,7},{7,6},{8,9},{9,8},{10,11... | collective-permute-start | bytes 32 | tf_op jit(solution)/shard_map/ppermute | solution.py:246
  55.2 21.0 %collective-permute-start.5 = (bf16[96,2048]{1,0:T(8,128)(2,1)S(1)}, bf16[96,2048]{1,0:T(8,128)(2,1)S(1)}, u32[]{:S(2)}, u32[]{:S(2)}) collective-permute-start(bf16[96,2048]{1,0:T(8,128)(2,1)S(1)} %reshape.41.w0_ref), channel_id=1, source_target_pairs={{0,256},{128,384},{256,0},{384,128},{1,257},{129,385},{257,1},{385... | collective-permute-start | bytes 1179656 | tf_op jit(solution)/shard_map/weights_over_y/ppermute | solution.py:246
  62.7 13.6 %collective-permute-start.4 = (bf16[96,2048]{1,0:T(8,128)(2,1)S(1)}, bf16[96,2048]{1,0:T(8,128)(2,1)S(1)}, u32[]{:S(2)}, u32[]{:S(2)}) collective-permute-start(bf16[96,2048]{1,0:T(8,128)(2,1)S(1)} %reshape.41.w0_ref), channel_id=1, source_target_pairs={{0,384},{128,0},{256,128},{384,256},{1,385},{129,1},{257,129},{385... | collective-permute-start | bytes 1179656 | tf_op jit(solution)/shard_map/weights_over_y/ppermute | solution.py:246
  64.8 14.9 %collective-permute-start.3 = (bf16[96,2048]{1,0:T(8,128)(2,1)S(1)}, bf16[96,2048]{1,0:T(8,128)(2,1)S(1)}, u32[]{:S(2)}, u32[]{:S(2)}) collective-permute-start(bf16[96,2048]{1,0:T(8,128)(2,1)S(1)} %reshape.41.w0_ref), channel_id=1, source_target_pairs={{0,128},{128,256},{256,384},{384,0},{1,129},{129,257},{257,385},{3... | collective-permute-start | bytes 1179656 | tf_op jit(solution)/shard_map/weights_over_y/ppermute | solution.py:246
  73.3 14.7 %copy-start = (bf16[8,256,2048]{2,1,0:T(8,128)(2,1)S(1)}, bf16[8,256,2048]{2,1,0:T(8,128)(2,1)}, u32[]{:S(2)}) copy-start(bf16[8,256,2048]{2,1,0:T(8,128)(2,1)} %all-gather.2.cloned.1.call-done) | copy-start | bytes 25165828
  83.0 10.2 %collective-permute-start.6 = (bf16[2,192,256]{2,1,0:T(8,128)(2,1)S(1)}, bf16[2,192,256]{2,1,0:T(8,128)(2,1)S(1)}, u32[]{:S(2)}, u32[]{:S(2)}) collective-permute-start(bf16[2,192,256]{2,1,0:T(8,128)(2,1)S(1)} %get-tuple-element.22), channel_id=1, source_target_pairs={{0,128},{128,256},{256,384},{1,129},{129,257},{257,385},{2,130},{1... | collective-permute-start | bytes 589832 | tf_op jit(solution)/shard_map/halo/ppermute | solution.py:279
  86.7 7.6 %collective-permute-start.7 = (bf16[2,192,256]{2,1,0:T(8,128)(2,1)S(1)}, bf16[2,192,256]{2,1,0:T(8,128)(2,1)S(1)}, u32[]{:S(2)}, u32[]{:S(2)}) collective-permute-start(bf16[2,192,256]{2,1,0:T(8,128)(2,1)S(1)} %get-tuple-element.23), channel_id=1, source_target_pairs={{128,0},{256,128},{384,256},{129,1},{257,129},{385,257},{130,2},{2... | collective-permute-start | bytes 589832 | tf_op jit(solution)/shard_map/halo/ppermute | solution.py:280
  119.8 19.4 %all-to-all-start.3 = ((f32[16,1,2]{2,1,0:T(1,128)}), f32[16,1,2]{2,1,0:T(1,128)S(1)}, u32[]{:S(2)}, u32[]{:S(2)}) async-start(f32[16,1,2]{2,1,0:T(1,128)} %broadcast_in_dim.25), calls=%async_computation.3 | async-start | bytes 16384 | tf_op jit(solution)/shard_map/peaks/all_to_all | solution.py:241
Sparse Core Ops, SparseCore 0:
  10.2 63.0 all-gather.1
